TPU v7x, 256 devices: a whole 4x4x8 slice. The times are simulated.
256 devices in a mesh: blk: 64 (over y_lo, x, z), dp: 4 (over y_hi, core).
Axes of the slice: x: 4, y: 4 (y_hi: 2, y_lo: 2; y = y_hi * 2 + y_lo), z: 8, core: 2. Of those that a mesh axis runs over, the one named last changes fastest.
Arguments:
- tokens: bfloat16 [4, 64, 2, 128, 1024], P('dp', 'blk'), may hold values from -11 to 11
- key_valid: int32 [4, 64, 2, 128], P('dp'), may hold values 0 or 1
- weights: bfloat16 [4096, 1024], replicated
- out_grad: bfloat16 [4, 64, 2, 128, 1024], P('dp', 'blk'), may hold values from -6 to 6
Outputs:
- grad_tokens: bfloat16 [4, 64, 2, 128, 1024], P('dp', 'blk')
- grad_out_weight: float32 [1024, 1024], P('blk', 'dp')
All inputs are finite; a program needn't handle non-finite values. No bound on the sum of `key_valid` on one device may be relied on, other than what follows from the above.
Results may differ from a plain program's by a relative error of at most 0.024.
Values may be sent and summed in bfloat16 or wider, within the bound.
No kernel may reach another device: no remote copies, remote signals or barrier semaphores. Data moves between devices by JAX's collectives and lax.ppermute only.
A program may use at most 128 MiB of HBM per device.

v0:
```python
import jax
import jax.numpy as jnp
from jax import lax
from jax.sharding import PartitionSpec as P

HEADS = 16
HEAD_DIM = 64
WIN = 4


NEG_FILL = -1e30


def with_halo(x, sides, width):
    for axis, dim in sides:
        size, length = (lax.axis_size(axis), x.shape[dim])
        up = [(i, (i + 1) % size) for i in range(size - 1)]
        down = [(j, i) for i, j in up]
        last = lax.slice_in_dim(x, length - width, length, axis=dim)
        initial = lax.slice_in_dim(x, 0, width, axis=dim)
        before = lax.ppermute(last, axis, up)
        after = lax.ppermute(initial, axis, down)
        x = jnp.concatenate([before, x, after], axis=dim)
    return x


def walk_chain(pairs, at_last, mover):
    chain_state = jnp.flip(pairs, axis=2)
    up_list = []
    down_list = []
    for hop_index in range(WIN - 1):
        framed = mover(chain_state)
        new_up = framed[:, :, 0]
        new_down = jnp.where(at_last, framed[:, :, 2], framed[:, :, 3])
        chain_state = jnp.stack([new_down, new_up], axis=2)
        up_list.append(new_up)
        down_list.append(new_down)
    first_set = jnp.stack(list(reversed(up_list)), axis=2)
    second_set = jnp.stack(list(reversed(down_list)), axis=2)
    return jnp.stack([first_set, second_set], axis=2)


def per_device(tokens, key_valid, weights, out_grad):
    block_count = lax.axis_size("blk")
    position = lax.axis_index("blk")
    seq_count = tokens.shape[0]
    block_rows = tokens.shape[3]
    model_width = tokens.shape[4]
    key_span = WIN * block_rows
    score_scale = HEAD_DIM ** (-0.5)
    contract = (((1,), (1,)), ((), ()))
    w_query = weights[:model_width]
    w_key = weights[model_width : 2 * model_width]
    w_value = weights[2 * model_width : 3 * model_width]
    w_out = weights[3 * model_width :]
    token_rows = tokens.reshape(-1, model_width)
    grad_rows = out_grad.reshape(-1, model_width)
    queries = jnp.dot(token_rows, w_query, preferred_element_type=jnp.float32).astype(jnp.bfloat16)
    keyed = jnp.dot(token_rows, w_key, preferred_element_type=jnp.float32).astype(jnp.bfloat16)
    valued = jnp.dot(token_rows, w_value, preferred_element_type=jnp.float32).astype(jnp.bfloat16)
    d_attn = lax.dot_general(grad_rows, w_out, contract, preferred_element_type=jnp.float32).astype(
        jnp.bfloat16
    )
    key_pairs = jnp.stack([keyed, valued]).reshape(2, seq_count, 2, block_rows, model_width)
    at_last = position == block_count - 1
    remote = walk_chain(key_pairs, at_last, lambda state: with_halo(state, (("blk", 2),), 1))
    key_sets = jnp.concatenate([remote, key_pairs[:, :, :, None]], axis=3).reshape(
        2, seq_count, 2, key_span, HEADS, HEAD_DIM
    )
    keys_all = key_sets[0]
    values_all = key_sets[1]
    half_blocks = jnp.stack([position, 2 * block_count - 1 - position])
    seq_valid = jnp.concatenate([key_valid[:, :, 0], jnp.flip(key_valid[:, :, 1], axis=1)], axis=1)
    seq_valid = jnp.concatenate(
        [jnp.zeros((seq_count, WIN - 1, block_rows), jnp.int32), seq_valid], axis=1
    )
    valid_halves = []
    for half_index in range(2):
        window = lax.dynamic_slice_in_dim(seq_valid, half_blocks[half_index], WIN, 1)
        valid_halves.append(window.reshape(seq_count, key_span))
    valid_keys = jnp.stack(valid_halves, axis=1)
    q_pos = half_blocks[:, None] * block_rows + jnp.arange(block_rows, dtype=jnp.int32)[None, :]
    k_pos = (half_blocks[:, None] - WIN + 1) * block_rows + jnp.arange(key_span, dtype=jnp.int32)[
        None, :
    ]
    k_grid = k_pos[None, :, None, :]
    q_grid = q_pos[None, :, :, None]
    allowed = (
        (k_grid >= 0) & (k_grid <= q_grid) & ((valid_keys[:, :, None, :] == 1) | (k_grid == q_grid))
    )
    allowed = allowed[:, :, None]
    query_heads = queries.reshape(seq_count, 2, block_rows, HEADS, HEAD_DIM)
    dout_heads = d_attn.reshape(seq_count, 2, block_rows, HEADS, HEAD_DIM)
    raw_scores = jnp.einsum(
        "sxqhd,sxkhd->sxhqk", query_heads, keys_all, preferred_element_type=jnp.float32
    )
    scores = jnp.where(allowed, raw_scores * score_scale, NEG_FILL)
    row_max = jnp.max(scores, axis=-1, keepdims=True)
    exp_terms = jnp.exp(scores - row_max)
    row_total = jnp.sum(exp_terms, axis=-1, keepdims=True)
    probabilities = exp_terms / row_total
    probs_low = probabilities.astype(jnp.bfloat16)
    out_heads = jnp.einsum(
        "sxhqk,sxkhd->sxqhd", probs_low, values_all, preferred_element_type=jnp.float32
    ).astype(jnp.bfloat16)
    delta_rows = jnp.einsum(
        "sxqhd,sxqhd->sxhq", dout_heads, out_heads, preferred_element_type=jnp.float32
    )
    dprob = jnp.einsum(
        "sxqhd,sxkhd->sxhqk", dout_heads, values_all, preferred_element_type=jnp.float32
    )
    dscore = (probabilities * (dprob - delta_rows[..., None])).astype(jnp.bfloat16)
    grad_q = (
        jnp.einsum("sxhqk,sxkhd->sxqhd", dscore, keys_all, preferred_element_type=jnp.float32)
        * score_scale
    )
    grad_k = (
        jnp.einsum("sxhqk,sxqhd->sxkhd", dscore, query_heads, preferred_element_type=jnp.float32)
        * score_scale
    )
    grad_v = jnp.einsum(
        "sxhqk,sxqhd->sxkhd", probs_low, dout_heads, preferred_element_type=jnp.float32
    )
    key_grads = jnp.stack([grad_k, grad_v]).reshape(2, seq_count, 2, WIN, block_rows, model_width)
    returned = key_grads[:, :, :, 0]
    for hop_index in range(WIN - 1, 0, -1):
        framed = with_halo(returned.astype(jnp.bfloat16), (("blk", 2),), 1).astype(returned.dtype)
        back_down = framed[:, :, 0]
        back_up = framed[:, :, 3] + jnp.where(at_last, returned[:, :, 1], 0.0)
        returned = jnp.stack([back_up, back_down], axis=2) + key_grads[:, :, :, WIN - hop_index]
    grad_q16 = grad_q.reshape(-1, model_width).astype(jnp.bfloat16)
    grad_k16 = returned[0].reshape(-1, model_width).astype(jnp.bfloat16)
    grad_v16 = returned[1].reshape(-1, model_width).astype(jnp.bfloat16)
    grad_in = lax.dot_general(grad_q16, w_query, contract, preferred_element_type=jnp.float32)
    grad_in = grad_in + lax.dot_general(
        grad_k16, w_key, contract, preferred_element_type=jnp.float32
    )
    grad_in = grad_in + lax.dot_general(
        grad_v16, w_value, contract, preferred_element_type=jnp.float32
    )
    grad_in = grad_in.astype(jnp.bfloat16).reshape(tokens.shape)
    out_rows = out_heads.reshape(-1, model_width)
    token_dims = (((0,), (0,)), ((), ()))
    block_sum = lax.psum_scatter(
        lax.dot_general(out_rows, grad_rows, token_dims, preferred_element_type=jnp.float32),
        "blk",
        scatter_dimension=0,
        tiled=True,
    )
    weight_grad = lax.psum_scatter(
        block_sum.astype(jnp.bfloat16), "dp", scatter_dimension=1, tiled=True
    ).astype(jnp.float32)
    return (grad_in, weight_grad)


def solution(mesh):
    placed = (
        P("dp", "blk", None, None, None),
        P("dp", None, None, None),
        P(),
        P("dp", "blk", None, None, None),
    )
    return jax.shard_map(
        per_device,
        mesh=mesh,
        in_specs=placed,
        out_specs=(P("dp", "blk", None, None, None), P("blk", "dp")),
        check_vma=False,
    )
```

profile of v0, /device:TPU:24, one launch (start us, length us, event | category | flops | bytes accessed | tf_op | source)
XLA Modules:
  0.0 470.4 jit_solution(7506196734336490594)
XLA Ops:
  7.2 2.5 fusion.41
  12.2 10.1 %collective-permute-start.3 = (bf16[2,1,1,128,1024]{4,3,2,1,0:T(8,128)(2,1)S(1)}, bf16[2,1,1,128,1024]{4,3,2,1,0:T(8,128)(2,1)}, u32[]{:S(2)}, u32[]{:S(2)}) collective-permute-start(bf16[2,1,1,128,1024]{4,3,2,1,0:T(8,128)(2,1)S(1)} %fusion.62), channel_id=1, source_target_pairs={{4,0},{8,4},{12,8},{16,12},{20,16},{24,20},{28,24},{32,28},{36,32}... | collective-permute-start | bytes 1572872 | tf_op jit(solution)/shard_map/ppermute | solution.py:22
  25.6 3.1 fusion.47
  28.8 4.7 %collective-permute-done.3 = bf16[2,1,1,128,1024]{4,3,2,1,0:T(8,128)(2,1)} collective-permute-done((bf16[2,1,1,128,1024]{4,3,2,1,0:T(8,128)(2,1)S(1)}, bf16[2,1,1,128,1024]{4,3,2,1,0:T(8,128)(2,1)}, u32[]{:S(2)}, u32[]{:S(2)}) %collective-permute-start.3) | collective-permute-done | bytes 524320 | tf_op jit(solution)/shard_map/ppermute | solution.py:22
  35.4 8.7 %collective-permute-start.4 = (bf16[2,1,1,128,1024]{4,3,2,0,1:T(8,128)(2,1)}, bf16[2,1,1,128,1024]{4,3,2,0,1:T(8,128)(2,1)S(1)}, u32[]{:S(2)}, u32[]{:S(2)}) collective-permute-start(bf16[2,1,1,128,1024]{4,3,2,0,1:T(8,128)(2,1)} %bitcast.9), channel_id=1, source_target_pairs={{4,0},{8,4},{12,8},{16,12},{20,16},{24,20},{28,24},{32,28},{36,32}... | collective-permute-start | bytes 1572872 | tf_op jit(solution)/shard_map/ppermute | solution.py:22
  49.0 5.7 %collective-permute-done.4 = bf16[2,1,1,128,1024]{4,3,2,0,1:T(8,128)(2,1)S(1)} collective-permute-done((bf16[2,1,1,128,1024]{4,3,2,0,1:T(8,128)(2,1)}, bf16[2,1,1,128,1024]{4,3,2,0,1:T(8,128)(2,1)S(1)}, u32[]{:S(2)}, u32[]{:S(2)}) %collective-permute-start.4) | collective-permute-done | bytes 524320 | tf_op jit(solution)/shard_map/ppermute | solution.py:22
  55.6 8.5 %collective-permute-start.5 = (bf16[2,1,1,128,1024]{4,3,2,0,1:T(8,128)(2,1)}, bf16[2,1,1,128,1024]{4,3,2,0,1:T(8,128)(2,1)}, u32[]{:S(2)}, u32[]{:S(2)}) collective-permute-start(bf16[2,1,1,128,1024]{4,3,2,0,1:T(8,128)(2,1)} %broadcast_select_fusion), channel_id=1, source_target_pairs={{4,0},{8,4},{12,8},{16,12},{20,16},{24,20},{28,24},{32,28},{36,32}... | collective-permute-start | bytes 1572872 | tf_op jit(solution)/shard_map/ppermute | solution.py:22
  64.1 3.1 fusion.44
  76.3 9.0 %collective-permute-done.2 = bf16[2,1,1,128,1024]{4,3,2,0,1:T(8,128)(2,1)} collective-permute-done((bf16[2,1,1,128,1024]{4,3,2,0,1:T(8,128)(2,1)}, bf16[2,1,1,128,1024]{4,3,2,0,1:T(8,128)(2,1)}, u32[]{:S(2)}, u32[]{:S(2)}) %collective-permute-start.2) | collective-permute-done | bytes 524320 | tf_op jit(solution)/shard_map/ppermute | solution.py:21
  87.3 2.5 fusion.77
  89.8 3.1 copy.42
  95.1 4.3 copy.37
  99.4 2.7 reshape.625
  102.2 7.3 %fusion.83 = (f32[2,16,128]{2,1,0:T(8,128)S(1)}, f32[2,16,128,512]{3,2,1,0:T(8,128)}) fusion(pred[2,128,512]{2,1,0:T(8,128)(4,1)S(1)} %or_and_fusion, bf16[2,128,16,64]{1,3,2,0:T(8,128)(2,1)} %copy.40, bf16[2,512,16,64]{1,3,2,0:T(8,128)(2,1)S(1)} %reshape.625), kind=kOutput, calls=%fused_computation.125 | convolution fusion | flops 276824576 | bytes 11157504 | tf_op jit(solution)/shard_map/sub | solution.py:99
  109.5 4.0 fusion.5
  116.3 2.7 fusion.63
  119.3 4.9 %convolution_bitcast_fusion = f32[1,2,512,16,64]{2,4,3,1,0:T(8,128)} fusion(bf16[2,16,128,512]{3,2,1,0:T(8,128)(2,1)} %copy-done.4, bf16[2,128,16,64]{1,0,3,2:T(2,128)(2,1)S(1)} %reshape.628), kind=kOutput, calls=%fused_computation.18 | convolution fusion | flops 268435456 | bytes 8912896 | tf_op jit(solution)/shard_map/sxhqk,sxqhd->sxkhd/dot_general | solution.py:121
  124.1 5.3 %stack.96 = f32[1,1,2,4,128,1024]{4,3,5,2,1,0:T(4,128)} reshape(f32[1,2,512,16,64]{2,4,3,1,0:T(8,128)} %convolution_bitcast_fusion) | data formatting | bytes 8388608 | tf_op jit(solution)/shard_map/stack | solution.py:124
  129.5 5.3 %copy.48 = f32[1,1,2,4,128,1024]{5,4,2,0,3,1:T(8,128)} copy(f32[1,1,2,4,128,1024]{4,3,5,2,1,0:T(4,128)} %stack.96) | data formatting | bytes 8388608 | tf_op jit(solution)/shard_map/stack | solution.py:124
  134.8 5.1 %multiply_convert_fusion = bf16[2,16,128,512]{3,2,1,0:T(8,128)(2,1)S(1)} fusion(f32[2,16,128]{2,1,0:T(8,128)S(1)} %get-tuple-element.30, f32[2,16,128,512]{3,2,1,0:T(8,128)} %get-tuple-element.29, f32[2,16,128]{2,1,0:T(8,128)S(1)} %get-tuple-element.28, bf16[2,512,16,64]{1,3,2,0:T(8,128)(2,1)} %reshape.629, bf16[2,128,16,64]{1,0,3,2:T(2,128)(2,1)S(1)} %reshape.628), kind=kOutput, calls=%fused_computation.7 | convolution fusion | flops 276824064 | bytes 15237120 | tf_op jit(solution)/shard_map/sxqhd,sxkhd->sxhqk/dot_general | solution.py:109
  141.9 2.7 multiply_bitcast_fusion
  144.6 5.3 %stack.95 = f32[1,1,2,4,128,1024]{4,3,5,2,1,0:T(4,128)} reshape(f32[1,2,512,16,64]{2,4,3,1,0:T(8,128)} %multiply_bitcast_fusion) | data formatting | bytes 8388608 | tf_op jit(solution)/shard_map/stack | solution.py:124
  149.9 5.3 %copy.47 = f32[1,1,2,4,128,1024]{5,4,2,0,3,1:T(8,128)} copy(f32[1,1,2,4,128,1024]{4,3,5,2,1,0:T(4,128)} %stack.95) | data formatting | bytes 8388608 | tf_op jit(solution)/shard_map/stack | solution.py:124
  155.2 2.5 fusion.7
  159.8 8.1 %collective-permute-start.7 = (bf16[2,1,1,128,1024]{4,3,0,2,1:T(8,128)(2,1)S(1)}, bf16[2,1,1,128,1024]{4,3,0,2,1:T(8,128)(2,1)S(1)}, u32[]{:S(2)}, u32[]{:S(2)}) collective-permute-start(bf16[2,1,1,128,1024]{4,3,0,2,1:T(8,128)(2,1)S(1)} %get-tuple-element.23), channel_id=1, source_target_pairs={{4,0},{8,4},{12,8},{16,12},{20,16},{24,20},{28,24},{32,28},{36,32}... | collective-permute-start | bytes 1572872 | tf_op jit(solution)/shard_map/ppermute | solution.py:22
  168.2 8.3 %collective-permute-done.6 = bf16[2,1,1,128,1024]{4,3,0,2,1:T(8,128)(2,1)S(1)} collective-permute-done((bf16[2,1,1,128,1024]{4,3,0,2,1:T(8,128)(2,1)S(1)}, bf16[2,1,1,128,1024]{4,3,0,2,1:T(8,128)(2,1)S(1)}, u32[]{:S(2)}, u32[]{:S(2)}) %collective-permute-start.6) | collective-permute-done | bytes 524320 | tf_op jit(solution)/shard_map/ppermute | solution.py:21
  180.6 8.6 %collective-permute-start.9 = (bf16[2,1,1,128,1024]{4,3,0,2,1:T(8,128)(2,1)S(1)}, bf16[2,1,1,128,1024]{4,3,0,2,1:T(8,128)(2,1)S(1)}, u32[]{:S(2)}, u32[]{:S(2)}) collective-permute-start(bf16[2,1,1,128,1024]{4,3,0,2,1:T(8,128)(2,1)S(1)} %get-tuple-element.21), channel_id=1, source_target_pairs={{4,0},{8,4},{12,8},{16,12},{20,16},{24,20},{28,24},{32,28},{36,32}... | collective-permute-start | bytes 1572872 | tf_op jit(solution)/shard_map/ppermute | solution.py:22
  189.7 6.6 %collective-permute-done.8 = bf16[2,1,1,128,1024]{4,3,0,2,1:T(8,128)(2,1)S(1)} collective-permute-done((bf16[2,1,1,128,1024]{4,3,0,2,1:T(8,128)(2,1)S(1)}, bf16[2,1,1,128,1024]{4,3,0,2,1:T(8,128)(2,1)S(1)}, u32[]{:S(2)}, u32[]{:S(2)}) %collective-permute-start.8) | collective-permute-done | bytes 524320 | tf_op jit(solution)/shard_map/ppermute | solution.py:21
  204.1 8.9 %collective-permute-start.11 = (bf16[2,1,1,128,1024]{4,3,2,0,1:T(8,128)(2,1)S(1)}, bf16[2,1,1,128,1024]{4,3,2,0,1:T(8,128)(2,1)S(1)}, u32[]{:S(2)}, u32[]{:S(2)}) collective-permute-start(bf16[2,1,1,128,1024]{4,3,2,0,1:T(8,128)(2,1)S(1)} %get-tuple-element.19), channel_id=1, source_target_pairs={{4,0},{8,4},{12,8},{16,12},{20,16},{24,20},{28,24},{32,28},{36,32}... | collective-permute-start | bytes 1572872 | tf_op jit(solution)/shard_map/ppermute | solution.py:22
  221.7 213.6 %reduce-scatter.3.cloned.1.call-done = f32[16,1024]{1,0:T(8,128)} async-done(((f32[1024,1024]{1,0:T(8,128)}), f32[16,1024]{1,0:T(8,128)}) %reduce-scatter.3.cloned.1.call-update) | async-done | bytes 65552 | tf_op jit(solution)/shard_map/reduce_scatter | solution.py:144
  436.7 3.2 fusion.34
  439.9 22.3 %reduce-scatter.5.cloned.1.call-done = bf16[16,256]{1,0:T(8,128)(2,1)} async-done(((bf16[16,1024]{1,0:T(8,128)(2,1)}), bf16[16,256]{1,0:T(8,128)(2,1)}) %reduce-scatter.5.cloned.1.call-update) | async-done | bytes 8208 | tf_op jit(solution)/shard_map/reduce_scatter | solution.py:150
  (103 shorter events, 57.7 us)
Async XLA Ops:
  7.2 18.5 %copy-start = (bf16[1,1,2,128,1024]{4,3,2,1,0:T(8,128)(2,1)S(1)}, bf16[1,1,2,128,1024]{4,3,2,1,0:T(8,128)(2,1)}, u32[]{:S(2)}) copy-start(bf16[1,1,2,128,1024]{4,3,2,1,0:T(8,128)(2,1)} %param.7) | copy-start | bytes 1572868
  7.2 428.1 %reduce-scatter.3.cloned.1.call-start = ((), (), s32[]{:S(2)}) async-start(), calls=%async_computation.2 | async-start | bytes 4259840 | tf_op jit(solution)/shard_map/reduce_scatter | solution.py:144
  7.2 2.6 copy-start.11
  12.1 13.3 %copy-start.10 = (s32[1,64,2,128]{3,2,1,0:T(2,128)S(1)}, s32[1,64,2,128]{3,2,1,0:T(2,128)}, u32[]{:S(2)}) copy-start(s32[1,64,2,128]{3,2,1,0:T(2,128)} %param.5) | copy-start | bytes 196612
  12.2 21.3 %collective-permute-start.3 = (bf16[2,1,1,128,1024]{4,3,2,1,0:T(8,128)(2,1)S(1)}, bf16[2,1,1,128,1024]{4,3,2,1,0:T(8,128)(2,1)}, u32[]{:S(2)}, u32[]{:S(2)}) collective-permute-start(bf16[2,1,1,128,1024]{4,3,2,1,0:T(8,128)(2,1)S(1)} %fusion.62), channel_id=1, source_target_pairs={{4,0},{8,4},{12,8},{16,12},{20,16},{24,20},{28,24},{32,28},{36,32}... | collective-permute-start | bytes 1572872 | tf_op jit(solution)/shard_map/ppermute | solution.py:22
  23.3 23.8 %collective-permute-start = (bf16[2,1,1,128,1024]{4,3,2,0,1:T(8,128)(2,1)}, bf16[2,1,1,128,1024]{4,3,2,0,1:T(8,128)(2,1)}, u32[]{:S(2)}, u32[]{:S(2)}) collective-permute-start(bf16[2,1,1,128,1024]{4,3,2,0,1:T(8,128)(2,1)} %slice.131), channel_id=1, source_target_pairs={{0,4},{4,8},{8,12},{12,16},{16,20},{20,24},{24,28},{28,32},{32,36}... | collective-permute-start | bytes 1572872 | tf_op jit(solution)/shard_map/ppermute | solution.py:21
  35.4 19.3 %collective-permute-start.4 = (bf16[2,1,1,128,1024]{4,3,2,0,1:T(8,128)(2,1)}, bf16[2,1,1,128,1024]{4,3,2,0,1:T(8,128)(2,1)S(1)}, u32[]{:S(2)}, u32[]{:S(2)}) collective-permute-start(bf16[2,1,1,128,1024]{4,3,2,0,1:T(8,128)(2,1)} %bitcast.9), channel_id=1, source_target_pairs={{4,0},{8,4},{12,8},{16,12},{20,16},{24,20},{28,24},{32,28},{36,32}... | collective-permute-start | bytes 1572872 | tf_op jit(solution)/shard_map/ppermute | solution.py:22
  45.5 18.6 %copy-start.12 = (bf16[1,1,2,128,1024]{4,3,2,1,0:T(8,128)(2,1)S(1)}, bf16[1,1,2,128,1024]{4,3,2,1,0:T(8,128)(2,1)}, u32[]{:S(2)}) copy-start(bf16[1,1,2,128,1024]{4,3,2,1,0:T(8,128)(2,1)} %param.4) | copy-start | bytes 1572868
  47.1 20.2 %collective-permute-start.1 = (bf16[2,1,1,128,1024]{4,3,2,0,1:T(8,128)(2,1)}, bf16[2,1,1,128,1024]{4,3,2,0,1:T(8,128)(2,1)}, u32[]{:S(2)}, u32[]{:S(2)}) collective-permute-start(bf16[2,1,1,128,1024]{4,3,2,0,1:T(8,128)(2,1)} %collective-permute-done), channel_id=1, source_target_pairs={{0,4},{4,8},{8,12},{12,16},{16,20},{20,24},{24,28},{28,32},{32,36}... | collective-permute-start | bytes 1572872 | tf_op jit(solution)/shard_map/ppermute | solution.py:21
  55.6 18.2 %collective-permute-start.5 = (bf16[2,1,1,128,1024]{4,3,2,0,1:T(8,128)(2,1)}, bf16[2,1,1,128,1024]{4,3,2,0,1:T(8,128)(2,1)}, u32[]{:S(2)}, u32[]{:S(2)}) collective-permute-start(bf16[2,1,1,128,1024]{4,3,2,0,1:T(8,128)(2,1)} %broadcast_select_fusion), channel_id=1, source_target_pairs={{4,0},{8,4},{12,8},{16,12},{20,16},{24,20},{28,24},{32,28},{36,32}... | collective-permute-start | bytes 1572872 | tf_op jit(solution)/shard_map/ppermute | solution.py:22
  67.2 18.0 %collective-permute-start.2 = (bf16[2,1,1,128,1024]{4,3,2,0,1:T(8,128)(2,1)}, bf16[2,1,1,128,1024]{4,3,2,0,1:T(8,128)(2,1)}, u32[]{:S(2)}, u32[]{:S(2)}) collective-permute-start(bf16[2,1,1,128,1024]{4,3,2,0,1:T(8,128)(2,1)} %collective-permute-done.1), channel_id=1, source_target_pairs={{0,4},{4,8},{8,12},{12,16},{16,20},{20,24},{24,28},{28,32},{32,36}... | collective-permute-start | bytes 1572872 | tf_op jit(solution)/shard_map/ppermute | solution.py:21
  109.5 4.0 copy-start.7
  109.5 4.3 copy-start.8
  113.8 1.9 copy-start.4
  119.0 343.3 %reduce-scatter.5.cloned.1.call-start = ((), (), s32[]{:S(2)}) async-start(), calls=%async_computation.3 | async-start | bytes 40960 | tf_op jit(solution)/shard_map/reduce_scatter | solution.py:150
  134.8 7.1 %copy-start.9 = (bf16[2,128,16,64]{1,3,2,0:T(8,128)(2,1)S(1)}, bf16[2,128,16,64]{1,3,2,0:T(8,128)(2,1)}, u32[]{:S(2)}) copy-start(bf16[2,128,16,64]{1,3,2,0:T(8,128)(2,1)} %copy.40) | copy-start | bytes 1572868
  139.9 2.0 copy-start.5
  157.9 18.6 %collective-permute-start.6 = (bf16[2,1,1,128,1024]{4,3,0,2,1:T(8,128)(2,1)S(1)}, bf16[2,1,1,128,1024]{4,3,0,2,1:T(8,128)(2,1)S(1)}, u32[]{:S(2)}, u32[]{:S(2)}) collective-permute-start(bf16[2,1,1,128,1024]{4,3,0,2,1:T(8,128)(2,1)S(1)} %get-tuple-element.22), channel_id=1, source_target_pairs={{0,4},{4,8},{8,12},{12,16},{16,20},{20,24},{24,28},{28,32},{32,36}... | collective-permute-start | bytes 1572872 | tf_op jit(solution)/shard_map/ppermute | solution.py:21
  159.8 17.9 %collective-permute-start.7 = (bf16[2,1,1,128,1024]{4,3,0,2,1:T(8,128)(2,1)S(1)}, bf16[2,1,1,128,1024]{4,3,0,2,1:T(8,128)(2,1)S(1)}, u32[]{:S(2)}, u32[]{:S(2)}) collective-permute-start(bf16[2,1,1,128,1024]{4,3,0,2,1:T(8,128)(2,1)S(1)} %get-tuple-element.23), channel_id=1, source_target_pairs={{4,0},{8,4},{12,8},{16,12},{20,16},{24,20},{28,24},{32,28},{36,32}... | collective-permute-start | bytes 1572872 | tf_op jit(solution)/shard_map/ppermute | solution.py:22
  178.6 17.7 %collective-permute-start.8 = (bf16[2,1,1,128,1024]{4,3,0,2,1:T(8,128)(2,1)S(1)}, bf16[2,1,1,128,1024]{4,3,0,2,1:T(8,128)(2,1)S(1)}, u32[]{:S(2)}, u32[]{:S(2)}) collective-permute-start(bf16[2,1,1,128,1024]{4,3,0,2,1:T(8,128)(2,1)S(1)} %get-tuple-element.20), channel_id=1, source_target_pairs={{0,4},{4,8},{8,12},{12,16},{16,20},{20,24},{24,28},{28,32},{32,36}... | collective-permute-start | bytes 1572872 | tf_op jit(solution)/shard_map/ppermute | solution.py:21
  180.6 17.0 %collective-permute-start.9 = (bf16[2,1,1,128,1024]{4,3,0,2,1:T(8,128)(2,1)S(1)}, bf16[2,1,1,128,1024]{4,3,0,2,1:T(8,128)(2,1)S(1)}, u32[]{:S(2)}, u32[]{:S(2)}) collective-permute-start(bf16[2,1,1,128,1024]{4,3,0,2,1:T(8,128)(2,1)S(1)} %get-tuple-element.21), channel_id=1, source_target_pairs={{4,0},{8,4},{12,8},{16,12},{20,16},{24,20},{28,24},{32,28},{36,32}... | collective-permute-start | bytes 1572872 | tf_op jit(solution)/shard_map/ppermute | solution.py:22
  197.7 2.2 copy-start.3
  197.8 3.4 copy-start.2
  197.8 17.3 %slice-start = ((s8[8388608]{0:T(1024)(128)(4,1)}), s8[4194304]{0:T(1024)(128)(4,1)S(1)}, s32[]{:S(2)}) async-start(s8[8388608]{0:T(1024)(128)(4,1)} %bitcast.179), calls=%async_computation.4 | async-start | bytes 8388608
  201.2 11.8 %copy-start.6 = (bf16[2,16,128,512]{3,2,1,0:T(8,128)(2,1)S(1)}, bf16[2,16,128,512]{3,2,1,0:T(8,128)(2,1)}, u32[]{:S(2)}) copy-start(bf16[2,16,128,512]{3,2,1,0:T(8,128)(2,1)} %copy-done.5) | copy-start | bytes 12582916
  201.2 13.9 %slice-start.1 = ((s8[8388608]{0:T(1024)(128)(4,1)}), s8[4194304]{0:T(1024)(128)(4,1)S(1)}, s32[]{:S(2)}) async-start(s8[8388608]{0:T(1024)(128)(4,1)} %bitcast.179), calls=%async_computation.5 | async-start | bytes 8388608
  201.8 16.9 %collective-permute-start.10 = (bf16[2,1,1,128,1024]{4,3,2,0,1:T(8,128)(2,1)S(1)}, bf16[2,1,1,128,1024]{4,3,2,0,1:T(8,128)(2,1)S(1)}, u32[]{:S(2)}, u32[]{:S(2)}) collective-permute-start(bf16[2,1,1,128,1024]{4,3,2,0,1:T(8,128)(2,1)S(1)} %get-tuple-element.18), channel_id=1, source_target_pairs={{0,4},{4,8},{8,12},{12,16},{16,20},{20,24},{24,28},{28,32},{32,36}... | collective-permute-start | bytes 1572872 | tf_op jit(solution)/shard_map/ppermute | solution.py:21
  204.1 16.0 %collective-permute-start.11 = (bf16[2,1,1,128,1024]{4,3,2,0,1:T(8,128)(2,1)S(1)}, bf16[2,1,1,128,1024]{4,3,2,0,1:T(8,128)(2,1)S(1)}, u32[]{:S(2)}, u32[]{:S(2)}) collective-permute-start(bf16[2,1,1,128,1024]{4,3,2,0,1:T(8,128)(2,1)S(1)} %get-tuple-element.19), channel_id=1, source_target_pairs={{4,0},{8,4},{12,8},{16,12},{20,16},{24,20},{28,24},{32,28},{36,32}... | collective-permute-start | bytes 1572872 | tf_op jit(solution)/shard_map/ppermute | solution.py:22
  436.7 26.9 %copy-start.1 = (bf16[1,1,2,128,1024]{4,3,2,1,0:T(8,128)(2,1)S(1)}, bf16[1,1,2,128,1024]{4,3,2,1,0:T(8,128)(2,1)}, u32[]{:S(2)}) copy-start(bf16[1,1,2,128,1024]{4,3,2,1,0:T(8,128)(2,1)} %param.7) | copy-start | bytes 1572868
Sparse Core Ops, SparseCore 0:
  119.1 316.0 reduce-scatter.2
  438.1 24.1 reduce-scatter.4
where the time goes:
time: 474 us; the launch traced here: 470 us
  waiting for transfers between devices  277 us (58%)
  starting transfers between devices  65.3 us (14%)
  local copies, waits for them, and re-layouts  49.2 us (10%)
  matrix products  41.6 us (9%)
  other arithmetic  22.4 us (5%)
  between operations  14.6 us (3%)
    reduce_scatter x1, waiting for transfers between devices, per_device(): lax.psum_scatter(lax.dot_general(out_rows, grad_rows, token_dims, preferr...  214 us
    ppermute x6, starting transfers between devices, with_halo(): after = lax.ppermute(initial, axis, down)  52.9 us
    ppermute x6, waiting for transfers between devices, with_halo(): before = lax.ppermute(last, axis, up)  26.2 us
    reduce_scatter x1, waiting for transfers between devices, per_device(): lax.psum_scatter(block_sum.astype(jnp.bfloat16), 'dp', scatter_dimension=...  22.3 us
    another operation x4, local copies, waits for them, and re-layouts, per_device(): jnp.stack([grad_k, grad_v])  21.3 us
    ppermute x6, waiting for transfers between devices, with_halo(): after = lax.ppermute(initial, axis, down)  15.2 us
    ppermute x6, starting transfers between devices, with_halo(): before = lax.ppermute(last, axis, up)  12.1 us
  transfers between devices with their start and end apart: 14, of which 12 were waited for; matrix products, arithmetic and copies ran while one was open for 14% of the time, Pallas kernels for 0%

commit v1 on v0

v1 whole, which is shorter than its diff:
```python
import jax
import jax.numpy as jnp
import numpy as np
from jax import lax
from jax.experimental import pallas as pl
from jax.experimental.pallas import tpu as pltpu
from jax.sharding import PartitionSpec as P

HEADS = 16
HEAD_DIM = 64
WIN = 4
BLOCK = 128
D = 1024
PAIR = 2 * HEAD_DIM
TILE = 256
BF = jnp.bfloat16
F32 = jnp.float32

BARRED = -1e30
FREE = 3e38
SCALE = HEAD_DIM**-0.5
EXP2_SCALE = float(SCALE * np.log2(np.e))

NN = (((1,), (0,)), ((), ()))
NT = (((1,), (1,)), ((), ()))


def mm(a, b, dims=NN):
    return lax.dot_general(a, b, dims, preferred_element_type=F32)


def params(mib):
    return pltpu.CompilerParams(vmem_limit_bytes=mib * 2**20)


def cost(flops, moved, exps=0):
    return pl.CostEstimate(flops=flops, bytes_accessed=moved, transcendentals=exps)


def weight_cols(which):
    return pl.BlockSpec((D, TILE), lambda t: (which, t))


def weight_rows(which):
    return pl.BlockSpec((TILE, D), lambda t: (which * (D // TILE) + t, 0))


def whole(shape):
    return pl.BlockSpec(shape, lambda t: (0,) * len(shape))


def own_kernel(x_ref, g_ref, wq_ref, wk_ref, wv_ref, wo_ref, q_ref, da_ref, kv_ref):
    x = x_ref[...].reshape(2 * BLOCK, D)
    g = g_ref[...].reshape(2 * BLOCK, D)
    q_ref[...] = mm(x, wq_ref[...]).astype(BF).reshape(2, BLOCK, TILE)
    da_ref[...] = mm(g, wo_ref[...], NT).astype(BF).reshape(2, BLOCK, TILE)
    kv_ref[0] = mm(x, wk_ref[...]).astype(BF).reshape(2, BLOCK, TILE)
    kv_ref[1] = mm(x, wv_ref[...]).astype(BF).reshape(2, BLOCK, TILE)


def own_projections(x, g, weights):
    rows = jax.ShapeDtypeStruct((2, BLOCK, D), BF)
    row_tile = pl.BlockSpec((2, BLOCK, TILE), lambda t: (0, 0, t))
    return pl.pallas_call(
        own_kernel,
        grid=(D // TILE,),
        in_specs=[
            whole((2, BLOCK, D)),
            whole((2, BLOCK, D)),
            weight_cols(0),
            weight_cols(1),
            weight_cols(2),
            weight_rows(3),
        ],
        out_specs=[row_tile, row_tile, pl.BlockSpec((2, 2, BLOCK, TILE), lambda t: (0, 0, 0, t))],
        out_shape=[rows, rows, jax.ShapeDtypeStruct((2, 2, BLOCK, D), BF)],
        compiler_params=params(32),
        cost_estimate=cost(8 * 2 * BLOCK * D * D, 8 * D * D + 12 * BLOCK * D),
        name="own_projections",
    )(x, g, weights, weights, weights, weights)


def halo_kernel(up_ref, down_ref, wk_ref, wv_ref, kv_ref):
    x = jnp.concatenate([up_ref[...], down_ref[...]], axis=0)
    kv_ref[0] = mm(x, wk_ref[...]).astype(BF).reshape(2, BLOCK, TILE)
    kv_ref[1] = mm(x, wv_ref[...]).astype(BF).reshape(2, BLOCK, TILE)


def halo_projections(up, down, weights):
    return pl.pallas_call(
        halo_kernel,
        grid=(D // TILE,),
        in_specs=[whole((BLOCK, D)), whole((BLOCK, D)), weight_cols(1), weight_cols(2)],
        out_specs=pl.BlockSpec((2, 2, BLOCK, TILE), lambda t: (0, 0, 0, t)),
        out_shape=jax.ShapeDtypeStruct((2, 2, BLOCK, D), BF),
        compiler_params=params(32),
        cost_estimate=cost(4 * 2 * BLOCK * D * D, 4 * D * D + 12 * BLOCK * D),
        name="halo_projections",
    )(up, down, weights, weights)


def attention_kernel(
    q_ref, da_ref, kv3_ref, kv2_ref, kv1_ref, kv0_ref, bias_ref,
    out_ref, dq_ref, d3_ref, d2_ref, d1_ref, d0_ref,
):
    lane = lax.broadcasted_iota(jnp.int32, (BLOCK, PAIR), 1)
    first = lane < HEAD_DIM

    def split(rows):
        zero = jnp.zeros_like(rows)
        return jnp.concatenate([jnp.where(first, rows, zero), jnp.where(first, zero, rows)], axis=0)

    def own_heads(square):
        return jnp.concatenate([square[:HEAD_DIM, :BLOCK], square[HEAD_DIM:, BLOCK:]], axis=0)

    kv_refs = (kv3_ref, kv2_ref, kv1_ref, kv0_ref)
    keys = jnp.concatenate([ref[0, 0] for ref in kv_refs], axis=0)
    values = jnp.concatenate([ref[1, 0] for ref in kv_refs], axis=0)
    d_attn = da_ref[0]
    q_split = split(q_ref[0])
    da_split = split(d_attn)
    bias = bias_ref[0]
    scores = jnp.minimum(mm(keys, q_split, NT), jnp.concatenate([bias, bias], axis=1))
    top = jnp.max(scores, axis=0, keepdims=True)
    terms = jnp.exp2((scores - top) * EXP2_SCALE)
    probs = terms * (1.0 / jnp.sum(terms, axis=0, keepdims=True))
    probs_low = probs.astype(BF)
    out_t = own_heads(mm(values.T, probs_low)).astype(BF)
    out_ref[0] = out_t.T
    weighted = d_attn.T.astype(F32) * out_t.astype(F32)
    delta = jnp.concatenate(
        [
            jnp.sum(weighted[:HEAD_DIM], axis=0, keepdims=True),
            jnp.sum(weighted[HEAD_DIM:], axis=0, keepdims=True),
        ],
        axis=1,
    )
    dscore = (probs * (mm(values, da_split, NT) - delta)).astype(BF)
    dq_ref[0] = (own_heads(mm(keys.T, dscore)) * SCALE).astype(BF).T
    d_keys = (mm(dscore, q_split) * SCALE).astype(BF)
    d_values = mm(probs_low, da_split).astype(BF)
    for place, ref in enumerate((d3_ref, d2_ref, d1_ref, d0_ref)):
        ref[0, 0] = d_keys[place * BLOCK : (place + 1) * BLOCK]
        ref[1, 0] = d_values[place * BLOCK : (place + 1) * BLOCK]


def attention(q, da, kvs, bias):
    rows = jax.ShapeDtypeStruct((2, BLOCK, D), BF)
    pairs = jax.ShapeDtypeStruct((2, 2, BLOCK, D), BF)
    row_spec = pl.BlockSpec((1, BLOCK, PAIR), lambda h, p: (h, 0, p))
    pair_spec = pl.BlockSpec((2, 1, BLOCK, PAIR), lambda h, p: (0, h, 0, p))
    bias_spec = pl.BlockSpec((1, WIN * BLOCK, BLOCK), lambda h, p: (h, 0, 0))
    return pl.pallas_call(
        attention_kernel,
        grid=(2, HEADS // 2),
        in_specs=[row_spec, row_spec] + [pair_spec] * 4 + [bias_spec],
        out_specs=[row_spec, row_spec] + [pair_spec] * 4,
        out_shape=[rows, rows] + [pairs] * 4,
        compiler_params=params(32),
        cost_estimate=cost(2 * 10 * BLOCK * WIN * BLOCK * D * 4, 12 * 2**20, 2**21),
        name="attention",
    )(q, da, *kvs, bias)


def back_kernel(d_ref, wk_ref, wv_ref, out_ref):
    rows = mm(d_ref[0].reshape(2 * BLOCK, D), wk_ref[...], NT)
    rows += mm(d_ref[1].reshape(2 * BLOCK, D), wv_ref[...], NT)
    out_ref[...] = rows.reshape(2, BLOCK, TILE).astype(out_ref.dtype)


def back_projections(d, weights, dtype):
    return pl.pallas_call(
        back_kernel,
        grid=(D // TILE,),
        in_specs=[whole((2, 2, BLOCK, D)), weight_rows(1), weight_rows(2)],
        out_specs=pl.BlockSpec((2, BLOCK, TILE), lambda t: (0, 0, t)),
        out_shape=jax.ShapeDtypeStruct((2, BLOCK, D), dtype),
        compiler_params=params(32),
        cost_estimate=cost(4 * 2 * BLOCK * D * D, 4 * D * D + 12 * BLOCK * D),
        name="back_projections",
    )(d, weights, weights)


def last_kernel(d_ref, dq_ref, wq_ref, wk_ref, wv_ref, out_ref):
    rows = mm(dq_ref[...].reshape(2 * BLOCK, D), wq_ref[...], NT)
    rows += mm(d_ref[0].reshape(2 * BLOCK, D), wk_ref[...], NT)
    rows += mm(d_ref[1].reshape(2 * BLOCK, D), wv_ref[...], NT)
    out_ref[...] = rows.reshape(2, BLOCK, TILE)


def last_projections(d, dq, weights):
    return pl.pallas_call(
        last_kernel,
        grid=(D // TILE,),
        in_specs=[
            whole((2, 2, BLOCK, D)),
            whole((2, BLOCK, D)),
            weight_rows(0),
            weight_rows(1),
            weight_rows(2),
        ],
        out_specs=pl.BlockSpec((2, BLOCK, TILE), lambda t: (0, 0, t)),
        out_shape=jax.ShapeDtypeStruct((2, BLOCK, D), F32),
        compiler_params=params(32),
        cost_estimate=cost(6 * 2 * BLOCK * D * D, 6 * D * D + 16 * BLOCK * D),
        name="last_projections",
    )(d, dq, weights, weights, weights)


def outer_kernel(core_ref, o_ref, keep_ref, send_ref, kept_ref, sent_ref):
    o_t = o_ref[...].reshape(2 * BLOCK, D).T
    for g_ref, r_ref in ((send_ref, sent_ref), (keep_ref, kept_ref)):
        product = mm(o_t, g_ref[...].reshape(2 * BLOCK, TILE)).astype(BF)
        r_ref[0, 0] = product[:, :BLOCK]
        r_ref[0, 1] = product[:, BLOCK:]


def outer_products(o, g, core):
    result = jax.ShapeDtypeStruct((2, 2, D, BLOCK), BF)
    result_spec = pl.BlockSpec((1, 2, D, BLOCK), lambda y, c: (y, 0, 0, 0))
    return pl.pallas_call(
        outer_kernel,
        grid_spec=pltpu.PrefetchScalarGridSpec(
            num_scalar_prefetch=1,
            grid=(2,),
            in_specs=[
                pl.BlockSpec((2, BLOCK, D), lambda y, c: (0, 0, 0)),
                pl.BlockSpec((2, BLOCK, TILE), lambda y, c: (0, 0, 2 * y + c[0])),
                pl.BlockSpec((2, BLOCK, TILE), lambda y, c: (0, 0, 2 * y + 1 - c[0])),
            ],
            out_specs=[result_spec, result_spec],
        ),
        out_shape=[result, result],
        compiler_params=params(32),
        cost_estimate=cost(4 * BLOCK * D * D, 2 * D * D + 8 * BLOCK * D),
        name="outer_products",
    )(core.reshape(1), o, g, g)


def chip_pairs(move):
    pairs = []
    for y in range(4):
        for x in range(4):
            for z in range(8):
                y2, x2, z2 = move(y, x, z)
                for core in range(2):
                    pairs.append((place(y, x, z, core), place(y2, x2, z2, core)))
    return pairs


def place(y, x, z, core):
    return ((y % 2) * 32 + x * 8 + z) * 4 + (y // 2) * 2 + core


FLIP = ((1, 0, 3, 2), (3, 2, 1, 0))


def add(a, b):
    return (a.astype(F32) + b.astype(F32)).astype(BF)


def ring_first(v, dim, index, pairs):
    def pick(i):
        return lax.slice_in_dim(v, i, i + 1, axis=dim)

    outer = jnp.concatenate([pick(0), pick(3)], axis=dim)
    inner = lax.slice_in_dim(v, 1, 3, axis=dim)
    mine = (index == 0) | (index == 3)
    moved = lax.ppermute(jnp.where(mine, inner, outer), ("blk", "dp"), pairs)
    return add(jnp.where(mine, outer, inner), moved)


def halve(v, dim, bit, pairs):
    low = lax.slice_in_dim(v, 0, 1, axis=dim)
    high = lax.slice_in_dim(v, 1, 2, axis=dim)
    moved = lax.ppermute(jnp.where(bit == 0, high, low), ("blk", "dp"), pairs)
    return add(jnp.where(bit == 0, low, high), moved)


def reduce_outer(kept, sent, y, x, z):
    core_pairs = [(i, i ^ 1) for i in range(4)]
    total = add(kept, lax.ppermute(sent, "dp", core_pairs))
    total = total.reshape(2, 2, 2, 4, 8, 16, BLOCK)
    parts = [total[:, i].reshape(4, 4, 8, 16, BLOCK) for i in range(2)]
    rings = (
        (0, y, [chip_pairs(lambda a, b, c, f=f: (f[a], b, c)) for f in FLIP]),
        (1, x, [chip_pairs(lambda a, b, c, f=f: (a, f[b], c)) for f in FLIP]),
    )
    for turn in range(2):
        dim_of = [rings[(i + turn + 1) % 2] for i in range(2)]
        parts = [ring_first(v, d, i, m[0]) for v, (d, i, m) in zip(parts, dim_of)]
        parts = [halve(v, d, i // 2, m[1]) for v, (d, i, m) in zip(parts, dim_of)]
    v = jnp.concatenate(parts, axis=0).reshape(2, 2, 2, 2, 16, BLOCK)
    for k, dim in ((1, 3), (2, 2), (4, 1)):
        v = halve(v, dim, (z // k) % 2, chip_pairs(lambda a, b, c, k=k: (a, b, c ^ k)))
    v = v.reshape(2, 16, BLOCK)
    return jnp.concatenate([v[0], v[1]], axis=1).astype(F32)


def score_limits(key_valid, position):
    blocks = 2 * 64
    both = jnp.stack([position, blocks - 1 - position])
    seq_valid = jnp.concatenate([key_valid[0, :, 0], jnp.flip(key_valid[0, :, 1], axis=0)], axis=0)
    seq_valid = jnp.concatenate([jnp.zeros((WIN - 1, BLOCK), jnp.int32), seq_valid], axis=0)
    valid = jnp.stack(
        [lax.dynamic_slice_in_dim(seq_valid, both[i], WIN, 0).reshape(WIN * BLOCK) for i in range(2)]
    )
    q_pos = jnp.arange(BLOCK, dtype=jnp.int32)[None, None, :]
    k_pos = (jnp.arange(WIN * BLOCK, dtype=jnp.int32) - (WIN - 1) * BLOCK)[None, :, None]
    inside = k_pos + both[:, None, None] * BLOCK >= 0
    allowed = inside & (k_pos <= q_pos) & ((valid[:, :, None] == 1) | (k_pos == q_pos))
    return jnp.where(allowed, FREE, BARRED).astype(F32)


def per_device(tokens, key_valid, weights, out_grad):
    position = lax.axis_index("blk")
    shot = lax.axis_index("dp")
    at_last = position == 63
    up = [(i, i + 1) for i in range(63)]
    down = [(i + 1, i) for i in range(63)]
    x = tokens.reshape(2, BLOCK, D)
    g = out_grad.reshape(2, BLOCK, D)

    bias = score_limits(key_valid, position)
    q, da, kv0 = own_projections(x, g, weights)
    kvs = [kv0]
    state_up, state_down = x[0], x[1]
    for _ in range(WIN - 1):
        new_up = lax.ppermute(state_up, "blk", up)
        new_down = jnp.where(at_last, state_up, lax.ppermute(state_down, "blk", down))
        kvs.append(halo_projections(new_up, new_down, weights))
        state_up, state_down = new_up, new_down
    o, dq, d3, d2, d1, d0 = attention(q, da, kvs[::-1], bias)

    kept, sent = outer_products(o, g, shot % 2)
    w_grad = reduce_outer(kept, sent, (shot // 2) * 2 + position // 32, (position // 8) % 4, position % 8)

    returned = back_projections(d3, weights, BF)
    terms = [back_projections(d2, weights, BF), back_projections(d1, weights, BF), last_projections(d0, dq, weights)]
    for term in terms:
        from_after = lax.ppermute(returned[0], "blk", down)
        from_before = lax.ppermute(returned[1], "blk", up)
        extra = jnp.where(at_last, returned[1], jnp.zeros_like(returned[1])).astype(F32)
        total = jnp.stack(
            [term[0].astype(F32) + from_after.astype(F32) + extra, term[1].astype(F32) + from_before.astype(F32)]
        )
        returned = total.astype(BF)
    return returned.reshape(tokens.shape), w_grad


def solution(mesh):
    placed = (
        P("dp", "blk", None, None, None),
        P("dp", None, None, None),
        P(),
        P("dp", "blk", None, None, None),
    )
    return jax.shard_map(
        per_device,
        mesh=mesh,
        in_specs=placed,
        out_specs=(P("dp", "blk", None, None, None), P("blk", "dp")),
        check_vma=False,
    )
```

time: 474 us -> 180 us (0.38)
  waiting for transfers between devices: 277 us -> 47.4 us
  Pallas kernels: 0 us -> 41.9 us
  matrix products: 41.6 us -> 0 us
  local copies, waits for them, and re-layouts: 49.2 us -> 14.6 us
  other arithmetic: 22.4 us -> 7.49 us
  between operations: 14.6 us -> 1.64 us
    reduce_scatter x2 -> x0, waiting for transfers between devices: 236 us -> none  [the longest x1 214 us: per_device(): lax.psum_scatter(lax.dot_general(out_rows, grad_rows, token_dims, preferr...]
    pallas_call x0 -> x10, Pallas kernels: none -> 41.9 us  [the longest x1 20.2 us: attention(): pl.pallas_call(attention_kernel, grid=(2, HEADS // 2), in_specs=[row_spec...]
    dot_general x13 -> x0, matrix products: 34.3 us -> none  [the longest x1 5.12 us: per_device(): jnp.einsum('sxqhd,sxkhd->sxhqk', dout_heads, values_all, preferred_elemen...]
    another operation x9 -> x0, local copies, waits for them, and re-layouts: 29.8 us -> none  [the longest x4 21.3 us: per_device(): jnp.stack([grad_k, grad_v])]
    slice x9 -> x4, local copies, waits for them, and re-layouts: 11 us -> 1.17 us  [the longest x1 0.98 us: score_limits(): key_valid[0, :, 0]]
    sub x1 -> x0, matrix products: 7.31 us -> none  [per_device(): exp_terms = jnp.exp(scores - row_max)]
    unnamed x32 -> x38, local copies, waits for them, and re-layouts: 6.04 us -> 12.2 us
    ppermute x12 -> x24, waiting for transfers between devices: 41.4 us -> 47.4 us  [the longest x7 14.6 us: halve(): moved = lax.ppermute(jnp.where(bit == 0, high, low), ('blk', 'dp'), pairs)]
  transfers between devices with their start and end apart: 14 -> 24, of which waited for: 12 -> 13; matrix products, arithmetic and copies ran while one was open for 14% -> 5% of each run, Pallas kernels for 0% -> 10%
where the time goes in v1:
time: 180 us; the launch traced here: 178 us
  starting transfers between devices  65.1 us (36%)
  waiting for transfers between devices  47.4 us (26%)
  Pallas kernels  41.9 us (23%)
  local copies, waits for them, and re-layouts  14.6 us (8%)
  other arithmetic  7.49 us (4%)
    ppermute x3, starting transfers between devices, per_device(): lax.ppermute(state_down, 'blk', down)  27.4 us
    pallas_call x1, Pallas kernels, attention(): pl.pallas_call(attention_kernel, grid=(2, HEADS // 2), in_specs=[row_spec...  20.2 us
    ppermute x3, starting transfers between devices, per_device(): from_after = lax.ppermute(returned[0], 'blk', down)  16.5 us
    ppermute x7, waiting for transfers between devices, halve(): moved = lax.ppermute(jnp.where(bit == 0, high, low), ('blk', 'dp'), pairs)  14.6 us
    unnamed x38, local copies, waits for them, and re-layouts  12.2 us
    ppermute x3, starting transfers between devices, per_device(): from_before = lax.ppermute(returned[1], 'blk', up)  9.75 us
    ppermute x4, waiting for transfers between devices, ring_first(): moved = lax.ppermute(jnp.where(mine, inner, outer), ('blk', 'dp'), pairs)  9.69 us
    ppermute x3, waiting for transfers between devices, per_device(): from_before = lax.ppermute(returned[1], 'blk', up)  8.6 us
  transfers between devices with their start and end apart: 24, of which 13 were waited for; matrix products, arithmetic and copies ran while one was open for 5% of the time, Pallas kernels for 10%

profile of v1, /device:TPU:24, one launch (start us, length us, event | category | flops | bytes accessed | tf_op | source)
XLA Modules:
  0.0 178.2 jit_solution(18265537626214222172)
XLA Ops:
  1.8 10.1 %collective-permute-start.3 = (bf16[128,1024]{1,0:T(8,128)(2,1)S(1)}, bf16[128,1024]{1,0:T(8,128)(2,1)S(1)}, u32[]{:S(2)}, u32[]{:S(2)}) collective-permute-start(bf16[128,1024]{1,0:T(8,128)(2,1)S(1)} %get-tuple-element.36), channel_id=1, source_target_pairs={{4,0},{8,4},{12,8},{16,12},{20,16},{24,20},{28,24},{32,28},{36,32}... | collective-permute-start | bytes 786440 | tf_op jit(solution)/shard_map/ppermute | solution.py:330
  12.0 1.9 %collective-permute-start = (bf16[128,1024]{1,0:T(8,128)(2,1)S(1)}, bf16[128,1024]{1,0:T(8,128)(2,1)S(1)}, u32[]{:S(2)}, u32[]{:S(2)}) collective-permute-start(bf16[128,1024]{1,0:T(8,128)(2,1)S(1)} %get-tuple-element.37), channel_id=1, source_target_pairs={{0,4},{4,8},{8,12},{12,16},{16,20},{20,24},{24,28},{28,32},{32,36}... | collective-permute-start | bytes 786440 | tf_op jit(solution)/shard_map/ppermute | solution.py:329
  15.3 2.2 %collective-permute-done.3 = bf16[128,1024]{1,0:T(8,128)(2,1)S(1)} collective-permute-done((bf16[128,1024]{1,0:T(8,128)(2,1)S(1)}, bf16[128,1024]{1,0:T(8,128)(2,1)S(1)}, u32[]{:S(2)}, u32[]{:S(2)}) %collective-permute-start.3) | collective-permute-done | bytes 262176 | tf_op jit(solution)/shard_map/ppermute | solution.py:330
  18.5 8.6 %collective-permute-start.4 = (bf16[128,1024]{1,0:T(8,128)(2,1)S(1)}, bf16[128,1024]{1,0:T(8,128)(2,1)S(1)}, u32[]{:S(2)}, u32[]{:S(2)}) collective-permute-start(bf16[128,1024]{1,0:T(8,128)(2,1)S(1)} %broadcast_select_fusion.4.down_ref), channel_id=1, source_target_pairs={{4,0},{8,4},{12,8},{16,12},{20,16},{24,20},{28,24},{32,28},{36,32}... | collective-permute-start | bytes 786440 | tf_op jit(solution)/shard_map/ppermute | solution.py:330
  31.8 8.6 %collective-permute-start.5 = (bf16[128,1024]{1,0:T(8,128)(2,1)S(1)}, bf16[128,1024]{1,0:T(8,128)(2,1)S(1)}, u32[]{:S(2)}, u32[]{:S(2)}) collective-permute-start(bf16[128,1024]{1,0:T(8,128)(2,1)S(1)} %broadcast_select_fusion.3.down_ref), channel_id=1, source_target_pairs={{4,0},{8,4},{12,8},{16,12},{20,16},{24,20},{28,24},{32,28},{36,32}... | collective-permute-start | bytes 786440 | tf_op jit(solution)/shard_map/ppermute | solution.py:330
  40.4 3.4 %copy-done = bf16[4096,1024]{1,0:T(8,128)(2,1)S(1)} copy-done((bf16[4096,1024]{1,0:T(8,128)(2,1)S(1)}, bf16[4096,1024]{1,0:T(8,128)(2,1)}, u32[]{:S(2)}) %copy-start) | copy-done | bytes 8388632
  43.8 4.0 %own_projections.1 = (bf16[2,128,1024]{2,1,0:T(8,128)(2,1)S(1)}, bf16[2,128,1024]{2,1,0:T(8,128)(2,1)S(1)}, bf16[2,2,128,1024]{3,2,1,0:T(8,128)(2,1)S(1)}) custom-call(bf16[2,128,1024]{2,1,0:T(8,128)(2,1)S(1)} %bitcast.85, bf16[2,128,1024]{2,1,0:T(8,128)(2,1)S(1)} %bitcast.86, bf16[4096,1024]{1,0:T(8,128)(2,1)S(1)} %copy-done, ...), custom_call_target="tpu_custom_call" | custom-call | flops 2147483648 | bytes 9961472 | tf_op jit(solution)/shard_map/own_projections/pallas_call | solution.py:64
  49.6 3.6 %copy-done.1 = bf16[4096,1024]{1,0:T(8,128)(2,1)S(1)} copy-done((bf16[4096,1024]{1,0:T(8,128)(2,1)S(1)}, bf16[4096,1024]{1,0:T(8,128)(2,1)}, u32[]{:S(2)}) %copy-start.1) | copy-done | bytes 8388632
  53.2 2.4 %halo_projections.5.kv1_ref = bf16[2,2,128,1024]{3,2,1,0:T(8,128)(2,1)S(1)} custom-call(bf16[128,1024]{1,0:T(8,128)(2,1)S(1)} %collective-permute-done.up_ref, bf16[128,1024]{1,0:T(8,128)(2,1)S(1)} %broadcast_select_fusion.4.down_ref, bf16[4096,1024]{1,0:T(8,128)(2,1)S(1)} %copy-done.1, bf16[4096,1024]{1,0:T(8,128)(2,1)S(1)} %copy-done.1), custom_call_target="tpu_custom_call" | custom-call | flops 1073741824 | bytes 5767168 | tf_op jit(solution)/shard_map/halo_projections/pallas_call | solution.py:90
  55.6 1.9 %collective-permute-start.2 = (bf16[128,1024]{1,0:T(8,128)(2,1)S(1)}, bf16[128,1024]{1,0:T(8,128)(2,1)S(1)}, u32[]{:S(2)}, u32[]{:S(2)}) collective-permute-start(bf16[128,1024]{1,0:T(8,128)(2,1)S(1)} %collective-permute-done.1.up_ref), channel_id=1, source_target_pairs={{0,4},{4,8},{8,12},{12,16},{16,20},{20,24},{24,28},{28,32},{32,36}... | collective-permute-start | bytes 786440 | tf_op jit(solution)/shard_map/ppermute | solution.py:329
  57.6 2.4 %halo_projections.4.kv2_ref = bf16[2,2,128,1024]{3,2,1,0:T(8,128)(2,1)S(1)} custom-call(bf16[128,1024]{1,0:T(8,128)(2,1)S(1)} %collective-permute-done.1.up_ref, bf16[128,1024]{1,0:T(8,128)(2,1)S(1)} %broadcast_select_fusion.3.down_ref, bf16[4096,1024]{1,0:T(8,128)(2,1)S(1)} %copy-done.1, bf16[4096,1024]{1,0:T(8,128)(2,1)S(1)} %copy-done.1), custom_call_target="tpu_custom_call" | custom-call | flops 1073741824 | bytes 5767168 | tf_op jit(solution)/shard_map/halo_projections/pallas_call | solution.py:90
  60.1 8.0 %collective-permute-done.2.up_ref = bf16[128,1024]{1,0:T(8,128)(2,1)S(1)} collective-permute-done((bf16[128,1024]{1,0:T(8,128)(2,1)S(1)}, bf16[128,1024]{1,0:T(8,128)(2,1)S(1)}, u32[]{:S(2)}, u32[]{:S(2)}) %collective-permute-start.2) | collective-permute-done | bytes 262176 | tf_op jit(solution)/shard_map/ppermute | solution.py:329
  68.1 2.4 %halo_projections.3.kv3_ref = bf16[2,2,128,1024]{3,2,1,0:T(8,128)(2,1)S(1)} custom-call(bf16[128,1024]{1,0:T(8,128)(2,1)S(1)} %collective-permute-done.2.up_ref, bf16[128,1024]{1,0:T(8,128)(2,1)S(1)} %broadcast_select_fusion.2.down_ref, bf16[4096,1024]{1,0:T(8,128)(2,1)S(1)} %copy-done.1, bf16[4096,1024]{1,0:T(8,128)(2,1)S(1)} %copy-done.1), custom_call_target="tpu_custom_call" | custom-call | flops 1073741824 | bytes 5767168 | tf_op jit(solution)/shard_map/halo_projections/pallas_call | solution.py:90
  70.6 20.2 %attention.1 = (bf16[2,128,1024]{2,1,0:T(8,128)(2,1)S(1)}, bf16[2,128,1024]{2,1,0:T(8,128)(2,1)S(1)}, bf16[2,2,128,1024]{3,2,1,0:T(8,128)(2,1)S(1)}, bf16[2,2,12...) custom-call(bf16[2,128,1024]{2,1,0:T(8,128)(2,1)S(1)} %copy-done.13, ...), custom_call_target="tpu_custom_call" | custom-call | flops 5368709120 | bytes 12582912 | tf_op jit(solution)/shard_map/attention/pallas_call | solution.py:153
  92.8 2.0 %back_projections.5 = bf16[2,128,1024]{2,1,0:T(8,128)(2,1)S(1)} custom-call(bf16[2,2,128,1024]{3,2,1,0:T(8,128)(2,1)S(1)} %get-tuple-element.20.d_ref, bf16[4096,1024]{1,0:T(8,128)(2,1)S(1)} %bitcast.84, bf16[4096,1024]{1,0:T(8,128)(2,1)S(1)} %bitcast.84), custom_call_target="tpu_custom_call" | custom-call | flops 1073741824 | bytes 5767168 | tf_op jit(solution)/shard_map/back_projections/pallas_call | solution.py:172
  94.8 1.9 %collective-permute-start.6 = (bf16[128,1024]{1,0:T(8,128)(2,1)S(1)}, bf16[128,1024]{1,0:T(8,128)(2,1)S(1)}, u32[]{:S(2)}, u32[]{:S(2)}) collective-permute-start(bf16[128,1024]{1,0:T(8,128)(2,1)S(1)} %get-tuple-element.35), channel_id=1, source_target_pairs={{4,0},{8,4},{12,8},{16,12},{20,16},{24,20},{28,24},{32,28},{36,32}... | collective-permute-start | bytes 786440 | tf_op jit(solution)/shard_map/ppermute | solution.py:341
  96.8 3.9 %collective-permute-start.8 = (bf16[128,1024]{1,0:T(8,128)(2,1)S(1)}, bf16[128,1024]{1,0:T(8,128)(2,1)S(1)}, u32[]{:S(2)}, u32[]{:S(2)}) collective-permute-start(bf16[128,1024]{1,0:T(8,128)(2,1)S(1)} %get-tuple-element.34), channel_id=1, source_target_pairs={{0,4},{4,8},{8,12},{12,16},{16,20},{20,24},{24,28},{28,32},{32,36}... | collective-permute-start | bytes 786440 | tf_op jit(solution)/shard_map/ppermute | solution.py:342
  100.7 2.0 %back_projections.4 = bf16[2,128,1024]{2,1,0:T(8,128)(2,1)S(1)} custom-call(bf16[2,2,128,1024]{3,2,1,0:T(8,128)(2,1)S(1)} %get-tuple-element.19.d_ref, bf16[4096,1024]{1,0:T(8,128)(2,1)S(1)} %bitcast.84, bf16[4096,1024]{1,0:T(8,128)(2,1)S(1)} %bitcast.84), custom_call_target="tpu_custom_call" | custom-call | flops 1073741824 | bytes 5767168 | tf_op jit(solution)/shard_map/back_projections/pallas_call | solution.py:172
  102.7 2.7 %collective-permute-done.6 = bf16[128,1024]{1,0:T(8,128)(2,1)S(1)} collective-permute-done((bf16[128,1024]{1,0:T(8,128)(2,1)S(1)}, bf16[128,1024]{1,0:T(8,128)(2,1)S(1)}, u32[]{:S(2)}, u32[]{:S(2)}) %collective-permute-start.6) | collective-permute-done | bytes 262176 | tf_op jit(solution)/shard_map/ppermute | solution.py:341
  106.2 6.4 %collective-permute-start.7 = (bf16[128,1024]{1,0:T(8,128)(2,1)}, bf16[128,1024]{1,0:T(8,128)(2,1)S(1)}, u32[]{:S(2)}, u32[]{:S(2)}) collective-permute-start(bf16[128,1024]{1,0:T(8,128)(2,1)} %fusion.8), channel_id=1, source_target_pairs={{4,0},{8,4},{12,8},{16,12},{20,16},{24,20},{28,24},{32,28},{36,32}... | collective-permute-start | bytes 786440 | tf_op jit(solution)/shard_map/ppermute | solution.py:341
  112.9 3.4 %copy-done.2 = bf16[4096,1024]{1,0:T(8,128)(2,1)S(1)} copy-done((bf16[4096,1024]{1,0:T(8,128)(2,1)S(1)}, bf16[4096,1024]{1,0:T(8,128)(2,1)}, u32[]{:S(2)}) %copy-start.2) | copy-done | bytes 8388632
  116.2 2.0 %back_projections.3 = bf16[2,128,1024]{2,1,0:T(8,128)(2,1)S(1)} custom-call(bf16[2,2,128,1024]{3,2,1,0:T(8,128)(2,1)S(1)} %get-tuple-element.18.d_ref, bf16[4096,1024]{1,0:T(8,128)(2,1)S(1)} %copy-done.2, bf16[4096,1024]{1,0:T(8,128)(2,1)S(1)} %copy-done.2), custom_call_target="tpu_custom_call" | custom-call | flops 1073741824 | bytes 5767168 | tf_op jit(solution)/shard_map/back_projections/pallas_call | solution.py:172
  118.3 2.5 %last_projections.1 = f32[2,128,1024]{2,1,0:T(8,128)S(1)} custom-call(bf16[2,2,128,1024]{3,2,1,0:T(8,128)(2,1)S(1)} %copy-done.5, bf16[2,128,1024]{2,1,0:T(8,128)(2,1)S(1)} %copy-done.8, bf16[4096,1024]{1,0:T(8,128)(2,1)S(1)} %copy-done.2, bf16[4096,1024]{1,0:T(8,128)(2,1)S(1)} %copy-done.2, bf16[4096,1024]{1,0:T(8,128)(2,1)S(1)} %copy-done.2), custom_call_target="tpu_custom_call" | custom-call | flops 1610612736 | bytes 8388608 | tf_op jit(solution)/shard_map/last_projections/pallas_call | solution.py:192
  121.0 1.9 %collective-permute-start.10 = (bf16[128,1024]{1,0:T(8,128)(2,1)S(1)}, bf16[128,1024]{1,0:T(8,128)(2,1)S(1)}, u32[]{:S(2)}, u32[]{:S(2)}) collective-permute-start(bf16[128,1024]{1,0:T(8,128)(2,1)S(1)} %get-tuple-element.27), channel_id=1, source_target_pairs={{0,4},{4,8},{8,12},{12,16},{16,20},{20,24},{24,28},{28,32},{32,36}... | collective-permute-start | bytes 786440 | tf_op jit(solution)/shard_map/ppermute | solution.py:342
  122.9 8.1 %collective-permute-start.9 = (bf16[128,1024]{1,0:T(8,128)(2,1)S(1)}, bf16[128,1024]{1,0:T(8,128)(2,1)S(1)}, u32[]{:S(2)}, u32[]{:S(2)}) collective-permute-start(bf16[128,1024]{1,0:T(8,128)(2,1)S(1)} %get-tuple-element.26), channel_id=1, source_target_pairs={{4,0},{8,4},{12,8},{16,12},{20,16},{24,20},{28,24},{32,28},{36,32}... | collective-permute-start | bytes 786440 | tf_op jit(solution)/shard_map/ppermute | solution.py:341
  133.2 7.1 %collective-permute-done.13 = bf16[4,2,8,16,128]{4,3,2,0,1:T(8,128)(2,1)S(1)} collective-permute-done((bf16[4,2,8,16,128]{4,3,2,0,1:T(8,128)(2,1)S(1)}, bf16[4,2,8,16,128]{4,3,2,0,1:T(8,128)(2,1)S(1)}, u32[]{:S(2)}, u32[]{:S(2)}) %collective-permute-start.13) | collective-permute-done | bytes 262176 | tf_op jit(solution)/shard_map/ppermute | solution.py:269
  140.8 5.9 %collective-permute-done.14 = bf16[4,1,8,16,128]{4,3,2,0,1:T(8,128)(2,1)S(1)} collective-permute-done((bf16[4,1,8,16,128]{4,3,2,0,1:T(8,128)(2,1)S(1)}, bf16[4,1,8,16,128]{4,3,2,0,1:T(8,128)(2,1)S(1)}, u32[]{:S(2)}, u32[]{:S(2)}) %collective-permute-start.14) | collective-permute-done | bytes 131104 | tf_op jit(solution)/shard_map/ppermute | solution.py:276
  148.8 2.5 %collective-permute-done.15 = bf16[2,1,8,16,128]{4,3,2,0,1:T(8,128)(2,1)S(1)} collective-permute-done((bf16[2,1,8,16,128]{4,3,2,0,1:T(8,128)(2,1)S(1)}, bf16[2,1,8,16,128]{4,3,2,0,1:T(8,128)(2,1)S(1)}, u32[]{:S(2)}, u32[]{:S(2)}) %collective-permute-start.15) | collective-permute-done | bytes 65568 | tf_op jit(solution)/shard_map/ppermute | solution.py:269
  151.5 3.2 %collective-permute-start.20 = (bf16[1,1,8,16,128]{4,3,2,0,1:T(8,128)(2,1)S(1)}, bf16[1,1,8,16,128]{4,3,2,0,1:T(8,128)(2,1)S(1)}, u32[]{:S(2)}, u32[]{:S(2)}) collective-permute-start(bf16[1,1,8,16,128]{4,3,2,0,1:T(8,128)(2,1)S(1)} %broadcast_select_fusion.9), channel_id=1, source_target_pairs={{0,96},{1,97},{4,100},{5,101},{8,104},{9,105},{12,108},{13,109},{1... | collective-permute-start | bytes 98312 | tf_op jit(solution)/shard_map/ppermute | solution.py:276
  157.1 3.9 %collective-permute-start.11 = (bf16[128,1024]{1,0:T(8,128)(2,1)S(1)}, bf16[128,1024]{1,0:T(8,128)(2,1)S(1)}, u32[]{:S(2)}, u32[]{:S(2)}) collective-permute-start(bf16[128,1024]{1,0:T(8,128)(2,1)S(1)} %get-tuple-element.25), channel_id=1, source_target_pairs={{0,4},{4,8},{8,12},{12,16},{16,20},{20,24},{24,28},{28,32},{32,36}... | collective-permute-start | bytes 786440 | tf_op jit(solution)/shard_map/ppermute | solution.py:342
  161.2 8.6 %collective-permute-done.11 = bf16[128,1024]{1,0:T(8,128)(2,1)S(1)} collective-permute-done((bf16[128,1024]{1,0:T(8,128)(2,1)S(1)}, bf16[128,1024]{1,0:T(8,128)(2,1)S(1)}, u32[]{:S(2)}, u32[]{:S(2)}) %collective-permute-start.11) | collective-permute-done | bytes 262176 | tf_op jit(solution)/shard_map/ppermute | solution.py:342
  170.8 6.7 %collective-permute-done.23 = bf16[2,1,1,1,16,128]{5,4,3,2,1,0:T(8,128)(2,1)S(1)} collective-permute-done((bf16[2,1,1,1,16,128]{5,4,3,2,1,0:T(8,128)(2,1)S(1)}, bf16[2,1,1,1,16,128]{5,4,3,2,1,0:T(8,128)(2,1)S(1)}, u32[]{:S(2)}, u32[]{:S(2)}) %collective-permute-start.23) | collective-permute-done | bytes 8224 | tf_op jit(solution)/shard_map/ppermute | solution.py:276
  (115 shorter events, 22.0 us)
Async XLA Ops:
  0.6 39.8 %copy-start.3 = (bf16[1,1,2,128,1024]{4,3,2,1,0:T(8,128)(2,1)S(1)}, bf16[1,1,2,128,1024]{4,3,2,1,0:T(8,128)(2,1)}, u32[]{:S(2)}) copy-start(bf16[1,1,2,128,1024]{4,3,2,1,0:T(8,128)(2,1)} %param.4) | copy-start | bytes 1572868
  0.6 39.8 %copy-start.6 = (bf16[1,1,2,128,1024]{4,3,2,1,0:T(8,128)(2,1)S(1)}, bf16[1,1,2,128,1024]{4,3,2,1,0:T(8,128)(2,1)}, u32[]{:S(2)}) copy-start(bf16[1,1,2,128,1024]{4,3,2,1,0:T(8,128)(2,1)} %param.7) | copy-start | bytes 1572868
  1.8 15.7 %collective-permute-start.3 = (bf16[128,1024]{1,0:T(8,128)(2,1)S(1)}, bf16[128,1024]{1,0:T(8,128)(2,1)S(1)}, u32[]{:S(2)}, u32[]{:S(2)}) collective-permute-start(bf16[128,1024]{1,0:T(8,128)(2,1)S(1)} %get-tuple-element.36), channel_id=1, source_target_pairs={{4,0},{8,4},{12,8},{16,12},{20,16},{24,20},{28,24},{32,28},{36,32}... | collective-permute-start | bytes 786440 | tf_op jit(solution)/shard_map/ppermute | solution.py:330
  12.0 16.4 %collective-permute-start = (bf16[128,1024]{1,0:T(8,128)(2,1)S(1)}, bf16[128,1024]{1,0:T(8,128)(2,1)S(1)}, u32[]{:S(2)}, u32[]{:S(2)}) collective-permute-start(bf16[128,1024]{1,0:T(8,128)(2,1)S(1)} %get-tuple-element.37), channel_id=1, source_target_pairs={{0,4},{4,8},{8,12},{12,16},{16,20},{20,24},{24,28},{28,32},{32,36}... | collective-permute-start | bytes 786440 | tf_op jit(solution)/shard_map/ppermute | solution.py:329
  18.5 13.3 %collective-permute-start.4 = (bf16[128,1024]{1,0:T(8,128)(2,1)S(1)}, bf16[128,1024]{1,0:T(8,128)(2,1)S(1)}, u32[]{:S(2)}, u32[]{:S(2)}) collective-permute-start(bf16[128,1024]{1,0:T(8,128)(2,1)S(1)} %broadcast_select_fusion.4.down_ref), channel_id=1, source_target_pairs={{4,0},{8,4},{12,8},{16,12},{20,16},{24,20},{28,24},{32,28},{36,32}... | collective-permute-start | bytes 786440 | tf_op jit(solution)/shard_map/ppermute | solution.py:330
  28.3 27.3 %collective-permute-start.1 = (bf16[128,1024]{1,0:T(8,128)(2,1)S(1)}, bf16[128,1024]{1,0:T(8,128)(2,1)S(1)}, u32[]{:S(2)}, u32[]{:S(2)}) collective-permute-start(bf16[128,1024]{1,0:T(8,128)(2,1)S(1)} %collective-permute-done.up_ref), channel_id=1, source_target_pairs={{0,4},{4,8},{8,12},{12,16},{16,20},{20,24},{24,28},{28,32},{32,36}... | collective-permute-start | bytes 786440 | tf_op jit(solution)/shard_map/ppermute | solution.py:329
  31.8 28.2 %collective-permute-start.5 = (bf16[128,1024]{1,0:T(8,128)(2,1)S(1)}, bf16[128,1024]{1,0:T(8,128)(2,1)S(1)}, u32[]{:S(2)}, u32[]{:S(2)}) collective-permute-start(bf16[128,1024]{1,0:T(8,128)(2,1)S(1)} %broadcast_select_fusion.3.down_ref), channel_id=1, source_target_pairs={{4,0},{8,4},{12,8},{16,12},{20,16},{24,20},{28,24},{32,28},{36,32}... | collective-permute-start | bytes 786440 | tf_op jit(solution)/shard_map/ppermute | solution.py:330
  55.6 12.5 %collective-permute-start.2 = (bf16[128,1024]{1,0:T(8,128)(2,1)S(1)}, bf16[128,1024]{1,0:T(8,128)(2,1)S(1)}, u32[]{:S(2)}, u32[]{:S(2)}) collective-permute-start(bf16[128,1024]{1,0:T(8,128)(2,1)S(1)} %collective-permute-done.1.up_ref), channel_id=1, source_target_pairs={{0,4},{4,8},{8,12},{12,16},{16,20},{20,24},{24,28},{28,32},{32,36}... | collective-permute-start | bytes 786440 | tf_op jit(solution)/shard_map/ppermute | solution.py:329
  60.1 10.5 %copy-start.9 = (f32[2,512,128]{2,1,0:T(8,128)S(1)}, f32[2,512,128]{2,1,0:T(8,128)}, u32[]{:S(2)}) copy-start(f32[2,512,128]{2,1,0:T(8,128)} %and_select_fusion.bias_ref) | copy-start | bytes 1572868
  60.1 10.5 %copy-start.11 = (bf16[2,2,128,1024]{3,2,1,0:T(8,128)(2,1)S(1)}, bf16[2,2,128,1024]{3,2,1,0:T(8,128)(2,1)}, u32[]{:S(2)}) copy-start(bf16[2,2,128,1024]{3,2,1,0:T(8,128)(2,1)} %copy-done.10) | copy-start | bytes 3145732
  60.1 10.5 %copy-start.13 = (bf16[2,128,1024]{2,1,0:T(8,128)(2,1)S(1)}, bf16[2,128,1024]{2,1,0:T(8,128)(2,1)}, u32[]{:S(2)}) copy-start(bf16[2,128,1024]{2,1,0:T(8,128)(2,1)} %copy-done.12) | copy-start | bytes 1572868
  60.1 10.5 %copy-start.15 = (bf16[2,128,1024]{2,1,0:T(8,128)(2,1)S(1)}, bf16[2,128,1024]{2,1,0:T(8,128)(2,1)}, u32[]{:S(2)}) copy-start(bf16[2,128,1024]{2,1,0:T(8,128)(2,1)} %copy-done.14) | copy-start | bytes 1572868
  70.5 22.2 %slice-start = ((s8[8388608]{0:T(1024)(128)(4,1)}), s8[4194304]{0:T(1024)(128)(4,1)S(1)}, s32[]{:S(2)}) async-start(s8[8388608]{0:T(1024)(128)(4,1)} %bitcast.83), calls=%async_computation | async-start | bytes 8388608
  70.6 22.2 %slice-start.1 = ((s8[8388608]{0:T(1024)(128)(4,1)}), s8[4194304]{0:T(1024)(128)(4,1)S(1)}, s32[]{:S(2)}) async-start(s8[8388608]{0:T(1024)(128)(4,1)} %bitcast.83), calls=%async_computation.1 | async-start | bytes 8388608
  92.7 38.3 %collective-permute-start.12 = (bf16[2,2,1024,128]{3,2,1,0:T(8,128)(2,1)}, bf16[2,2,1024,128]{3,2,1,0:T(8,128)(2,1)}, u32[]{:S(2)}, u32[]{:S(2)}) collective-permute-start(bf16[2,2,1024,128]{3,2,1,0:T(8,128)(2,1)} %get-tuple-element.23), channel_id=1, source_target_pairs={{0,1},{1,0},{2,3},{3,2},{4,5},{5,4},{6,7},{7,6},{8,9},{9,8},{10,11... | collective-permute-start | bytes 3145736 | tf_op jit(solution)/shard_map/ppermute | solution.py:282
  94.8 10.6 %collective-permute-start.6 = (bf16[128,1024]{1,0:T(8,128)(2,1)S(1)}, bf16[128,1024]{1,0:T(8,128)(2,1)S(1)}, u32[]{:S(2)}, u32[]{:S(2)}) collective-permute-start(bf16[128,1024]{1,0:T(8,128)(2,1)S(1)} %get-tuple-element.35), channel_id=1, source_target_pairs={{4,0},{8,4},{12,8},{16,12},{20,16},{24,20},{28,24},{32,28},{36,32}... | collective-permute-start | bytes 786440 | tf_op jit(solution)/shard_map/ppermute | solution.py:341
  96.8 24.0 %collective-permute-start.8 = (bf16[128,1024]{1,0:T(8,128)(2,1)S(1)}, bf16[128,1024]{1,0:T(8,128)(2,1)S(1)}, u32[]{:S(2)}, u32[]{:S(2)}) collective-permute-start(bf16[128,1024]{1,0:T(8,128)(2,1)S(1)} %get-tuple-element.34), channel_id=1, source_target_pairs={{0,4},{4,8},{8,12},{12,16},{16,20},{20,24},{24,28},{28,32},{32,36}... | collective-permute-start | bytes 786440 | tf_op jit(solution)/shard_map/ppermute | solution.py:342
  106.2 14.5 %collective-permute-start.7 = (bf16[128,1024]{1,0:T(8,128)(2,1)}, bf16[128,1024]{1,0:T(8,128)(2,1)S(1)}, u32[]{:S(2)}, u32[]{:S(2)}) collective-permute-start(bf16[128,1024]{1,0:T(8,128)(2,1)} %fusion.8), channel_id=1, source_target_pairs={{4,0},{8,4},{12,8},{16,12},{20,16},{24,20},{28,24},{32,28},{36,32}... | collective-permute-start | bytes 786440 | tf_op jit(solution)/shard_map/ppermute | solution.py:341
  121.0 35.9 %collective-permute-start.10 = (bf16[128,1024]{1,0:T(8,128)(2,1)S(1)}, bf16[128,1024]{1,0:T(8,128)(2,1)S(1)}, u32[]{:S(2)}, u32[]{:S(2)}) collective-permute-start(bf16[128,1024]{1,0:T(8,128)(2,1)S(1)} %get-tuple-element.27), channel_id=1, source_target_pairs={{0,4},{4,8},{8,12},{12,16},{16,20},{20,24},{24,28},{28,32},{32,36}... | collective-permute-start | bytes 786440 | tf_op jit(solution)/shard_map/ppermute | solution.py:342
  122.9 34.0 %collective-permute-start.9 = (bf16[128,1024]{1,0:T(8,128)(2,1)S(1)}, bf16[128,1024]{1,0:T(8,128)(2,1)S(1)}, u32[]{:S(2)}, u32[]{:S(2)}) collective-permute-start(bf16[128,1024]{1,0:T(8,128)(2,1)S(1)} %get-tuple-element.26), channel_id=1, source_target_pairs={{4,0},{8,4},{12,8},{16,12},{20,16},{24,20},{28,24},{32,28},{36,32}... | collective-permute-start | bytes 786440 | tf_op jit(solution)/shard_map/ppermute | solution.py:341
  132.9 7.4 %collective-permute-start.13 = (bf16[4,2,8,16,128]{4,3,2,0,1:T(8,128)(2,1)S(1)}, bf16[4,2,8,16,128]{4,3,2,0,1:T(8,128)(2,1)S(1)}, u32[]{:S(2)}, u32[]{:S(2)}) collective-permute-start(bf16[4,2,8,16,128]{4,3,2,0,1:T(8,128)(2,1)S(1)} %broadcast_select_fusion.1), channel_id=1, source_target_pairs={{0,32},{1,33},{4,36},{5,37},{8,40},{9,41},{12,44},{13,45},{16,48},... | collective-permute-start | bytes 786440 | tf_op jit(solution)/shard_map/ppermute | solution.py:269
  133.1 7.5 %collective-permute-start.17 = (bf16[2,4,8,16,128]{4,3,2,0,1:T(8,128)(2,1)S(1)}, bf16[2,4,8,16,128]{4,3,2,0,1:T(8,128)(2,1)S(1)}, u32[]{:S(2)}, u32[]{:S(2)}) collective-permute-start(bf16[2,4,8,16,128]{4,3,2,0,1:T(8,128)(2,1)S(1)} %broadcast_select_fusion), channel_id=1, source_target_pairs={{0,128},{1,129},{4,132},{5,133},{8,136},{9,137},{12,140},{13,141},... | collective-permute-start | bytes 786440 | tf_op jit(solution)/shard_map/ppermute | solution.py:269
  140.4 6.3 %collective-permute-start.14 = (bf16[4,1,8,16,128]{4,3,2,0,1:T(8,128)(2,1)S(1)}, bf16[4,1,8,16,128]{4,3,2,0,1:T(8,128)(2,1)S(1)}, u32[]{:S(2)}, u32[]{:S(2)}) collective-permute-start(bf16[4,1,8,16,128]{4,3,2,0,1:T(8,128)(2,1)S(1)} %broadcast_select_fusion.6), channel_id=1, source_target_pairs={{0,96},{1,97},{4,100},{5,101},{8,104},{9,105},{12,108},{13,109},{1... | collective-permute-start | bytes 393224 | tf_op jit(solution)/shard_map/ppermute | solution.py:276
  140.7 6.3 %collective-permute-start.18 = (bf16[1,4,8,16,128]{4,3,2,0,1:T(8,128)(2,1)S(1)}, bf16[1,4,8,16,128]{4,3,2,0,1:T(8,128)(2,1)S(1)}, u32[]{:S(2)}, u32[]{:S(2)}) collective-permute-start(bf16[1,4,8,16,128]{4,3,2,0,1:T(8,128)(2,1)S(1)} %broadcast_select_fusion.5), channel_id=1, source_target_pairs={{0,130},{1,131},{4,134},{5,135},{8,138},{9,139},{12,142},{13,143},... | collective-permute-start | bytes 393224 | tf_op jit(solution)/shard_map/ppermute | solution.py:276
  146.8 4.5 %collective-permute-start.15 = (bf16[2,1,8,16,128]{4,3,2,0,1:T(8,128)(2,1)S(1)}, bf16[2,1,8,16,128]{4,3,2,0,1:T(8,128)(2,1)S(1)}, u32[]{:S(2)}, u32[]{:S(2)}) collective-permute-start(bf16[2,1,8,16,128]{4,3,2,0,1:T(8,128)(2,1)S(1)} %broadcast_select_fusion.8), channel_id=1, source_target_pairs={{0,128},{1,129},{4,132},{5,133},{8,136},{9,137},{12,140},{13,141},... | collective-permute-start | bytes 196616 | tf_op jit(solution)/shard_map/ppermute | solution.py:269
  147.1 4.4 %collective-permute-start.19 = (bf16[1,2,8,16,128]{4,3,2,0,1:T(8,128)(2,1)S(1)}, bf16[1,2,8,16,128]{4,3,2,0,1:T(8,128)(2,1)S(1)}, u32[]{:S(2)}, u32[]{:S(2)}) collective-permute-start(bf16[1,2,8,16,128]{4,3,2,0,1:T(8,128)(2,1)S(1)} %broadcast_select_fusion.7), channel_id=1, source_target_pairs={{0,32},{1,33},{4,36},{5,37},{8,40},{9,41},{12,44},{13,45},{16,48},... | collective-permute-start | bytes 196616 | tf_op jit(solution)/shard_map/ppermute | solution.py:269
  151.3 5.2 %collective-permute-start.16 = (bf16[1,1,8,16,128]{4,3,2,0,1:T(8,128)(2,1)S(1)}, bf16[1,1,8,16,128]{4,3,2,0,1:T(8,128)(2,1)S(1)}, u32[]{:S(2)}, u32[]{:S(2)}) collective-permute-start(bf16[1,1,8,16,128]{4,3,2,0,1:T(8,128)(2,1)S(1)} %broadcast_select_fusion.10), channel_id=1, source_target_pairs={{0,130},{1,131},{4,134},{5,135},{8,138},{9,139},{12,142},{13,143},... | collective-permute-start | bytes 98312 | tf_op jit(solution)/shard_map/ppermute | solution.py:276
  151.5 5.2 %collective-permute-start.20 = (bf16[1,1,8,16,128]{4,3,2,0,1:T(8,128)(2,1)S(1)}, bf16[1,1,8,16,128]{4,3,2,0,1:T(8,128)(2,1)S(1)}, u32[]{:S(2)}, u32[]{:S(2)}) collective-permute-start(bf16[1,1,8,16,128]{4,3,2,0,1:T(8,128)(2,1)S(1)} %broadcast_select_fusion.9), channel_id=1, source_target_pairs={{0,96},{1,97},{4,100},{5,101},{8,104},{9,105},{12,108},{13,109},{1... | collective-permute-start | bytes 98312 | tf_op jit(solution)/shard_map/ppermute | solution.py:276
  156.8 4.2 %collective-permute-start.21 = (bf16[2,2,2,1,16,128]{5,4,3,2,1,0:T(8,128)(2,1)S(1)}, bf16[2,2,2,1,16,128]{5,4,3,2,1,0:T(8,128)(2,1)S(1)}, u32[]{:S(2)}, u32[]{:S(2)}) collective-permute-start(bf16[2,2,2,1,16,128]{5,4,3,2,1,0:T(8,128)(2,1)S(1)} %broadcast_select_fusion.11), channel_id=1, source_target_pairs={{0,4},{1,5},{4,0},{5,1},{8,12},{9,13},{12,8},{13,9},{16,20},{17,21... | collective-permute-start | bytes 98312 | tf_op jit(solution)/shard_map/ppermute | solution.py:276
  157.1 12.7 %collective-permute-start.11 = (bf16[128,1024]{1,0:T(8,128)(2,1)S(1)}, bf16[128,1024]{1,0:T(8,128)(2,1)S(1)}, u32[]{:S(2)}, u32[]{:S(2)}) collective-permute-start(bf16[128,1024]{1,0:T(8,128)(2,1)S(1)} %get-tuple-element.25), channel_id=1, source_target_pairs={{0,4},{4,8},{8,12},{12,16},{16,20},{20,24},{24,28},{28,32},{32,36}... | collective-permute-start | bytes 786440 | tf_op jit(solution)/shard_map/ppermute | solution.py:342
  161.1 8.8 %collective-permute-start.22 = (bf16[2,2,1,1,16,128]{5,4,3,2,1,0:T(8,128)(2,1)S(1)}, bf16[2,2,1,1,16,128]{5,4,3,2,1,0:T(8,128)(2,1)S(1)}, u32[]{:S(2)}, u32[]{:S(2)}) collective-permute-start(bf16[2,2,1,1,16,128]{5,4,3,2,1,0:T(8,128)(2,1)S(1)} %broadcast_select_fusion.12), channel_id=1, source_target_pairs={{0,8},{1,9},{4,12},{5,13},{8,0},{9,1},{12,4},{13,5},{16,24},{17,25... | collective-permute-start | bytes 49160 | tf_op jit(solution)/shard_map/ppermute | solution.py:276
  169.9 7.6 %collective-permute-start.23 = (bf16[2,1,1,1,16,128]{5,4,3,2,1,0:T(8,128)(2,1)S(1)}, bf16[2,1,1,1,16,128]{5,4,3,2,1,0:T(8,128)(2,1)S(1)}, u32[]{:S(2)}, u32[]{:S(2)}) collective-permute-start(bf16[2,1,1,1,16,128]{5,4,3,2,1,0:T(8,128)(2,1)S(1)} %broadcast_select_fusion.13), channel_id=1, source_target_pairs={{0,16},{1,17},{4,20},{5,21},{8,24},{9,25},{12,28},{13,29},{16,0},{... | collective-permute-start | bytes 24584 | tf_op jit(solution)/shard_map/ppermute | solution.py:276
  (10 other events, 30.1 us)

commit v2 on v1

--- a/solution.py
+++ b/solution.py
@@ -12,6 +12,7 @@
 BLOCK = 128
 D = 1024
 PAIR = 2 * HEAD_DIM
+PAIRS_A_STEP = 4
 TILE = 256
 BF = jnp.bfloat16
 F32 = jnp.float32
@@ -103,61 +104,68 @@
     q_ref, da_ref, kv3_ref, kv2_ref, kv1_ref, kv0_ref, bias_ref,
     out_ref, dq_ref, d3_ref, d2_ref, d1_ref, d0_ref,
 ):
-    lane = lax.broadcasted_iota(jnp.int32, (BLOCK, PAIR), 1)
-    first = lane < HEAD_DIM
+    first = lax.broadcasted_iota(jnp.int32, (BLOCK, PAIR), 1) < HEAD_DIM
+    kv_refs = (kv3_ref, kv2_ref, kv1_ref, kv0_ref)
+    d_refs = (d3_ref, d2_ref, d1_ref, d0_ref)
+    lanes = [slice(i * PAIR, (i + 1) * PAIR) for i in range(PAIRS_A_STEP)]
 
     def split(rows):
         zero = jnp.zeros_like(rows)
         return jnp.concatenate([jnp.where(first, rows, zero), jnp.where(first, zero, rows)], axis=0)
 
-    def own_heads(square):
-        return jnp.concatenate([square[:HEAD_DIM, :BLOCK], square[HEAD_DIM:, BLOCK:]], axis=0)
-
-    kv_refs = (kv3_ref, kv2_ref, kv1_ref, kv0_ref)
-    keys = jnp.concatenate([ref[0, 0] for ref in kv_refs], axis=0)
-    values = jnp.concatenate([ref[1, 0] for ref in kv_refs], axis=0)
-    d_attn = da_ref[0]
-    q_split = split(q_ref[0])
-    da_split = split(d_attn)
-    bias = bias_ref[0]
-    scores = jnp.minimum(mm(keys, q_split, NT), jnp.concatenate([bias, bias], axis=1))
-    top = jnp.max(scores, axis=0, keepdims=True)
-    terms = jnp.exp2((scores - top) * EXP2_SCALE)
-    probs = terms * (1.0 / jnp.sum(terms, axis=0, keepdims=True))
-    probs_low = probs.astype(BF)
-    out_t = own_heads(mm(values.T, probs_low)).astype(BF)
-    out_ref[0] = out_t.T
-    weighted = d_attn.T.astype(F32) * out_t.astype(F32)
-    delta = jnp.concatenate(
-        [
-            jnp.sum(weighted[:HEAD_DIM], axis=0, keepdims=True),
-            jnp.sum(weighted[HEAD_DIM:], axis=0, keepdims=True),
-        ],
-        axis=1,
-    )
-    dscore = (probs * (mm(values, da_split, NT) - delta)).astype(BF)
-    dq_ref[0] = (own_heads(mm(keys.T, dscore)) * SCALE).astype(BF).T
-    d_keys = (mm(dscore, q_split) * SCALE).astype(BF)
-    d_values = mm(probs_low, da_split).astype(BF)
-    for place, ref in enumerate((d3_ref, d2_ref, d1_ref, d0_ref)):
-        ref[0, 0] = d_keys[place * BLOCK : (place + 1) * BLOCK]
-        ref[1, 0] = d_values[place * BLOCK : (place + 1) * BLOCK]
+    def merge(rows):
+        return jnp.where(first, rows[:BLOCK], rows[BLOCK:])
+
+    def twice(rows):
+        return jnp.concatenate([rows, rows], axis=0)
+
+    bias = twice(bias_ref[0])
+    ones = jnp.ones((WIN * BLOCK, PAIR), BF)
+    keys = [jnp.concatenate([ref[0, 0, :, c] for ref in kv_refs], axis=0) for c in lanes]
+    values = [jnp.concatenate([ref[1, 0, :, c] for ref in kv_refs], axis=0) for c in lanes]
+    queries = [split(q_ref[0, :, c]) for c in lanes]
+    d_attn = [split(da_ref[0, :, c]) for c in lanes]
+    scores = [jnp.minimum(mm(q, k, NT), bias) for q, k in zip(queries, keys)]
+    tops = [jnp.max(s, axis=1, keepdims=True) for s in scores]
+    terms = [jnp.exp2((s - t) * EXP2_SCALE).astype(BF) for s, t in zip(scores, tops)]
+    sums = [mm(t, jnp.concatenate([v, ones], axis=1)) for t, v in zip(terms, values)]
+    shares = [1.0 / s[:, PAIR:] for s in sums]
+    outs = [merge(s[:, :PAIR] * r).astype(BF) for s, r in zip(sums, shares)]
+    for c, o in zip(lanes, outs):
+        out_ref[0, :, c] = o
+    scaled = [d.astype(F32) * r for d, r in zip(d_attn, shares)]
+    deltas = [
+        jnp.sum(d * twice(o.astype(F32)), axis=1, keepdims=True) for d, o in zip(scaled, outs)
+    ]
+    scaled = [d.astype(BF) for d in scaled]
+    d_probs = [mm(d, v, NT) for d, v in zip(scaled, values)]
+    d_scores = [(p - d).astype(BF) * t for p, d, t in zip(d_probs, deltas, terms)]
+    d_values = [mm(d.T, t).astype(BF).T for d, t in zip(scaled, terms)]
+    d_queries = [merge(mm(d, k)) for d, k in zip(d_scores, keys)]
+    for c, d in zip(lanes, d_queries):
+        dq_ref[0, :, c] = (d * SCALE).astype(BF)
+    d_keys = [(mm(q.T, d) * SCALE).astype(BF).T for q, d in zip(queries, d_scores)]
+    for c, dk, dv in zip(lanes, d_keys, d_values):
+        for i, ref in enumerate(d_refs):
+            ref[0, 0, :, c] = dk[i * BLOCK : (i + 1) * BLOCK]
+            ref[1, 0, :, c] = dv[i * BLOCK : (i + 1) * BLOCK]
 
 
 def attention(q, da, kvs, bias):
     rows = jax.ShapeDtypeStruct((2, BLOCK, D), BF)
     pairs = jax.ShapeDtypeStruct((2, 2, BLOCK, D), BF)
-    row_spec = pl.BlockSpec((1, BLOCK, PAIR), lambda h, p: (h, 0, p))
-    pair_spec = pl.BlockSpec((2, 1, BLOCK, PAIR), lambda h, p: (0, h, 0, p))
-    bias_spec = pl.BlockSpec((1, WIN * BLOCK, BLOCK), lambda h, p: (h, 0, 0))
+    width = PAIRS_A_STEP * PAIR
+    row_spec = pl.BlockSpec((1, BLOCK, width), lambda h, p: (h, 0, p))
+    pair_spec = pl.BlockSpec((2, 1, BLOCK, width), lambda h, p: (0, h, 0, p))
+    bias_spec = pl.BlockSpec((1, BLOCK, WIN * BLOCK), lambda h, p: (h, 0, 0))
     return pl.pallas_call(
         attention_kernel,
-        grid=(2, HEADS // 2),
+        grid=(2, D // width),
         in_specs=[row_spec, row_spec] + [pair_spec] * 4 + [bias_spec],
         out_specs=[row_spec, row_spec] + [pair_spec] * 4,
         out_shape=[rows, rows] + [pairs] * 4,
         compiler_params=params(32),
-        cost_estimate=cost(2 * 10 * BLOCK * WIN * BLOCK * D * 4, 12 * 2**20, 2**21),
+        cost_estimate=cost(2 * 10 * BLOCK * WIN * BLOCK * D * 2, 12 * 2**20, 2**21),
         name="attention",
     )(q, da, *kvs, bias)
 
@@ -210,14 +218,12 @@
 def outer_kernel(core_ref, o_ref, keep_ref, send_ref, kept_ref, sent_ref):
     o_t = o_ref[...].reshape(2 * BLOCK, D).T
     for g_ref, r_ref in ((send_ref, sent_ref), (keep_ref, kept_ref)):
-        product = mm(o_t, g_ref[...].reshape(2 * BLOCK, TILE)).astype(BF)
-        r_ref[0, 0] = product[:, :BLOCK]
-        r_ref[0, 1] = product[:, BLOCK:]
+        r_ref[0] = mm(o_t, g_ref[...].reshape(2 * BLOCK, TILE)).astype(BF)
 
 
 def outer_products(o, g, core):
-    result = jax.ShapeDtypeStruct((2, 2, D, BLOCK), BF)
-    result_spec = pl.BlockSpec((1, 2, D, BLOCK), lambda y, c: (y, 0, 0, 0))
+    result = jax.ShapeDtypeStruct((2, D, TILE), BF)
+    result_spec = pl.BlockSpec((1, D, TILE), lambda y, c: (y, 0, 0))
     return pl.pallas_call(
         outer_kernel,
         grid_spec=pltpu.PrefetchScalarGridSpec(
@@ -237,64 +243,28 @@
     )(core.reshape(1), o, g, g)
 
 
-def chip_pairs(move):
-    pairs = []
-    for y in range(4):
-        for x in range(4):
-            for z in range(8):
-                y2, x2, z2 = move(y, x, z)
-                for core in range(2):
-                    pairs.append((place(y, x, z, core), place(y2, x2, z2, core)))
-    return pairs
-
-
 def place(y, x, z, core):
     return ((y % 2) * 32 + x * 8 + z) * 4 + (y // 2) * 2 + core
 
 
-FLIP = ((1, 0, 3, 2), (3, 2, 1, 0))
+CORE_PAIRS = [(i, i ^ 1) for i in range(4)]
+PLANES = [
+    [place(y, x, z, core) for y in range(4) for x in range(4)] for z in range(8) for core in range(2)
+]
+LINES = [[32 * y + 8 * x + z for z in range(8)] for y in range(2) for x in range(4)]
 
 
 def add(a, b):
     return (a.astype(F32) + b.astype(F32)).astype(BF)
 
 
-def ring_first(v, dim, index, pairs):
-    def pick(i):
-        return lax.slice_in_dim(v, i, i + 1, axis=dim)
-
-    outer = jnp.concatenate([pick(0), pick(3)], axis=dim)
-    inner = lax.slice_in_dim(v, 1, 3, axis=dim)
-    mine = (index == 0) | (index == 3)
-    moved = lax.ppermute(jnp.where(mine, inner, outer), ("blk", "dp"), pairs)
-    return add(jnp.where(mine, outer, inner), moved)
-
-
-def halve(v, dim, bit, pairs):
-    low = lax.slice_in_dim(v, 0, 1, axis=dim)
-    high = lax.slice_in_dim(v, 1, 2, axis=dim)
-    moved = lax.ppermute(jnp.where(bit == 0, high, low), ("blk", "dp"), pairs)
-    return add(jnp.where(bit == 0, low, high), moved)
-
-
-def reduce_outer(kept, sent, y, x, z):
-    core_pairs = [(i, i ^ 1) for i in range(4)]
-    total = add(kept, lax.ppermute(sent, "dp", core_pairs))
-    total = total.reshape(2, 2, 2, 4, 8, 16, BLOCK)
-    parts = [total[:, i].reshape(4, 4, 8, 16, BLOCK) for i in range(2)]
-    rings = (
-        (0, y, [chip_pairs(lambda a, b, c, f=f: (f[a], b, c)) for f in FLIP]),
-        (1, x, [chip_pairs(lambda a, b, c, f=f: (a, f[b], c)) for f in FLIP]),
-    )
-    for turn in range(2):
-        dim_of = [rings[(i + turn + 1) % 2] for i in range(2)]
-        parts = [ring_first(v, d, i, m[0]) for v, (d, i, m) in zip(parts, dim_of)]
-        parts = [halve(v, d, i // 2, m[1]) for v, (d, i, m) in zip(parts, dim_of)]
-    v = jnp.concatenate(parts, axis=0).reshape(2, 2, 2, 2, 16, BLOCK)
-    for k, dim in ((1, 3), (2, 2), (4, 1)):
-        v = halve(v, dim, (z // k) % 2, chip_pairs(lambda a, b, c, k=k: (a, b, c ^ k)))
-    v = v.reshape(2, 16, BLOCK)
-    return jnp.concatenate([v[0], v[1]], axis=1).astype(F32)
+def reduce_outer(kept, sent):
+    total = add(kept, lax.ppermute(sent, "dp", CORE_PAIRS))
+    total = total.reshape(16, 8 * 16, TILE)
+    total = lax.all_to_all(total, ("blk", "dp"), 0, 0, axis_index_groups=PLANES)
+    total = jnp.sum(total.astype(F32), axis=0).astype(BF).reshape(8, 16, TILE)
+    total = lax.all_to_all(total, "blk", 0, 0, axis_index_groups=LINES)
+    return jnp.sum(total.astype(F32), axis=0)
 
 
 def score_limits(key_valid, position):
@@ -305,10 +275,10 @@
     valid = jnp.stack(
         [lax.dynamic_slice_in_dim(seq_valid, both[i], WIN, 0).reshape(WIN * BLOCK) for i in range(2)]
     )
-    q_pos = jnp.arange(BLOCK, dtype=jnp.int32)[None, None, :]
-    k_pos = (jnp.arange(WIN * BLOCK, dtype=jnp.int32) - (WIN - 1) * BLOCK)[None, :, None]
+    q_pos = jnp.arange(BLOCK, dtype=jnp.int32)[None, :, None]
+    k_pos = (jnp.arange(WIN * BLOCK, dtype=jnp.int32) - (WIN - 1) * BLOCK)[None, None, :]
     inside = k_pos + both[:, None, None] * BLOCK >= 0
-    allowed = inside & (k_pos <= q_pos) & ((valid[:, :, None] == 1) | (k_pos == q_pos))
+    allowed = inside & (k_pos <= q_pos) & ((valid[:, None, :] == 1) | (k_pos == q_pos))
     return jnp.where(allowed, FREE, BARRED).astype(F32)
 
 
@@ -328,12 +298,13 @@
     for _ in range(WIN - 1):
         new_up = lax.ppermute(state_up, "blk", up)
         new_down = jnp.where(at_last, state_up, lax.ppermute(state_down, "blk", down))
+        new_up, new_down, kvs[-1] = lax.optimization_barrier((new_up, new_down, kvs[-1]))
         kvs.append(halo_projections(new_up, new_down, weights))
         state_up, state_down = new_up, new_down
     o, dq, d3, d2, d1, d0 = attention(q, da, kvs[::-1], bias)
 
     kept, sent = outer_products(o, g, shot % 2)
-    w_grad = reduce_outer(kept, sent, (shot // 2) * 2 + position // 32, (position // 8) % 4, position % 8)
+    w_grad = reduce_outer(kept, sent)
 
     returned = back_projections(d3, weights, BF)
     terms = [back_projections(d2, weights, BF), back_projections(d1, weights, BF), last_projections(d0, dq, weights)]

time: 180 us -> 156 us (0.87)
  the two profiles are of different devices: /device:TPU:24 before, /device:TPU:1 now
where the time goes in v2:
time: 156 us; the launch traced here: 155 us
  starting transfers between devices  67.7 us (43%)
  waiting for transfers between devices  34.9 us (22%)
  Pallas kernels  29.5 us (19%)
  local copies, waits for them, and re-layouts  15.1 us (10%)
  other arithmetic  6.3 us (4%)
    all_to_all x1, starting transfers between devices, reduce_outer(): total = lax.all_to_all(total, ('blk', 'dp'), 0, 0, axis_index_groups=PLANES)  27.1 us
    all_to_all x1, waiting for transfers between devices, reduce_outer(): total = lax.all_to_all(total, ('blk', 'dp'), 0, 0, axis_index_groups=PLANES)  14.3 us
    ppermute x3, starting transfers between devices, per_device(): new_up = lax.ppermute(state_up, 'blk', up)  13.3 us
    unnamed x26, local copies, waits for them, and re-layouts  13 us
    ppermute x3, starting transfers between devices, per_device(): from_before = lax.ppermute(returned[1], 'blk', up)  11.9 us
    ppermute x3, waiting for transfers between devices, per_device(): from_after = lax.ppermute(returned[0], 'blk', down)  9.74 us
    pallas_call x1, Pallas kernels, attention(): pl.pallas_call(attention_kernel, grid=(2, D // width), in_specs=[row_spec...  8.55 us
    pallas_call x3, Pallas kernels, halo_projections(): pl.pallas_call(halo_kernel, grid=(D // TILE,), in_specs=[whole((BLOCK, D)...  7.29 us
  transfers between devices with their start and end apart: 15, of which 6 were waited for; matrix products, arithmetic and copies ran while one was open for 4% of the time, Pallas kernels for 10%

profile of v2, /device:TPU:1, one launch (start us, length us, event | category | flops | bytes accessed | tf_op | source)
XLA Modules:
  0.0 154.6 jit_solution(3258031376436690029)
XLA Ops:
  1.7 1.3 collective-permute-start.1
  3.0 5.0 %collective-permute-start = (bf16[128,1024]{1,0:T(8,128)(2,1)S(1)}, bf16[128,1024]{1,0:T(8,128)(2,1)S(1)}, u32[]{:S(2)}, u32[]{:S(2)}) collective-permute-start(bf16[128,1024]{1,0:T(8,128)(2,1)S(1)} %get-tuple-element.49), channel_id=1, source_target_pairs={{0,4},{4,8},{8,12},{12,16},{16,20},{20,24},{24,28},{28,32},{32,36}... | collective-permute-start | bytes 786440 | tf_op jit(solution)/shard_map/ppermute | solution.py:299
  9.2 3.4 %copy-done = bf16[4096,1024]{1,0:T(8,128)(2,1)S(1)} copy-done((bf16[4096,1024]{1,0:T(8,128)(2,1)S(1)}, bf16[4096,1024]{1,0:T(8,128)(2,1)}, u32[]{:S(2)}) %copy-start) | copy-done | bytes 8388632
  14.7 4.0 %own_projections.1 = (bf16[2,128,1024]{2,1,0:T(8,128)(2,1)S(1)}, bf16[2,128,1024]{2,1,0:T(8,128)(2,1)S(1)}, bf16[2,2,128,1024]{3,2,1,0:T(8,128)(2,1)S(1)}) custom-call(bf16[2,128,1024]{2,1,0:T(8,128)(2,1)S(1)} %bitcast.71, bf16[2,128,1024]{2,1,0:T(8,128)(2,1)S(1)} %bitcast.72, bf16[4096,1024]{1,0:T(8,128)(2,1)S(1)} %copy-done, ...), custom_call_target="tpu_custom_call" | custom-call | flops 2147483648 | bytes 9961472 | tf_op jit(solution)/shard_map/own_projections/pallas_call | solution.py:65
  19.6 1.3 collective-permute-start.3
  21.0 4.2 %collective-permute-start.2 = (bf16[128,1024]{1,0:T(8,128)(2,1)S(1)}, bf16[128,1024]{1,0:T(8,128)(2,1)S(1)}, u32[]{:S(2)}, u32[]{:S(2)}) collective-permute-start(bf16[128,1024]{1,0:T(8,128)(2,1)S(1)} %collective-permute-done.up_ref), channel_id=1, source_target_pairs={{0,4},{4,8},{8,12},{12,16},{16,20},{20,24},{24,28},{28,32},{32,36}... | collective-permute-start | bytes 786440 | tf_op jit(solution)/shard_map/ppermute | solution.py:299
  25.2 3.4 %copy-done.1 = bf16[4096,1024]{1,0:T(8,128)(2,1)S(1)} copy-done((bf16[4096,1024]{1,0:T(8,128)(2,1)S(1)}, bf16[4096,1024]{1,0:T(8,128)(2,1)}, u32[]{:S(2)}) %copy-start.1) | copy-done | bytes 8388632
  28.6 2.4 %halo_projections.3.kv1_ref = bf16[2,2,128,1024]{3,2,1,0:T(8,128)(2,1)S(1)} custom-call(bf16[128,1024]{1,0:T(8,128)(2,1)S(1)} %collective-permute-done.up_ref, bf16[128,1024]{1,0:T(8,128)(2,1)S(1)} %broadcast_select_fusion.2.down_ref, bf16[4096,1024]{1,0:T(8,128)(2,1)S(1)} %copy-done.1, bf16[4096,1024]{1,0:T(8,128)(2,1)S(1)} %copy-done.1), custom_call_target="tpu_custom_call" | custom-call | flops 1073741824 | bytes 5767168 | tf_op jit(solution)/shard_map/halo_projections/pallas_call | solution.py:91
  31.1 1.3 collective-permute-start.5
  32.5 4.2 %collective-permute-start.4 = (bf16[128,1024]{1,0:T(8,128)(2,1)S(1)}, bf16[128,1024]{1,0:T(8,128)(2,1)S(1)}, u32[]{:S(2)}, u32[]{:S(2)}) collective-permute-start(bf16[128,1024]{1,0:T(8,128)(2,1)S(1)} %collective-permute-done.2.up_ref), channel_id=1, source_target_pairs={{0,4},{4,8},{8,12},{12,16},{16,20},{20,24},{24,28},{28,32},{32,36}... | collective-permute-start | bytes 786440 | tf_op jit(solution)/shard_map/ppermute | solution.py:299
  36.7 2.4 %halo_projections.4.kv2_ref = bf16[2,2,128,1024]{3,2,1,0:T(8,128)(2,1)S(1)} custom-call(bf16[128,1024]{1,0:T(8,128)(2,1)S(1)} %collective-permute-done.2.up_ref, bf16[128,1024]{1,0:T(8,128)(2,1)S(1)} %broadcast_select_fusion.1.down_ref, bf16[4096,1024]{1,0:T(8,128)(2,1)S(1)} %copy-done.1, bf16[4096,1024]{1,0:T(8,128)(2,1)S(1)} %copy-done.1), custom_call_target="tpu_custom_call" | custom-call | flops 1073741824 | bytes 5767168 | tf_op jit(solution)/shard_map/halo_projections/pallas_call | solution.py:91
  39.9 2.4 %halo_projections.5.kv3_ref = bf16[2,2,128,1024]{3,2,1,0:T(8,128)(2,1)S(1)} custom-call(bf16[128,1024]{1,0:T(8,128)(2,1)S(1)} %collective-permute-done.4.up_ref, bf16[128,1024]{1,0:T(8,128)(2,1)S(1)} %broadcast_select_fusion.down_ref, bf16[4096,1024]{1,0:T(8,128)(2,1)S(1)} %copy-done.1, bf16[4096,1024]{1,0:T(8,128)(2,1)S(1)} %copy-done.1), custom_call_target="tpu_custom_call" | custom-call | flops 1073741824 | bytes 5767168 | tf_op jit(solution)/shard_map/halo_projections/pallas_call | solution.py:91
  42.4 8.6 %attention.1 = (bf16[2,128,1024]{2,1,0:T(8,128)(2,1)S(1)}, bf16[2,128,1024]{2,1,0:T(8,128)(2,1)S(1)}, bf16[2,2,128,1024]{3,2,1,0:T(8,128)(2,1)S(1)}, bf16[2,2,12...) custom-call(bf16[2,128,1024]{2,1,0:T(8,128)(2,1)S(1)} %copy-done.8, ...), custom_call_target="tpu_custom_call" | custom-call | flops 2684354560 | bytes 12582912 | tf_op jit(solution)/shard_map/attention/pallas_call | solution.py:161
  51.0 2.0 %back_projections.5 = bf16[2,128,1024]{2,1,0:T(8,128)(2,1)S(1)} custom-call(bf16[2,2,128,1024]{3,2,1,0:T(8,128)(2,1)S(1)} %get-tuple-element.38.d_ref, bf16[4096,1024]{1,0:T(8,128)(2,1)S(1)} %bitcast.70, bf16[4096,1024]{1,0:T(8,128)(2,1)S(1)} %bitcast.70), custom_call_target="tpu_custom_call" | custom-call | flops 1073741824 | bytes 5767168 | tf_op jit(solution)/shard_map/back_projections/pallas_call | solution.py:180
  54.1 4.2 %collective-permute-start.12 = (bf16[2,1024,256]{2,1,0:T(8,128)(2,1)S(1)}, bf16[2,1024,256]{2,1,0:T(8,128)(2,1)S(1)}, u32[]{:S(2)}, u32[]{:S(2)}) collective-permute-start(bf16[2,1024,256]{2,1,0:T(8,128)(2,1)S(1)} %get-tuple-element.41), channel_id=1, source_target_pairs={{0,1},{1,0},{2,3},{3,2},{4,5},{5,4},{6,7},{7,6},{8,9},{9,8},{10,11... | collective-permute-start | bytes 3145736 | tf_op jit(solution)/shard_map/ppermute | solution.py:262
  58.4 1.3 collective-permute-start.6
  59.7 4.7 %collective-permute-start.8 = (bf16[128,1024]{1,0:T(8,128)(2,1)S(1)}, bf16[128,1024]{1,0:T(8,128)(2,1)S(1)}, u32[]{:S(2)}, u32[]{:S(2)}) collective-permute-start(bf16[128,1024]{1,0:T(8,128)(2,1)S(1)} %get-tuple-element.46), channel_id=1, source_target_pairs={{0,4},{4,8},{8,12},{12,16},{16,20},{20,24},{24,28},{28,32},{32,36}... | collective-permute-start | bytes 786440 | tf_op jit(solution)/shard_map/ppermute | solution.py:313
  64.5 2.0 %back_projections.4 = bf16[2,128,1024]{2,1,0:T(8,128)(2,1)S(1)} custom-call(bf16[2,2,128,1024]{3,2,1,0:T(8,128)(2,1)S(1)} %get-tuple-element.37.d_ref, bf16[4096,1024]{1,0:T(8,128)(2,1)S(1)} %bitcast.70, bf16[4096,1024]{1,0:T(8,128)(2,1)S(1)} %bitcast.70), custom_call_target="tpu_custom_call" | custom-call | flops 1073741824 | bytes 5767168 | tf_op jit(solution)/shard_map/back_projections/pallas_call | solution.py:180
  66.5 2.7 %collective-permute-done.6 = bf16[128,1024]{1,0:T(8,128)(2,1)S(1)} collective-permute-done((bf16[128,1024]{1,0:T(8,128)(2,1)S(1)}, bf16[128,1024]{1,0:T(8,128)(2,1)S(1)}, u32[]{:S(2)}, u32[]{:S(2)}) %collective-permute-start.6) | collective-permute-done | bytes 262176 | tf_op jit(solution)/shard_map/ppermute | solution.py:312
  69.3 1.3 collective-permute-start.7
  70.6 2.0 %back_projections.3 = bf16[2,128,1024]{2,1,0:T(8,128)(2,1)S(1)} custom-call(bf16[2,2,128,1024]{3,2,1,0:T(8,128)(2,1)S(1)} %get-tuple-element.36.d_ref, bf16[4096,1024]{1,0:T(8,128)(2,1)S(1)} %bitcast.70, bf16[4096,1024]{1,0:T(8,128)(2,1)S(1)} %bitcast.70), custom_call_target="tpu_custom_call" | custom-call | flops 1073741824 | bytes 5767168 | tf_op jit(solution)/shard_map/back_projections/pallas_call | solution.py:180
  72.6 7.1 %collective-permute-done.7 = bf16[128,1024]{1,0:T(8,128)(2,1)S(1)} collective-permute-done((bf16[128,1024]{1,0:T(8,128)(2,1)S(1)}, bf16[128,1024]{1,0:T(8,128)(2,1)S(1)}, u32[]{:S(2)}, u32[]{:S(2)}) %collective-permute-start.7) | collective-permute-done | bytes 262176 | tf_op jit(solution)/shard_map/ppermute | solution.py:312
  80.7 1.3 collective-permute-start.9
  82.0 5.9 %collective-permute-start.10 = (bf16[128,1024]{1,0:T(8,128)(2,1)}, bf16[128,1024]{1,0:T(8,128)(2,1)}, u32[]{:S(2)}, u32[]{:S(2)}) collective-permute-start(bf16[128,1024]{1,0:T(8,128)(2,1)} %get-tuple-element.45), channel_id=1, source_target_pairs={{0,4},{4,8},{8,12},{12,16},{16,20},{20,24},{24,28},{28,32},{32,36}... | collective-permute-start | bytes 786440 | tf_op jit(solution)/shard_map/ppermute | solution.py:313
  89.1 27.1 %all-to-all-start = ((bf16[16,128,256]{2,1,0:T(8,128)(2,1)}), bf16[16,128,256]{2,1,0:T(8,128)(2,1)S(1)}, u32[]{:S(2)}, u32[]{:S(2)}) async-start(bf16[16,128,256]{2,1,0:T(8,128)(2,1)} %bitcast.21), calls=%async_computation | async-start | bytes 2097152 | tf_op jit(solution)/shard_map/all_to_all | solution.py:264
  116.2 3.4 %copy-done.2 = bf16[4096,1024]{1,0:T(8,128)(2,1)S(1)} copy-done((bf16[4096,1024]{1,0:T(8,128)(2,1)S(1)}, bf16[4096,1024]{1,0:T(8,128)(2,1)}, u32[]{:S(2)}) %copy-start.2) | copy-done | bytes 8388632
  119.6 2.5 %last_projections.1 = f32[2,128,1024]{2,1,0:T(8,128)S(1)} custom-call(bf16[2,2,128,1024]{3,2,1,0:T(8,128)(2,1)S(1)} %get-tuple-element.34.d_ref, bf16[2,128,1024]{2,1,0:T(8,128)(2,1)S(1)} %get-tuple-element.35.dq_ref, bf16[4096,1024]{1,0:T(8,128)(2,1)S(1)} %copy-done.2, bf16[4096,1024]{1,0:T(8,128)(2,1)S(1)} %copy-done.2, bf16[4096,1024]{1,0:T(8,128)(2,1)S(1)} %copy-done.2), custom_call_target="tpu_custom_call" | custom-call | flops 1610612736 | bytes 8388608 | tf_op jit(solution)/shard_map/last_projections/pallas_call | solution.py:200
  123.3 1.3 collective-permute-start.11
  124.6 3.8 %collective-permute-done.11 = bf16[128,1024]{1,0:T(8,128)(2,1)S(1)} collective-permute-done((bf16[128,1024]{1,0:T(8,128)(2,1)S(1)}, bf16[128,1024]{1,0:T(8,128)(2,1)S(1)}, u32[]{:S(2)}, u32[]{:S(2)}) %collective-permute-start.11) | collective-permute-done | bytes 262176 | tf_op jit(solution)/shard_map/ppermute | solution.py:313
  128.5 14.3 %all-to-all-done = bf16[16,128,256]{2,1,0:T(8,128)(2,1)S(1)} async-done(((bf16[16,128,256]{2,1,0:T(8,128)(2,1)}), bf16[16,128,256]{2,1,0:T(8,128)(2,1)S(1)}, u32[]{:S(2)}, u32[]{:S(2)}) %all-to-all-start) | async-done | bytes 1048608 | tf_op jit(solution)/shard_map/all_to_all | solution.py:264
  143.5 3.3 %all-to-all-start.1 = ((bf16[8,16,256]{2,1,0:T(8,128)(2,1)}), bf16[8,16,256]{2,1,0:T(8,128)(2,1)S(1)}, u32[]{:S(2)}, u32[]{:S(2)}) async-start(bf16[8,16,256]{2,1,0:T(8,128)(2,1)} %bitcast.22), calls=%async_computation.1 | async-start | bytes 131072 | tf_op jit(solution)/shard_map/all_to_all | solution.py:266
  147.7 6.3 %all-to-all-done.1 = bf16[8,16,256]{2,1,0:T(8,128)(2,1)S(1)} async-done(((bf16[8,16,256]{2,1,0:T(8,128)(2,1)}), bf16[8,16,256]{2,1,0:T(8,128)(2,1)S(1)}, u32[]{:S(2)}, u32[]{:S(2)}) %all-to-all-start.1) | async-done | bytes 65568 | tf_op jit(solution)/shard_map/all_to_all | solution.py:266
  (59 shorter events, 13.2 us)
Async XLA Ops:
  1.7 17.9 %collective-permute-start.1 = (bf16[128,1024]{1,0:T(8,128)(2,1)S(1)}, bf16[128,1024]{1,0:T(8,128)(2,1)S(1)}, u32[]{:S(2)}, u32[]{:S(2)}) collective-permute-start(bf16[128,1024]{1,0:T(8,128)(2,1)S(1)} %get-tuple-element.48), channel_id=1, source_target_pairs={{4,0},{8,4},{12,8},{16,12},{20,16},{24,20},{28,24},{32,28},{36,32}... | collective-permute-start | bytes 786440 | tf_op jit(solution)/shard_map/ppermute | solution.py:300
  3.0 16.6 %collective-permute-start = (bf16[128,1024]{1,0:T(8,128)(2,1)S(1)}, bf16[128,1024]{1,0:T(8,128)(2,1)S(1)}, u32[]{:S(2)}, u32[]{:S(2)}) collective-permute-start(bf16[128,1024]{1,0:T(8,128)(2,1)S(1)} %get-tuple-element.49), channel_id=1, source_target_pairs={{0,4},{4,8},{8,12},{12,16},{16,20},{20,24},{24,28},{28,32},{32,36}... | collective-permute-start | bytes 786440 | tf_op jit(solution)/shard_map/ppermute | solution.py:299
  9.2 3.4 %copy-start = (bf16[4096,1024]{1,0:T(8,128)(2,1)S(1)}, bf16[4096,1024]{1,0:T(8,128)(2,1)}, u32[]{:S(2)}) copy-start(bf16[4096,1024]{1,0:T(8,128)(2,1)} %wv_ref.15) | copy-start | bytes 25165828
  12.6 1.0 copy-start.3
  13.6 1.0 copy-start.5
  14.7 4.9 %copy-start.4 = (bf16[1,1,2,128,1024]{4,3,2,1,0:T(8,128)(2,1)S(1)}, bf16[1,1,2,128,1024]{4,3,2,1,0:T(8,128)(2,1)}, u32[]{:S(2)}) copy-start(bf16[1,1,2,128,1024]{4,3,2,1,0:T(8,128)(2,1)} %param.4) | copy-start | bytes 1572868
  18.7 0.8 copy-start.7
  19.5 11.5 %copy-start.9 = (bf16[2,128,1024]{2,1,0:T(8,128)(2,1)}, bf16[2,128,1024]{2,1,0:T(8,128)(2,1)S(1)}, u32[]{:S(2)}) copy-start(bf16[2,128,1024]{2,1,0:T(8,128)(2,1)S(1)} %get-tuple-element.23.da_ref) | copy-start | bytes 1572868
  19.6 11.4 %collective-permute-start.3 = (bf16[128,1024]{1,0:T(8,128)(2,1)S(1)}, bf16[128,1024]{1,0:T(8,128)(2,1)S(1)}, u32[]{:S(2)}, u32[]{:S(2)}) collective-permute-start(bf16[128,1024]{1,0:T(8,128)(2,1)S(1)} %broadcast_select_fusion.2.down_ref), channel_id=1, source_target_pairs={{4,0},{8,4},{12,8},{16,12},{20,16},{24,20},{28,24},{32,28},{36,32}... | collective-permute-start | bytes 786440 | tf_op jit(solution)/shard_map/ppermute | solution.py:300
  21.0 10.0 %collective-permute-start.2 = (bf16[128,1024]{1,0:T(8,128)(2,1)S(1)}, bf16[128,1024]{1,0:T(8,128)(2,1)S(1)}, u32[]{:S(2)}, u32[]{:S(2)}) collective-permute-start(bf16[128,1024]{1,0:T(8,128)(2,1)S(1)} %collective-permute-done.up_ref), channel_id=1, source_target_pairs={{0,4},{4,8},{8,12},{12,16},{16,20},{20,24},{24,28},{28,32},{32,36}... | collective-permute-start | bytes 786440 | tf_op jit(solution)/shard_map/ppermute | solution.py:299
  25.2 3.4 %copy-start.1 = (bf16[4096,1024]{1,0:T(8,128)(2,1)S(1)}, bf16[4096,1024]{1,0:T(8,128)(2,1)}, u32[]{:S(2)}) copy-start(bf16[4096,1024]{1,0:T(8,128)(2,1)} %wv_ref.15) | copy-start | bytes 25165828
  31.1 8.1 %collective-permute-start.5 = (bf16[128,1024]{1,0:T(8,128)(2,1)S(1)}, bf16[128,1024]{1,0:T(8,128)(2,1)S(1)}, u32[]{:S(2)}, u32[]{:S(2)}) collective-permute-start(bf16[128,1024]{1,0:T(8,128)(2,1)S(1)} %broadcast_select_fusion.1.down_ref), channel_id=1, source_target_pairs={{4,0},{8,4},{12,8},{16,12},{20,16},{24,20},{28,24},{32,28},{36,32}... | collective-permute-start | bytes 786440 | tf_op jit(solution)/shard_map/ppermute | solution.py:300
  32.5 7.5 %collective-permute-start.4 = (bf16[128,1024]{1,0:T(8,128)(2,1)S(1)}, bf16[128,1024]{1,0:T(8,128)(2,1)S(1)}, u32[]{:S(2)}, u32[]{:S(2)}) collective-permute-start(bf16[128,1024]{1,0:T(8,128)(2,1)S(1)} %collective-permute-done.2.up_ref), channel_id=1, source_target_pairs={{0,4},{4,8},{8,12},{12,16},{16,20},{20,24},{24,28},{28,32},{32,36}... | collective-permute-start | bytes 786440 | tf_op jit(solution)/shard_map/ppermute | solution.py:299
  36.6 14.3 %slice-start = ((s8[8388608]{0:T(1024)(128)(4,1)}), s8[4194304]{0:T(1024)(128)(4,1)S(1)}, s32[]{:S(2)}) async-start(s8[8388608]{0:T(1024)(128)(4,1)} %bitcast.69), calls=%async_computation.2 | async-start | bytes 8388608
  39.2 3.2 %copy-start.8 = (bf16[2,128,1024]{2,1,0:T(8,128)(2,1)S(1)}, bf16[2,128,1024]{2,1,0:T(8,128)(2,1)}, u32[]{:S(2)}) copy-start(bf16[2,128,1024]{2,1,0:T(8,128)(2,1)} %copy-done.7) | copy-start | bytes 1572868
  39.2 3.2 %copy-start.10 = (bf16[2,128,1024]{2,1,0:T(8,128)(2,1)S(1)}, bf16[2,128,1024]{2,1,0:T(8,128)(2,1)}, u32[]{:S(2)}) copy-start(bf16[2,128,1024]{2,1,0:T(8,128)(2,1)} %copy-done.9) | copy-start | bytes 1572868
  39.2 11.8 %slice-start.1 = ((s8[8388608]{0:T(1024)(128)(4,1)}), s8[4194304]{0:T(1024)(128)(4,1)S(1)}, s32[]{:S(2)}) async-start(s8[8388608]{0:T(1024)(128)(4,1)} %bitcast.69), calls=%async_computation.3 | async-start | bytes 8388608
  51.0 2.0 %copy-start.6 = (bf16[1,1,2,128,1024]{4,3,2,1,0:T(8,128)(2,1)S(1)}, bf16[1,1,2,128,1024]{4,3,2,1,0:T(8,128)(2,1)}, u32[]{:S(2)}) copy-start(bf16[1,1,2,128,1024]{4,3,2,1,0:T(8,128)(2,1)} %param.7) | copy-start | bytes 1572868
  54.1 33.7 %collective-permute-start.12 = (bf16[2,1024,256]{2,1,0:T(8,128)(2,1)S(1)}, bf16[2,1024,256]{2,1,0:T(8,128)(2,1)S(1)}, u32[]{:S(2)}, u32[]{:S(2)}) collective-permute-start(bf16[2,1024,256]{2,1,0:T(8,128)(2,1)S(1)} %get-tuple-element.41), channel_id=1, source_target_pairs={{0,1},{1,0},{2,3},{3,2},{4,5},{5,4},{6,7},{7,6},{8,9},{9,8},{10,11... | collective-permute-start | bytes 3145736 | tf_op jit(solution)/shard_map/ppermute | solution.py:262
  58.4 10.8 %collective-permute-start.6 = (bf16[128,1024]{1,0:T(8,128)(2,1)S(1)}, bf16[128,1024]{1,0:T(8,128)(2,1)S(1)}, u32[]{:S(2)}, u32[]{:S(2)}) collective-permute-start(bf16[128,1024]{1,0:T(8,128)(2,1)S(1)} %get-tuple-element.47), channel_id=1, source_target_pairs={{4,0},{8,4},{12,8},{16,12},{20,16},{24,20},{28,24},{32,28},{36,32}... | collective-permute-start | bytes 786440 | tf_op jit(solution)/shard_map/ppermute | solution.py:312
  59.7 12.9 %collective-permute-start.8 = (bf16[128,1024]{1,0:T(8,128)(2,1)S(1)}, bf16[128,1024]{1,0:T(8,128)(2,1)S(1)}, u32[]{:S(2)}, u32[]{:S(2)}) collective-permute-start(bf16[128,1024]{1,0:T(8,128)(2,1)S(1)} %get-tuple-element.46), channel_id=1, source_target_pairs={{0,4},{4,8},{8,12},{12,16},{16,20},{20,24},{24,28},{28,32},{32,36}... | collective-permute-start | bytes 786440 | tf_op jit(solution)/shard_map/ppermute | solution.py:313
  69.3 10.4 %collective-permute-start.7 = (bf16[128,1024]{1,0:T(8,128)(2,1)S(1)}, bf16[128,1024]{1,0:T(8,128)(2,1)S(1)}, u32[]{:S(2)}, u32[]{:S(2)}) collective-permute-start(bf16[128,1024]{1,0:T(8,128)(2,1)S(1)} %fusion.8), channel_id=1, source_target_pairs={{4,0},{8,4},{12,8},{16,12},{20,16},{24,20},{28,24},{32,28},{36,32}... | collective-permute-start | bytes 786440 | tf_op jit(solution)/shard_map/ppermute | solution.py:312
  80.7 41.4 %collective-permute-start.9 = (bf16[128,1024]{1,0:T(8,128)(2,1)}, bf16[128,1024]{1,0:T(8,128)(2,1)S(1)}, u32[]{:S(2)}, u32[]{:S(2)}) collective-permute-start(bf16[128,1024]{1,0:T(8,128)(2,1)} %get-tuple-element.44), channel_id=1, source_target_pairs={{4,0},{8,4},{12,8},{16,12},{20,16},{24,20},{28,24},{32,28},{36,32}... | collective-permute-start | bytes 786440 | tf_op jit(solution)/shard_map/ppermute | solution.py:312
  82.0 40.2 %collective-permute-start.10 = (bf16[128,1024]{1,0:T(8,128)(2,1)}, bf16[128,1024]{1,0:T(8,128)(2,1)}, u32[]{:S(2)}, u32[]{:S(2)}) collective-permute-start(bf16[128,1024]{1,0:T(8,128)(2,1)} %get-tuple-element.45), channel_id=1, source_target_pairs={{0,4},{4,8},{8,12},{12,16},{16,20},{20,24},{24,28},{28,32},{32,36}... | collective-permute-start | bytes 786440 | tf_op jit(solution)/shard_map/ppermute | solution.py:313
  89.1 53.6 %all-to-all-start = ((bf16[16,128,256]{2,1,0:T(8,128)(2,1)}), bf16[16,128,256]{2,1,0:T(8,128)(2,1)S(1)}, u32[]{:S(2)}, u32[]{:S(2)}) async-start(bf16[16,128,256]{2,1,0:T(8,128)(2,1)} %bitcast.21), calls=%async_computation | async-start | bytes 2097152 | tf_op jit(solution)/shard_map/all_to_all | solution.py:264
  116.2 3.4 %copy-start.2 = (bf16[4096,1024]{1,0:T(8,128)(2,1)S(1)}, bf16[4096,1024]{1,0:T(8,128)(2,1)}, u32[]{:S(2)}) copy-start(bf16[4096,1024]{1,0:T(8,128)(2,1)} %wv_ref.15) | copy-start | bytes 25165828
  123.3 5.1 %collective-permute-start.11 = (bf16[128,1024]{1,0:T(8,128)(2,1)S(1)}, bf16[128,1024]{1,0:T(8,128)(2,1)S(1)}, u32[]{:S(2)}, u32[]{:S(2)}) collective-permute-start(bf16[128,1024]{1,0:T(8,128)(2,1)S(1)} %get-tuple-element.43), channel_id=1, source_target_pairs={{0,4},{4,8},{8,12},{12,16},{16,20},{20,24},{24,28},{28,32},{32,36}... | collective-permute-start | bytes 786440 | tf_op jit(solution)/shard_map/ppermute | solution.py:313
  143.5 10.5 %all-to-all-start.1 = ((bf16[8,16,256]{2,1,0:T(8,128)(2,1)}), bf16[8,16,256]{2,1,0:T(8,128)(2,1)S(1)}, u32[]{:S(2)}, u32[]{:S(2)}) async-start(bf16[8,16,256]{2,1,0:T(8,128)(2,1)} %bitcast.22), calls=%async_computation.1 | async-start | bytes 131072 | tf_op jit(solution)/shard_map/all_to_all | solution.py:266

commit v3 on v2

--- a/solution.py
+++ b/solution.py
@@ -36,6 +36,14 @@
 
 def cost(flops, moved, exps=0):
     return pl.CostEstimate(flops=flops, bytes_accessed=moved, transcendentals=exps)
+
+
+def in_hbm(*arrays):
+    return [pltpu.with_memory_space_constraint(a, pltpu.HBM) for a in arrays]
+
+
+def in_vmem(*arrays):
+    return [pltpu.with_memory_space_constraint(a, pltpu.VMEM) for a in arrays]
 
 
 def weight_cols(which):
@@ -75,10 +83,10 @@
         ],
         out_specs=[row_tile, row_tile, pl.BlockSpec((2, 2, BLOCK, TILE), lambda t: (0, 0, 0, t))],
         out_shape=[rows, rows, jax.ShapeDtypeStruct((2, 2, BLOCK, D), BF)],
-        compiler_params=params(32),
+        compiler_params=params(12),
         cost_estimate=cost(8 * 2 * BLOCK * D * D, 8 * D * D + 12 * BLOCK * D),
         name="own_projections",
-    )(x, g, weights, weights, weights, weights)
+    )(*in_hbm(x, g, weights, weights, weights, weights))
 
 
 def halo_kernel(up_ref, down_ref, wk_ref, wv_ref, kv_ref):
@@ -94,10 +102,10 @@
         in_specs=[whole((BLOCK, D)), whole((BLOCK, D)), weight_cols(1), weight_cols(2)],
         out_specs=pl.BlockSpec((2, 2, BLOCK, TILE), lambda t: (0, 0, 0, t)),
         out_shape=jax.ShapeDtypeStruct((2, 2, BLOCK, D), BF),
-        compiler_params=params(32),
+        compiler_params=params(10),
         cost_estimate=cost(4 * 2 * BLOCK * D * D, 4 * D * D + 12 * BLOCK * D),
         name="halo_projections",
-    )(up, down, weights, weights)
+    )(up, down, *in_vmem(weights, weights))
 
 
 def attention_kernel(
@@ -164,10 +172,10 @@
         in_specs=[row_spec, row_spec] + [pair_spec] * 4 + [bias_spec],
         out_specs=[row_spec, row_spec] + [pair_spec] * 4,
         out_shape=[rows, rows] + [pairs] * 4,
-        compiler_params=params(32),
+        compiler_params=params(24),
         cost_estimate=cost(2 * 10 * BLOCK * WIN * BLOCK * D * 2, 12 * 2**20, 2**21),
         name="attention",
-    )(q, da, *kvs, bias)
+    )(*in_vmem(q, da, *kvs, bias))
 
 
 def back_kernel(d_ref, wk_ref, wv_ref, out_ref):
@@ -183,10 +191,10 @@
         in_specs=[whole((2, 2, BLOCK, D)), weight_rows(1), weight_rows(2)],
         out_specs=pl.BlockSpec((2, BLOCK, TILE), lambda t: (0, 0, t)),
         out_shape=jax.ShapeDtypeStruct((2, BLOCK, D), dtype),
-        compiler_params=params(32),
+        compiler_params=params(10),
         cost_estimate=cost(4 * 2 * BLOCK * D * D, 4 * D * D + 12 * BLOCK * D),
         name="back_projections",
-    )(d, weights, weights)
+    )(*in_vmem(d, weights, weights))
 
 
 def last_kernel(d_ref, dq_ref, wq_ref, wk_ref, wv_ref, out_ref):
@@ -209,10 +217,10 @@
         ],
         out_specs=pl.BlockSpec((2, BLOCK, TILE), lambda t: (0, 0, t)),
         out_shape=jax.ShapeDtypeStruct((2, BLOCK, D), F32),
-        compiler_params=params(32),
+        compiler_params=params(12),
         cost_estimate=cost(6 * 2 * BLOCK * D * D, 6 * D * D + 16 * BLOCK * D),
         name="last_projections",
-    )(d, dq, weights, weights, weights)
+    )(*in_vmem(d, dq, weights, weights, weights))
 
 
 def outer_kernel(core_ref, o_ref, keep_ref, send_ref, kept_ref, sent_ref):
@@ -237,10 +245,10 @@
             out_specs=[result_spec, result_spec],
         ),
         out_shape=[result, result],
-        compiler_params=params(32),
+        compiler_params=params(12),
         cost_estimate=cost(4 * BLOCK * D * D, 2 * D * D + 8 * BLOCK * D),
         name="outer_products",
-    )(core.reshape(1), o, g, g)
+    )(core, *in_vmem(o, g, g))
 
 
 def place(y, x, z, core):
@@ -258,23 +266,26 @@
     return (a.astype(F32) + b.astype(F32)).astype(BF)
 
 
-def reduce_outer(kept, sent):
-    total = add(kept, lax.ppermute(sent, "dp", CORE_PAIRS))
+def sum_over_plane(total):
     total = total.reshape(16, 8 * 16, TILE)
     total = lax.all_to_all(total, ("blk", "dp"), 0, 0, axis_index_groups=PLANES)
-    total = jnp.sum(total.astype(F32), axis=0).astype(BF).reshape(8, 16, TILE)
+    return jnp.sum(total.astype(F32), axis=0).astype(BF).reshape(8, 16, TILE)
+
+
+def sum_over_line(total):
     total = lax.all_to_all(total, "blk", 0, 0, axis_index_groups=LINES)
     return jnp.sum(total.astype(F32), axis=0)
 
 
-def score_limits(key_valid, position):
-    blocks = 2 * 64
-    both = jnp.stack([position, blocks - 1 - position])
+def window_validity(key_valid, both):
     seq_valid = jnp.concatenate([key_valid[0, :, 0], jnp.flip(key_valid[0, :, 1], axis=0)], axis=0)
     seq_valid = jnp.concatenate([jnp.zeros((WIN - 1, BLOCK), jnp.int32), seq_valid], axis=0)
-    valid = jnp.stack(
+    return jnp.stack(
         [lax.dynamic_slice_in_dim(seq_valid, both[i], WIN, 0).reshape(WIN * BLOCK) for i in range(2)]
     )
+
+
+def score_limits(valid, both):
     q_pos = jnp.arange(BLOCK, dtype=jnp.int32)[None, :, None]
     k_pos = (jnp.arange(WIN * BLOCK, dtype=jnp.int32) - (WIN - 1) * BLOCK)[None, None, :]
     inside = k_pos + both[:, None, None] * BLOCK >= 0
@@ -285,13 +296,20 @@
 def per_device(tokens, key_valid, weights, out_grad):
     position = lax.axis_index("blk")
     shot = lax.axis_index("dp")
+    at_first = position == 0
     at_last = position == 63
-    up = [(i, i + 1) for i in range(63)]
-    down = [(i + 1, i) for i in range(63)]
+    up = [(i, (i + 1) % 64) for i in range(64)]
+    down = [(t, s) for s, t in up]
     x = tokens.reshape(2, BLOCK, D)
     g = out_grad.reshape(2, BLOCK, D)
 
-    bias = score_limits(key_valid, position)
+    both = jnp.stack([position, 2 * 64 - 1 - position])
+    valid = window_validity(key_valid, both)
+    core = (shot % 2).reshape(1)
+    x, g, valid, both, core, at_first, at_last = lax.optimization_barrier(
+        (x, g, valid, both, core, at_first, at_last)
+    )
+    bias = score_limits(valid, both)
     q, da, kv0 = own_projections(x, g, weights)
     kvs = [kv0]
     state_up, state_down = x[0], x[1]
@@ -303,19 +321,30 @@
         state_up, state_down = new_up, new_down
     o, dq, d3, d2, d1, d0 = attention(q, da, kvs[::-1], bias)
 
-    kept, sent = outer_products(o, g, shot % 2)
-    w_grad = reduce_outer(kept, sent)
-
     returned = back_projections(d3, weights, BF)
+    o, returned = lax.optimization_barrier((o, returned))
+    kept, sent = outer_products(o, g, core)
+    chip_sum = add(kept, lax.ppermute(sent, "dp", CORE_PAIRS))
+    d2, chip_sum = lax.optimization_barrier((d2, chip_sum))
     terms = [back_projections(d2, weights, BF), back_projections(d1, weights, BF), last_projections(d0, dq, weights)]
-    for term in terms:
+    for hop, term in enumerate(terms):
         from_after = lax.ppermute(returned[0], "blk", down)
         from_before = lax.ppermute(returned[1], "blk", up)
         extra = jnp.where(at_last, returned[1], jnp.zeros_like(returned[1])).astype(F32)
+        from_before = jnp.where(at_first, jnp.zeros_like(from_before), from_before)
         total = jnp.stack(
             [term[0].astype(F32) + from_after.astype(F32) + extra, term[1].astype(F32) + from_before.astype(F32)]
         )
         returned = total.astype(BF)
+        if hop == 0:
+            returned, chip_sum = lax.optimization_barrier((returned, chip_sum))
+            plane_sum = sum_over_plane(chip_sum)
+            returned, plane_sum, terms[1], terms[2] = lax.optimization_barrier(
+                (returned, plane_sum, terms[1], terms[2])
+            )
+            w_grad = sum_over_line(plane_sum)
+        if hop == 1:
+            returned, w_grad = lax.optimization_barrier((returned, w_grad))
     return returned.reshape(tokens.shape), w_grad
 
 

time: 156 us -> 129 us (0.83)
  the two profiles are of different devices: /device:TPU:1 before, /device:TPU:24 now
where the time goes in v3:
time: 129 us; the launch traced here: 128 us
  waiting for transfers between devices  42 us (33%)
  Pallas kernels  32.5 us (25%)
  starting transfers between devices  25.2 us (20%)
  blocking collectives  10.8 us (8%)
  local copies, waits for them, and re-layouts  10 us (8%)
  other arithmetic  6.16 us (5%)
    ppermute x3, waiting for transfers between devices, per_device(): new_up = lax.ppermute(state_up, 'blk', up)  15.6 us
    ppermute x3, waiting for transfers between devices, per_device(): from_before = lax.ppermute(returned[1], 'blk', up)  11.2 us
    all_to_all x1, blocking collectives, sum_over_line(): total = lax.all_to_all(total, 'blk', 0, 0, axis_index_groups=LINES)  10.8 us
    ppermute x3, starting transfers between devices, per_device(): lax.ppermute(state_down, 'blk', down)  10.3 us
    pallas_call x1, Pallas kernels, attention(): pl.pallas_call(attention_kernel, grid=(2, D // width), in_specs=[row_spec...  8.56 us
    pallas_call x3, Pallas kernels, halo_projections(): pl.pallas_call(halo_kernel, grid=(D // TILE,), in_specs=[whole((BLOCK, D)...  7.27 us
    pallas_call x1, Pallas kernels, own_projections(): pl.pallas_call(own_kernel, grid=(D // TILE,), in_specs=[whole((2, BLOCK,...  7.08 us
    ppermute x3, waiting for transfers between devices, per_device(): from_after = lax.ppermute(returned[0], 'blk', down)  6.84 us
  transfers between devices with their start and end apart: 14, of which 11 were waited for; matrix products, arithmetic and copies ran while one was open for 2% of the time, Pallas kernels for 14%

profile of v3, /device:TPU:24, one launch (start us, length us, event | category | flops | bytes accessed | tf_op | source)
XLA Modules:
  0.0 127.6 jit_solution(8333288452795261626)
XLA Ops:
  2.9 8.3 %collective-permute-start.1 = (bf16[128,1024]{1,0:T(8,128)(2,1)S(1)}, bf16[128,1024]{1,0:T(8,128)(2,1)S(1)}, u32[]{:S(2)}, u32[]{:S(2)}) collective-permute-start(bf16[128,1024]{1,0:T(8,128)(2,1)S(1)} %get-tuple-element.92), channel_id=1, source_target_pairs={{4,0},{8,4},{12,8},{16,12},{20,16},{24,20},{28,24},{32,28},{36,32}... | collective-permute-start | bytes 786440 | tf_op jit(solution)/shard_map/ppermute | solution.py:318
  11.4 7.1 %own_projections.1 = (bf16[2,128,1024]{2,1,0:T(8,128)(2,1)S(1)}, bf16[2,128,1024]{2,1,0:T(8,128)(2,1)S(1)}, bf16[2,2,128,1024]{3,2,1,0:T(8,128)(2,1)S(1)}) custom-call(bf16[2,128,1024]{2,1,0:T(8,128)(2,1)} %bitcast.86, bf16[2,128,1024]{2,1,0:T(8,128)(2,1)} %bitcast.81, bf16[4096,1024]{1,0:T(8,128)(2,1)} %wv_ref.15, bf16[4096,1024]{1,0:T(8,128)(2,1)} %wv_ref.15, ...), custom_call_target="tpu_custom_call" | custom-call | flops 2147483648 | bytes 9961472 | tf_op jit(solution)/shard_map/own_projections/pallas_call | solution.py:73
  18.5 4.7 %collective-permute-done.up_ref = bf16[128,1024]{1,0:T(8,128)(2,1)S(1)} collective-permute-done((bf16[128,1024]{1,0:T(8,128)(2,1)S(1)}, bf16[128,1024]{1,0:T(8,128)(2,1)S(1)}, u32[]{:S(2)}, u32[]{:S(2)}) %collective-permute-start) | collective-permute-done | bytes 262176 | tf_op jit(solution)/shard_map/ppermute | solution.py:317
  23.2 1.6 %collective-permute-start.3 = (bf16[128,1024]{1,0:T(8,128)(2,1)S(1)}, bf16[128,1024]{1,0:T(8,128)(2,1)S(1)}, u32[]{:S(2)}, u32[]{:S(2)}) collective-permute-start(bf16[128,1024]{1,0:T(8,128)(2,1)S(1)} %broadcast_select_fusion.2.down_ref), channel_id=1, source_target_pairs={{4,0},{8,4},{12,8},{16,12},{20,16},{24,20},{28,24},{32,28},{36,32}... | collective-permute-start | bytes 786440 | tf_op jit(solution)/shard_map/ppermute | solution.py:318
  25.3 2.4 %halo_projections.3.kv1_ref = bf16[2,2,128,1024]{3,2,1,0:T(8,128)(2,1)S(1)} custom-call(bf16[128,1024]{1,0:T(8,128)(2,1)S(1)} %collective-permute-done.up_ref, bf16[128,1024]{1,0:T(8,128)(2,1)S(1)} %broadcast_select_fusion.2.down_ref, bf16[4096,1024]{1,0:T(8,128)(2,1)S(1)} %bitcast.80, bf16[4096,1024]{1,0:T(8,128)(2,1)S(1)} %bitcast.80), custom_call_target="tpu_custom_call" | custom-call | flops 1073741824 | bytes 5767168 | tf_op jit(solution)/shard_map/halo_projections/pallas_call | solution.py:99
  27.8 2.3 %collective-permute-done.3 = bf16[128,1024]{1,0:T(8,128)(2,1)S(1)} collective-permute-done((bf16[128,1024]{1,0:T(8,128)(2,1)S(1)}, bf16[128,1024]{1,0:T(8,128)(2,1)S(1)}, u32[]{:S(2)}, u32[]{:S(2)}) %collective-permute-start.3) | collective-permute-done | bytes 262176 | tf_op jit(solution)/shard_map/ppermute | solution.py:318
  30.1 6.2 %collective-permute-done.2.up_ref = bf16[128,1024]{1,0:T(8,128)(2,1)S(1)} collective-permute-done((bf16[128,1024]{1,0:T(8,128)(2,1)S(1)}, bf16[128,1024]{1,0:T(8,128)(2,1)S(1)}, u32[]{:S(2)}, u32[]{:S(2)}) %collective-permute-start.2) | collective-permute-done | bytes 262176 | tf_op jit(solution)/shard_map/ppermute | solution.py:317
  36.8 1.8 %collective-permute-start.4 = (bf16[128,1024]{1,0:T(8,128)(2,1)S(1)}, bf16[128,1024]{1,0:T(8,128)(2,1)S(1)}, u32[]{:S(2)}, u32[]{:S(2)}) collective-permute-start(bf16[128,1024]{1,0:T(8,128)(2,1)S(1)} %collective-permute-done.2.up_ref), channel_id=1, source_target_pairs={{0,4},{4,8},{8,12},{12,16},{16,20},{20,24},{24,28},{28,32},{32,36}... | collective-permute-start | bytes 786440 | tf_op jit(solution)/shard_map/ppermute | solution.py:317
  38.6 2.4 %halo_projections.4.kv2_ref = bf16[2,2,128,1024]{3,2,1,0:T(8,128)(2,1)S(1)} custom-call(bf16[128,1024]{1,0:T(8,128)(2,1)S(1)} %collective-permute-done.2.up_ref, bf16[128,1024]{1,0:T(8,128)(2,1)S(1)} %broadcast_select_fusion.1.down_ref, bf16[4096,1024]{1,0:T(8,128)(2,1)S(1)} %bitcast.80, bf16[4096,1024]{1,0:T(8,128)(2,1)S(1)} %bitcast.80), custom_call_target="tpu_custom_call" | custom-call | flops 1073741824 | bytes 5767168 | tf_op jit(solution)/shard_map/halo_projections/pallas_call | solution.py:99
  41.0 1.7 %collective-permute-done.5 = bf16[128,1024]{1,0:T(8,128)(2,1)S(1)} collective-permute-done((bf16[128,1024]{1,0:T(8,128)(2,1)S(1)}, bf16[128,1024]{1,0:T(8,128)(2,1)S(1)}, u32[]{:S(2)}, u32[]{:S(2)}) %collective-permute-start.5) | collective-permute-done | bytes 262176 | tf_op jit(solution)/shard_map/ppermute | solution.py:318
  42.8 4.7 %collective-permute-done.4.up_ref = bf16[128,1024]{1,0:T(8,128)(2,1)S(1)} collective-permute-done((bf16[128,1024]{1,0:T(8,128)(2,1)S(1)}, bf16[128,1024]{1,0:T(8,128)(2,1)S(1)}, u32[]{:S(2)}, u32[]{:S(2)}) %collective-permute-start.4) | collective-permute-done | bytes 262176 | tf_op jit(solution)/shard_map/ppermute | solution.py:317
  47.5 2.4 %halo_projections.5.kv3_ref = bf16[2,2,128,1024]{3,2,1,0:T(8,128)(2,1)S(1)} custom-call(bf16[128,1024]{1,0:T(8,128)(2,1)S(1)} %collective-permute-done.4.up_ref, bf16[128,1024]{1,0:T(8,128)(2,1)S(1)} %broadcast_select_fusion.down_ref, bf16[4096,1024]{1,0:T(8,128)(2,1)S(1)} %bitcast.80, bf16[4096,1024]{1,0:T(8,128)(2,1)S(1)} %bitcast.80), custom_call_target="tpu_custom_call" | custom-call | flops 1073741824 | bytes 5767168 | tf_op jit(solution)/shard_map/halo_projections/pallas_call | solution.py:99
  49.9 8.6 %attention.1 = (bf16[2,128,1024]{2,1,0:T(8,128)(2,1)S(1)}, bf16[2,128,1024]{2,1,0:T(8,128)(2,1)S(1)}, bf16[2,2,128,1024]{3,2,1,0:T(8,128)(2,1)S(1)}, bf16[2,2,12...) custom-call(bf16[2,128,1024]{2,1,0:T(8,128)(2,1)S(1)} %get-tuple-element.43., ...), custom_call_target="tpu_custom_call" | custom-call | flops 2684354560 | bytes 12582912 | tf_op jit(solution)/shard_map/attention/pallas_call | solution.py:169
  58.5 2.0 %back_projections.3 = bf16[2,128,1024]{2,1,0:T(8,128)(2,1)S(1)} custom-call(bf16[2,2,128,1024]{3,2,1,0:T(8,128)(2,1)S(1)} %get-tuple-element.61.d_ref, bf16[4096,1024]{1,0:T(8,128)(2,1)S(1)} %bitcast.80, bf16[4096,1024]{1,0:T(8,128)(2,1)S(1)} %bitcast.80), custom_call_target="tpu_custom_call" | custom-call | flops 1073741824 | bytes 5767168 | tf_op jit(solution)/shard_map/back_projections/pallas_call | solution.py:188
  60.5 1.1 outer_products.1
  61.9 2.0 %collective-permute-start.8 = (bf16[128,1024]{1,0:T(8,128)(2,1)S(1)}, bf16[128,1024]{1,0:T(8,128)(2,1)S(1)}, u32[]{:S(2)}, u32[]{:S(2)}) collective-permute-start(bf16[128,1024]{1,0:T(8,128)(2,1)S(1)} %get-tuple-element.91), channel_id=1, source_target_pairs={{0,4},{4,8},{8,12},{12,16},{16,20},{20,24},{24,28},{28,32},{32,36}... | collective-permute-start | bytes 786440 | tf_op jit(solution)/shard_map/ppermute | solution.py:332
  64.4 1.2 add_convert_fusion
  65.6 2.0 %back_projections.4 = bf16[2,128,1024]{2,1,0:T(8,128)(2,1)S(1)} custom-call(bf16[2,2,128,1024]{3,2,1,0:T(8,128)(2,1)S(1)} %get-tuple-element.65.d_ref, bf16[4096,1024]{1,0:T(8,128)(2,1)S(1)} %bitcast.80, bf16[4096,1024]{1,0:T(8,128)(2,1)S(1)} %bitcast.80), custom_call_target="tpu_custom_call" | custom-call | flops 1073741824 | bytes 5767168 | tf_op jit(solution)/shard_map/back_projections/pallas_call | solution.py:188
  67.6 3.0 %collective-permute-done.7 = bf16[128,1024]{1,0:T(8,128)(2,1)S(1)} collective-permute-done((bf16[128,1024]{1,0:T(8,128)(2,1)S(1)}, bf16[128,1024]{1,0:T(8,128)(2,1)S(1)}, u32[]{:S(2)}, u32[]{:S(2)}) %collective-permute-start.7) | collective-permute-done | bytes 262176 | tf_op jit(solution)/shard_map/ppermute | solution.py:331
  70.5 4.5 %collective-permute-done.8 = bf16[128,1024]{1,0:T(8,128)(2,1)S(1)} collective-permute-done((bf16[128,1024]{1,0:T(8,128)(2,1)S(1)}, bf16[128,1024]{1,0:T(8,128)(2,1)S(1)}, u32[]{:S(2)}, u32[]{:S(2)}) %collective-permute-start.8) | collective-permute-done | bytes 262176 | tf_op jit(solution)/shard_map/ppermute | solution.py:332
  76.1 5.2 %all-to-all-start = ((bf16[16,128,256]{2,1,0:T(8,128)(2,1)}), bf16[16,128,256]{2,1,0:T(8,128)(2,1)}, u32[]{:S(2)}, u32[]{:S(2)}) async-start(bf16[16,128,256]{2,1,0:T(8,128)(2,1)} %bitcast.84), calls=%async_computation | async-start | bytes 2097152 | tf_op jit(solution)/shard_map/all_to_all | solution.py:271
  81.4 3.4 %copy-done = bf16[4096,1024]{1,0:T(8,128)(2,1)S(1)} copy-done((bf16[4096,1024]{1,0:T(8,128)(2,1)S(1)}, bf16[4096,1024]{1,0:T(8,128)(2,1)}, u32[]{:S(2)}) %copy-start) | copy-done | bytes 8388632
  84.8 2.0 %back_projections.5 = bf16[2,128,1024]{2,1,0:T(8,128)(2,1)S(1)} custom-call(bf16[2,2,128,1024]{3,2,1,0:T(8,128)(2,1)S(1)} %get-tuple-element.71.d_ref, bf16[4096,1024]{1,0:T(8,128)(2,1)S(1)} %copy-done, bf16[4096,1024]{1,0:T(8,128)(2,1)S(1)} %copy-done), custom_call_target="tpu_custom_call" | custom-call | flops 1073741824 | bytes 5767168 | tf_op jit(solution)/shard_map/back_projections/pallas_call | solution.py:188
  86.8 3.4 %copy-done.1 = bf16[4096,1024]{1,0:T(8,128)(2,1)S(1)} copy-done((bf16[4096,1024]{1,0:T(8,128)(2,1)S(1)}, bf16[4096,1024]{1,0:T(8,128)(2,1)}, u32[]{:S(2)}) %copy-start.1) | copy-done | bytes 8388632
  90.1 2.5 %last_projections.1 = f32[2,128,1024]{2,1,0:T(8,128)S(1)} custom-call(bf16[2,2,128,1024]{3,2,1,0:T(8,128)(2,1)S(1)} %get-tuple-element.72.d_ref, bf16[2,128,1024]{2,1,0:T(8,128)(2,1)S(1)} %get-tuple-element.73.dq_ref, bf16[4096,1024]{1,0:T(8,128)(2,1)S(1)} %copy-done.1, bf16[4096,1024]{1,0:T(8,128)(2,1)S(1)} %copy-done.1, bf16[4096,1024]{1,0:T(8,128)(2,1)S(1)} %copy-done.1), custom_call_target="tpu_custom_call" | custom-call | flops 1610612736 | bytes 8388608 | tf_op jit(solution)/shard_map/last_projections/pallas_call | solution.py:208
  92.6 3.8 %all-to-all-done = bf16[16,128,256]{2,1,0:T(8,128)(2,1)} async-done(((bf16[16,128,256]{2,1,0:T(8,128)(2,1)}), bf16[16,128,256]{2,1,0:T(8,128)(2,1)}, u32[]{:S(2)}, u32[]{:S(2)}) %all-to-all-start) | async-done | bytes 1048608 | tf_op jit(solution)/shard_map/all_to_all | solution.py:271
  96.4 1.4 %reduce_sum.21 = bf16[128,256]{1,0:T(8,128)(2,1)S(1)} reduce(bf16[16,128,256]{2,1,0:T(8,128)(2,1)} %all-to-all-done, bf16[]{:T(256)} %constant.46.clone.1), dimensions={0}, to_apply=%region_0.1 | reduce | flops 491520 | bytes 1114114 | tf_op jit(solution)/shard_map/reduce_sum | solution.py:272
  99.0 2.0 %collective-permute-start.10 = (bf16[128,1024]{1,0:T(8,128)(2,1)S(1)}, bf16[128,1024]{1,0:T(8,128)(2,1)S(1)}, u32[]{:S(2)}, u32[]{:S(2)}) collective-permute-start(bf16[128,1024]{1,0:T(8,128)(2,1)S(1)} %get-tuple-element.87), channel_id=1, source_target_pairs={{0,4},{4,8},{8,12},{12,16},{16,20},{20,24},{24,28},{28,32},{32,36}... | collective-permute-start | bytes 786440 | tf_op jit(solution)/shard_map/ppermute | solution.py:332
  101.0 10.8 %all_to_all.10 = bf16[8,16,256]{2,1,0:T(8,128)(2,1)S(1)} all-to-all(bf16[8,16,256]{2,1,0:T(8,128)(2,1)S(1)} %bitcast.88), channel_id=1, replica_groups={{0,4,8,12,16,20,24,28},{32,36,40,44,48,52,56,60},{64,68,72,76,80,84,88,..., dimensions={0} | all-to-all | bytes 131072 | tf_op jit(solution)/shard_map/all_to_all | solution.py:276
  112.7 3.3 %collective-permute-start.11 = (bf16[128,1024]{1,0:T(8,128)(2,1)S(1)}, bf16[128,1024]{1,0:T(8,128)(2,1)S(1)}, u32[]{:S(2)}, u32[]{:S(2)}) collective-permute-start(bf16[128,1024]{1,0:T(8,128)(2,1)S(1)} %get-tuple-element.82), channel_id=1, source_target_pairs={{4,0},{8,4},{12,8},{16,12},{20,16},{24,20},{28,24},{32,28},{36,32}... | collective-permute-start | bytes 786440 | tf_op jit(solution)/shard_map/ppermute | solution.py:331
  116.0 3.9 %collective-permute-done.11 = bf16[128,1024]{1,0:T(8,128)(2,1)S(1)} collective-permute-done((bf16[128,1024]{1,0:T(8,128)(2,1)S(1)}, bf16[128,1024]{1,0:T(8,128)(2,1)S(1)}, u32[]{:S(2)}, u32[]{:S(2)}) %collective-permute-start.11) | collective-permute-done | bytes 262176 | tf_op jit(solution)/shard_map/ppermute | solution.py:331
  119.9 6.7 %collective-permute-done.12 = bf16[128,1024]{1,0:T(8,128)(2,1)S(1)} collective-permute-done((bf16[128,1024]{1,0:T(8,128)(2,1)S(1)}, bf16[128,1024]{1,0:T(8,128)(2,1)S(1)}, u32[]{:S(2)}, u32[]{:S(2)}) %collective-permute-start.12) | collective-permute-done | bytes 262176 | tf_op jit(solution)/shard_map/ppermute | solution.py:332
  (52 shorter events, 8.4 us)
Async XLA Ops:
  2.9 15.5 %collective-permute-start.1 = (bf16[128,1024]{1,0:T(8,128)(2,1)S(1)}, bf16[128,1024]{1,0:T(8,128)(2,1)S(1)}, u32[]{:S(2)}, u32[]{:S(2)}) collective-permute-start(bf16[128,1024]{1,0:T(8,128)(2,1)S(1)} %get-tuple-element.92), channel_id=1, source_target_pairs={{4,0},{8,4},{12,8},{16,12},{20,16},{24,20},{28,24},{32,28},{36,32}... | collective-permute-start | bytes 786440 | tf_op jit(solution)/shard_map/ppermute | solution.py:318
  11.3 12.0 %collective-permute-start = (bf16[128,1024]{1,0:T(8,128)(2,1)S(1)}, bf16[128,1024]{1,0:T(8,128)(2,1)S(1)}, u32[]{:S(2)}, u32[]{:S(2)}) collective-permute-start(bf16[128,1024]{1,0:T(8,128)(2,1)S(1)} %get-tuple-element.93), channel_id=1, source_target_pairs={{0,4},{4,8},{8,12},{12,16},{16,20},{20,24},{24,28},{28,32},{32,36}... | collective-permute-start | bytes 786440 | tf_op jit(solution)/shard_map/ppermute | solution.py:317
  11.3 14.0 %slice-start = ((s8[8388608]{0:T(1024)(128)(4,1)}), s8[4194304]{0:T(1024)(128)(4,1)S(1)}, s32[]{:S(2)}) async-start(s8[8388608]{0:T(1024)(128)(4,1)} %bitcast.79), calls=%async_computation.2 | async-start | bytes 8388608
  11.4 7.1 %copy-start.3 = (bf16[1,1,2,128,1024]{4,3,2,1,0:T(8,128)(2,1)S(1)}, bf16[1,1,2,128,1024]{4,3,2,1,0:T(8,128)(2,1)}, u32[]{:S(2)}) copy-start(bf16[1,1,2,128,1024]{4,3,2,1,0:T(8,128)(2,1)} %param.4) | copy-start | bytes 1572868
  11.4 14.0 %slice-start.1 = ((s8[8388608]{0:T(1024)(128)(4,1)}), s8[4194304]{0:T(1024)(128)(4,1)S(1)}, s32[]{:S(2)}) async-start(s8[8388608]{0:T(1024)(128)(4,1)} %bitcast.79), calls=%async_computation.3 | async-start | bytes 8388608
  23.2 6.9 %collective-permute-start.3 = (bf16[128,1024]{1,0:T(8,128)(2,1)S(1)}, bf16[128,1024]{1,0:T(8,128)(2,1)S(1)}, u32[]{:S(2)}, u32[]{:S(2)}) collective-permute-start(bf16[128,1024]{1,0:T(8,128)(2,1)S(1)} %broadcast_select_fusion.2.down_ref), channel_id=1, source_target_pairs={{4,0},{8,4},{12,8},{16,12},{20,16},{24,20},{28,24},{32,28},{36,32}... | collective-permute-start | bytes 786440 | tf_op jit(solution)/shard_map/ppermute | solution.py:318
  25.0 11.4 %collective-permute-start.2 = (bf16[128,1024]{1,0:T(8,128)(2,1)S(1)}, bf16[128,1024]{1,0:T(8,128)(2,1)S(1)}, u32[]{:S(2)}, u32[]{:S(2)}) collective-permute-start(bf16[128,1024]{1,0:T(8,128)(2,1)S(1)} %collective-permute-done.up_ref), channel_id=1, source_target_pairs={{0,4},{4,8},{8,12},{12,16},{16,20},{20,24},{24,28},{28,32},{32,36}... | collective-permute-start | bytes 786440 | tf_op jit(solution)/shard_map/ppermute | solution.py:317
  36.4 6.4 %collective-permute-start.5 = (bf16[128,1024]{1,0:T(8,128)(2,1)S(1)}, bf16[128,1024]{1,0:T(8,128)(2,1)S(1)}, u32[]{:S(2)}, u32[]{:S(2)}) collective-permute-start(bf16[128,1024]{1,0:T(8,128)(2,1)S(1)} %broadcast_select_fusion.1.down_ref), channel_id=1, source_target_pairs={{4,0},{8,4},{12,8},{16,12},{20,16},{24,20},{28,24},{32,28},{36,32}... | collective-permute-start | bytes 786440 | tf_op jit(solution)/shard_map/ppermute | solution.py:318
  36.8 10.7 %collective-permute-start.4 = (bf16[128,1024]{1,0:T(8,128)(2,1)S(1)}, bf16[128,1024]{1,0:T(8,128)(2,1)S(1)}, u32[]{:S(2)}, u32[]{:S(2)}) collective-permute-start(bf16[128,1024]{1,0:T(8,128)(2,1)S(1)} %collective-permute-done.2.up_ref), channel_id=1, source_target_pairs={{0,4},{4,8},{8,12},{12,16},{16,20},{20,24},{24,28},{28,32},{32,36}... | collective-permute-start | bytes 786440 | tf_op jit(solution)/shard_map/ppermute | solution.py:317
  58.5 2.0 %copy-start.2 = (bf16[1,1,2,128,1024]{4,3,2,1,0:T(8,128)(2,1)S(1)}, bf16[1,1,2,128,1024]{4,3,2,1,0:T(8,128)(2,1)}, u32[]{:S(2)}) copy-start(bf16[1,1,2,128,1024]{4,3,2,1,0:T(8,128)(2,1)} %param.7) | copy-start | bytes 1572868
  61.6 2.7 %collective-permute-start.6 = (bf16[2,1024,256]{2,1,0:T(8,128)(2,1)S(1)}, bf16[2,1024,256]{2,1,0:T(8,128)(2,1)S(1)}, u32[]{:S(2)}, u32[]{:S(2)}) collective-permute-start(bf16[2,1024,256]{2,1,0:T(8,128)(2,1)S(1)} %get-tuple-element.64), channel_id=1, source_target_pairs={{0,1},{1,0},{2,3},{3,2},{4,5},{5,4},{6,7},{7,6},{8,9},{9,8},{10,11... | collective-permute-start | bytes 3145736 | tf_op jit(solution)/shard_map/ppermute | solution.py:327
  61.8 8.8 %collective-permute-start.7 = (bf16[128,1024]{1,0:T(8,128)(2,1)S(1)}, bf16[128,1024]{1,0:T(8,128)(2,1)S(1)}, u32[]{:S(2)}, u32[]{:S(2)}) collective-permute-start(bf16[128,1024]{1,0:T(8,128)(2,1)S(1)} %get-tuple-element.90), channel_id=1, source_target_pairs={{4,0},{8,4},{12,8},{16,12},{20,16},{24,20},{28,24},{32,28},{36,32}... | collective-permute-start | bytes 786440 | tf_op jit(solution)/shard_map/ppermute | solution.py:331
  61.9 13.1 %collective-permute-start.8 = (bf16[128,1024]{1,0:T(8,128)(2,1)S(1)}, bf16[128,1024]{1,0:T(8,128)(2,1)S(1)}, u32[]{:S(2)}, u32[]{:S(2)}) collective-permute-start(bf16[128,1024]{1,0:T(8,128)(2,1)S(1)} %get-tuple-element.91), channel_id=1, source_target_pairs={{0,4},{4,8},{8,12},{12,16},{16,20},{20,24},{24,28},{28,32},{32,36}... | collective-permute-start | bytes 786440 | tf_op jit(solution)/shard_map/ppermute | solution.py:332
  76.1 20.3 %all-to-all-start = ((bf16[16,128,256]{2,1,0:T(8,128)(2,1)}), bf16[16,128,256]{2,1,0:T(8,128)(2,1)}, u32[]{:S(2)}, u32[]{:S(2)}) async-start(bf16[16,128,256]{2,1,0:T(8,128)(2,1)} %bitcast.84), calls=%async_computation | async-start | bytes 2097152 | tf_op jit(solution)/shard_map/all_to_all | solution.py:271
  81.4 3.4 %copy-start = (bf16[4096,1024]{1,0:T(8,128)(2,1)S(1)}, bf16[4096,1024]{1,0:T(8,128)(2,1)}, u32[]{:S(2)}) copy-start(bf16[4096,1024]{1,0:T(8,128)(2,1)} %wv_ref.15) | copy-start | bytes 25165828
  86.7 3.4 %copy-start.1 = (bf16[4096,1024]{1,0:T(8,128)(2,1)S(1)}, bf16[4096,1024]{1,0:T(8,128)(2,1)}, u32[]{:S(2)}) copy-start(bf16[4096,1024]{1,0:T(8,128)(2,1)} %wv_ref.15) | copy-start | bytes 25165828
  92.6 19.8 %copy-start.4 = (bf16[2,128,1024]{2,1,0:T(8,128)(2,1)S(1)}, bf16[2,128,1024]{2,1,0:T(8,128)(2,1)}, u32[]{:S(2)}) copy-start(bf16[2,128,1024]{2,1,0:T(8,128)(2,1)} %pad_maximum_fusion) | copy-start | bytes 1572868
  98.9 13.5 %collective-permute-start.9 = (bf16[128,1024]{1,0:T(8,128)(2,1)S(1)}, bf16[128,1024]{1,0:T(8,128)(2,1)S(1)}, u32[]{:S(2)}, u32[]{:S(2)}) collective-permute-start(bf16[128,1024]{1,0:T(8,128)(2,1)S(1)} %get-tuple-element.86), channel_id=1, source_target_pairs={{4,0},{8,4},{12,8},{16,12},{20,16},{24,20},{28,24},{32,28},{36,32}... | collective-permute-start | bytes 786440 | tf_op jit(solution)/shard_map/ppermute | solution.py:331
  99.0 13.4 %collective-permute-start.10 = (bf16[128,1024]{1,0:T(8,128)(2,1)S(1)}, bf16[128,1024]{1,0:T(8,128)(2,1)S(1)}, u32[]{:S(2)}, u32[]{:S(2)}) collective-permute-start(bf16[128,1024]{1,0:T(8,128)(2,1)S(1)} %get-tuple-element.87), channel_id=1, source_target_pairs={{0,4},{4,8},{8,12},{12,16},{16,20},{20,24},{24,28},{28,32},{32,36}... | collective-permute-start | bytes 786440 | tf_op jit(solution)/shard_map/ppermute | solution.py:332
  112.7 7.2 %collective-permute-start.11 = (bf16[128,1024]{1,0:T(8,128)(2,1)S(1)}, bf16[128,1024]{1,0:T(8,128)(2,1)S(1)}, u32[]{:S(2)}, u32[]{:S(2)}) collective-permute-start(bf16[128,1024]{1,0:T(8,128)(2,1)S(1)} %get-tuple-element.82), channel_id=1, source_target_pairs={{4,0},{8,4},{12,8},{16,12},{20,16},{24,20},{28,24},{32,28},{36,32}... | collective-permute-start | bytes 786440 | tf_op jit(solution)/shard_map/ppermute | solution.py:331
  116.0 10.6 %collective-permute-start.12 = (bf16[128,1024]{1,0:T(8,128)(2,1)S(1)}, bf16[128,1024]{1,0:T(8,128)(2,1)S(1)}, u32[]{:S(2)}, u32[]{:S(2)}) collective-permute-start(bf16[128,1024]{1,0:T(8,128)(2,1)S(1)} %get-tuple-element.83), channel_id=1, source_target_pairs={{0,4},{4,8},{8,12},{12,16},{16,20},{20,24},{24,28},{28,32},{32,36}... | collective-permute-start | bytes 786440 | tf_op jit(solution)/shard_map/ppermute | solution.py:332

commit v4 on v3

v4 whole, which is shorter than its diff:
```python
import jax
import jax.numpy as jnp
import numpy as np
from jax import lax
from jax.experimental import pallas as pl
from jax.experimental.pallas import tpu as pltpu
from jax.sharding import PartitionSpec as P

HEADS = 16
HEAD_DIM = 64
WIN = 4
BLOCK = 128
D = 1024
PAIR = 2 * HEAD_DIM
PAIRS_A_STEP = 4
TILE = 256
BF = jnp.bfloat16
F32 = jnp.float32

BARRED = -1e30
FREE = 3e38
SCALE = HEAD_DIM**-0.5
EXP2_SCALE = float(SCALE * np.log2(np.e))

NN = (((1,), (0,)), ((), ()))
NT = (((1,), (1,)), ((), ()))


def mm(a, b, dims=NN):
    return lax.dot_general(a, b, dims, preferred_element_type=F32)


def params(mib):
    return pltpu.CompilerParams(vmem_limit_bytes=mib * 2**20)


def cost(flops, moved, exps=0):
    return pl.CostEstimate(flops=flops, bytes_accessed=moved, transcendentals=exps)


def in_hbm(*arrays):
    return [pltpu.with_memory_space_constraint(a, pltpu.HBM) for a in arrays]


def in_vmem(*arrays):
    return [pltpu.with_memory_space_constraint(a, pltpu.VMEM) for a in arrays]


def weight_cols(which):
    return pl.BlockSpec((D, TILE), lambda t: (which, t))


def weight_rows(which):
    return pl.BlockSpec((TILE, D), lambda t: (which * (D // TILE) + t, 0))


def whole(shape):
    return pl.BlockSpec(shape, lambda t: (0,) * len(shape))


def own_kernel(x_ref, wk_ref, wv_ref, kv_ref, wk_out, wv_out):
    wk_out[...] = wk_ref[...]
    wv_out[...] = wv_ref[...]
    x = x_ref[...].reshape(2 * BLOCK, D)
    kv_ref[0] = mm(x, wk_ref[...]).astype(BF).reshape(2, BLOCK, TILE)
    kv_ref[1] = mm(x, wv_ref[...]).astype(BF).reshape(2, BLOCK, TILE)


def own_projections(x, weights):
    return pl.pallas_call(
        own_kernel,
        grid=(D // TILE,),
        in_specs=[whole((2, BLOCK, D)), weight_cols(1), weight_cols(2)],
        out_specs=[pl.BlockSpec((2, 2, BLOCK, TILE), lambda t: (0, 0, 0, t))] + [weight_cols(0)] * 2,
        out_shape=[jax.ShapeDtypeStruct((2, 2, BLOCK, D), BF)] + [jax.ShapeDtypeStruct((D, D), BF)] * 2,
        compiler_params=params(12),
        cost_estimate=cost(8 * 2 * BLOCK * D * D, 12 * D * D + 12 * BLOCK * D),
        name="own_projections",
    )(*in_hbm(x, weights, weights))


def query_kernel(x_ref, g_ref, wq_ref, wo_ref, q_ref, da_ref, wq_out):
    wq_out[...] = wq_ref[...]
    x = x_ref[...].reshape(2 * BLOCK, D)
    g = g_ref[...].reshape(2 * BLOCK, D)
    q_ref[...] = mm(x, wq_ref[...]).astype(BF).reshape(2, BLOCK, TILE)
    da_ref[...] = mm(g, wo_ref[...], NT).astype(BF).reshape(2, BLOCK, TILE)


def query_projections(x, g, weights):
    rows = jax.ShapeDtypeStruct((2, BLOCK, D), BF)
    row_tile = pl.BlockSpec((2, BLOCK, TILE), lambda t: (0, 0, t))
    return pl.pallas_call(
        query_kernel,
        grid=(D // TILE,),
        in_specs=[whole((2, BLOCK, D)), whole((2, BLOCK, D)), weight_cols(0), weight_rows(3)],
        out_specs=[row_tile, row_tile, weight_cols(0)],
        out_shape=[rows, rows, jax.ShapeDtypeStruct((D, D), BF)],
        compiler_params=params(12),
        cost_estimate=cost(8 * 2 * BLOCK * D * D, 12 * D * D + 12 * BLOCK * D),
        name="query_projections",
    )(*in_hbm(x, g, weights, weights))


def halo_kernel(up_ref, down_ref, wk_ref, wv_ref, kv_ref):
    x = jnp.concatenate([up_ref[...], down_ref[...]], axis=0)
    kv_ref[0] = mm(x, wk_ref[...]).astype(BF).reshape(2, BLOCK, TILE)
    kv_ref[1] = mm(x, wv_ref[...]).astype(BF).reshape(2, BLOCK, TILE)


def halo_projections(up, down, wk, wv):
    return pl.pallas_call(
        halo_kernel,
        grid=(D // TILE,),
        in_specs=[whole((BLOCK, D)), whole((BLOCK, D)), weight_cols(0), weight_cols(0)],
        out_specs=pl.BlockSpec((2, 2, BLOCK, TILE), lambda t: (0, 0, 0, t)),
        out_shape=jax.ShapeDtypeStruct((2, 2, BLOCK, D), BF),
        compiler_params=params(10),
        cost_estimate=cost(4 * 2 * BLOCK * D * D, 4 * D * D + 12 * BLOCK * D),
        name="halo_projections",
    )(up, down, *in_vmem(wk, wv))


def attention_kernel(
    place, valid_ref, q_ref, da_ref, kv3_ref, kv2_ref, kv1_ref, kv0_ref,
    out_ref, dq_ref, d3_ref, d2_ref, d1_ref, d0_ref,
):
    first = lax.broadcasted_iota(jnp.int32, (BLOCK, PAIR), 1) < HEAD_DIM
    kv_refs = (kv3_ref, kv2_ref, kv1_ref, kv0_ref)
    d_refs = (d3_ref, d2_ref, d1_ref, d0_ref)
    lanes = [slice(i * PAIR, (i + 1) * PAIR) for i in range(PAIRS_A_STEP)]

    def split(rows):
        zero = jnp.zeros_like(rows)
        return jnp.concatenate([jnp.where(first, rows, zero), jnp.where(first, zero, rows)], axis=0)

    def merge(rows):
        return jnp.where(first, rows[:BLOCK], rows[BLOCK:])

    def twice(rows):
        return jnp.concatenate([rows, rows], axis=0)

    block = jnp.where(pl.program_id(0) == 0, place[0], 127 - place[0])
    limits = []
    for back in range(WIN - 1, -1, -1):
        key_block = block - back
        slot = jnp.maximum(jnp.where(key_block < 64, key_block, 127 - key_block), 0)
        halves = valid_ref[pl.ds(slot, 1)].reshape(2, BLOCK)
        serves = jnp.where(key_block < 64, halves[:1], halves[1:])
        limit = jnp.where((serves == 1) & (key_block >= 0), FREE, BARRED)
        limits.append(jnp.broadcast_to(limit, (BLOCK, BLOCK)))
    row = lax.broadcasted_iota(jnp.int32, (BLOCK, BLOCK), 0)
    column = lax.broadcasted_iota(jnp.int32, (BLOCK, BLOCK), 1)
    limits[-1] = jnp.where(row == column, FREE, jnp.where(row > column, limits[-1], BARRED))
    bias = twice(jnp.concatenate(limits, axis=1))
    ones = jnp.ones((WIN * BLOCK, PAIR), BF)
    keys = [jnp.concatenate([ref[0, 0, :, c] for ref in kv_refs], axis=0) for c in lanes]
    values = [jnp.concatenate([ref[1, 0, :, c] for ref in kv_refs], axis=0) for c in lanes]
    queries = [split(q_ref[0, :, c]) for c in lanes]
    d_attn = [split(da_ref[0, :, c]) for c in lanes]
    scores = [jnp.minimum(mm(q, k, NT), bias) for q, k in zip(queries, keys)]
    tops = [jnp.max(s, axis=1, keepdims=True) for s in scores]
    terms = [jnp.exp2((s - t) * EXP2_SCALE).astype(BF) for s, t in zip(scores, tops)]
    sums = [mm(t, jnp.concatenate([v, ones], axis=1)) for t, v in zip(terms, values)]
    shares = [1.0 / s[:, PAIR:] for s in sums]
    outs = [merge(s[:, :PAIR] * r).astype(BF) for s, r in zip(sums, shares)]
    for c, o in zip(lanes, outs):
        out_ref[0, :, c] = o
    scaled = [d.astype(F32) * r for d, r in zip(d_attn, shares)]
    deltas = [
        jnp.sum(d * twice(o.astype(F32)), axis=1, keepdims=True) for d, o in zip(scaled, outs)
    ]
    scaled = [d.astype(BF) for d in scaled]
    d_probs = [mm(d, v, NT) for d, v in zip(scaled, values)]
    d_scores = [(p - d).astype(BF) * t for p, d, t in zip(d_probs, deltas, terms)]
    d_values = [mm(d.T, t).astype(BF).T for d, t in zip(scaled, terms)]
    d_queries = [merge(mm(d, k)) for d, k in zip(d_scores, keys)]
    for c, d in zip(lanes, d_queries):
        dq_ref[0, :, c] = (d * SCALE).astype(BF)
    d_keys = [(mm(q.T, d) * SCALE).astype(BF).T for q, d in zip(queries, d_scores)]
    for c, dk, dv in zip(lanes, d_keys, d_values):
        for i, ref in enumerate(d_refs):
            ref[0, 0, :, c] = dk[i * BLOCK : (i + 1) * BLOCK]
            ref[1, 0, :, c] = dv[i * BLOCK : (i + 1) * BLOCK]


def attention(place, key_valid, q, da, kvs):
    rows = jax.ShapeDtypeStruct((2, BLOCK, D), BF)
    pairs = jax.ShapeDtypeStruct((2, 2, BLOCK, D), BF)
    width = PAIRS_A_STEP * PAIR
    row_spec = pl.BlockSpec((1, BLOCK, width), lambda h, p, s: (h, 0, p))
    pair_spec = pl.BlockSpec((2, 1, BLOCK, width), lambda h, p, s: (0, h, 0, p))
    valid_spec = pl.BlockSpec((64, 2, BLOCK), lambda h, p, s: (0, 0, 0))
    return pl.pallas_call(
        attention_kernel,
        grid_spec=pltpu.PrefetchScalarGridSpec(
            num_scalar_prefetch=1,
            grid=(2, D // width),
            in_specs=[valid_spec, row_spec, row_spec] + [pair_spec] * 4,
            out_specs=[row_spec, row_spec] + [pair_spec] * 4,
        ),
        out_shape=[rows, rows] + [pairs] * 4,
        compiler_params=params(24),
        cost_estimate=cost(2 * 10 * BLOCK * WIN * BLOCK * D * 2, 12 * 2**20, 2**21),
        name="attention",
    )(place, key_valid, *in_vmem(q, da, *kvs))


def back_kernel(d_ref, wk_ref, wv_ref, first_ref, second_ref):
    rows = mm(d_ref[0].reshape(2 * BLOCK, D), wk_ref[...], NT)
    rows += mm(d_ref[1].reshape(2 * BLOCK, D), wv_ref[...], NT)
    first_ref[...] = rows[:BLOCK].astype(BF)
    second_ref[...] = rows[BLOCK:].astype(BF)


def back_projections(d, wk, wv):
    return pl.pallas_call(
        back_kernel,
        grid=(D // TILE,),
        in_specs=[whole((2, 2, BLOCK, D)), weight_rows(0), weight_rows(0)],
        out_specs=[pl.BlockSpec((BLOCK, TILE), lambda t: (0, t))] * 2,
        out_shape=[jax.ShapeDtypeStruct((BLOCK, D), BF)] * 2,
        compiler_params=params(10),
        cost_estimate=cost(4 * 2 * BLOCK * D * D, 4 * D * D + 12 * BLOCK * D),
        name="back_projections",
    )(*in_vmem(d, wk, wv))


def last_kernel(d_ref, dq_ref, wq_ref, wk_ref, wv_ref, first_ref, second_ref):
    rows = mm(dq_ref[...].reshape(2 * BLOCK, D), wq_ref[...], NT)
    rows += mm(d_ref[0].reshape(2 * BLOCK, D), wk_ref[...], NT)
    rows += mm(d_ref[1].reshape(2 * BLOCK, D), wv_ref[...], NT)
    first_ref[...] = rows[:BLOCK]
    second_ref[...] = rows[BLOCK:]


def last_projections(d, dq, wq, wk, wv):
    return pl.pallas_call(
        last_kernel,
        grid=(D // TILE,),
        in_specs=[
            whole((2, 2, BLOCK, D)),
            whole((2, BLOCK, D)),
            weight_rows(0),
            weight_rows(0),
            weight_rows(0),
        ],
        out_specs=[pl.BlockSpec((BLOCK, TILE), lambda t: (0, t))] * 2,
        out_shape=[jax.ShapeDtypeStruct((BLOCK, D), F32)] * 2,
        compiler_params=params(12),
        cost_estimate=cost(6 * 2 * BLOCK * D * D, 6 * D * D + 16 * BLOCK * D),
        name="last_projections",
    )(*in_vmem(d, dq, wq, wk, wv))


def outer_kernel(core_ref, o_ref, keep_ref, send_ref, kept_ref, sent_ref):
    o_t = o_ref[...].reshape(2 * BLOCK, D).T
    for g_ref, r_ref in ((send_ref, sent_ref), (keep_ref, kept_ref)):
        r_ref[0] = mm(o_t, g_ref[...].reshape(2 * BLOCK, TILE)).astype(BF)


def outer_products(o, g, core):
    result = jax.ShapeDtypeStruct((2, D, TILE), BF)
    result_spec = pl.BlockSpec((1, D, TILE), lambda y, c: (y, 0, 0))
    return pl.pallas_call(
        outer_kernel,
        grid_spec=pltpu.PrefetchScalarGridSpec(
            num_scalar_prefetch=1,
            grid=(2,),
            in_specs=[
                pl.BlockSpec((2, BLOCK, D), lambda y, c: (0, 0, 0)),
                pl.BlockSpec((2, BLOCK, TILE), lambda y, c: (0, 0, 2 * y + c[0])),
                pl.BlockSpec((2, BLOCK, TILE), lambda y, c: (0, 0, 2 * y + 1 - c[0])),
            ],
            out_specs=[result_spec, result_spec],
        ),
        out_shape=[result, result],
        compiler_params=params(12),
        cost_estimate=cost(4 * BLOCK * D * D, 2 * D * D + 8 * BLOCK * D),
        name="outer_products",
    )(core, *in_vmem(o, g, g))


def hop_kernel(place_ref, t0_ref, t1_ref, after_ref, before_ref, state_ref, out_ref):
    blk = place_ref[0]
    folded = jnp.where(blk == 63, state_ref[...].astype(F32), 0.0)
    before = jnp.where(blk == 0, 0.0, before_ref[...].astype(F32))
    first = t0_ref[...].astype(F32) + after_ref[...].astype(F32) + folded
    out_ref[0] = first.astype(BF)
    out_ref[1] = (t1_ref[...].astype(F32) + before).astype(BF)


def inner_hop_kernel(place_ref, t0_ref, t1_ref, after_ref, before_ref, state_ref, first_ref, second_ref):
    blk = place_ref[0]
    folded = jnp.where(blk == 63, state_ref[...].astype(F32), 0.0)
    before = jnp.where(blk == 0, 0.0, before_ref[...].astype(F32))
    first = t0_ref[...].astype(F32) + after_ref[...].astype(F32) + folded
    first_ref[...] = first.astype(BF)
    second_ref[...] = (t1_ref[...].astype(F32) + before).astype(BF)


def hop_back(place, terms, after, before, state, last):
    spec = pl.BlockSpec((BLOCK, D // 2), lambda t, p: (0, t))
    if last:
        out_specs = pl.BlockSpec((2, BLOCK, D // 2), lambda t, p: (0, 0, t))
        out_shape = jax.ShapeDtypeStruct((2, BLOCK, D), BF)
    else:
        out_specs = [spec] * 2
        out_shape = [jax.ShapeDtypeStruct((BLOCK, D), BF)] * 2
    return pl.pallas_call(
        hop_kernel if last else inner_hop_kernel,
        grid_spec=pltpu.PrefetchScalarGridSpec(
            num_scalar_prefetch=1, grid=(2,), in_specs=[spec] * 5, out_specs=out_specs
        ),
        out_shape=out_shape,
        compiler_params=params(6),
        cost_estimate=cost(8 * BLOCK * D, 14 * BLOCK * D),
        name="hop_back",
    )(place, *in_vmem(*terms, after, before, state))


def chip(y, x, z, core):
    return ((y % 2) * 32 + x * 8 + z) * 4 + (y // 2) * 2 + core


CORE_PAIRS = [(i, i ^ 1) for i in range(4)]
LINES = [[32 * y + 8 * x + z for z in range(8)] for y in range(2) for x in range(4)]
FLIP = ((1, 0, 3, 2), (3, 2, 1, 0))


def halving_pairs(second, turn):
    pairs = []
    for y in range(4):
        for x in range(4):
            for z in range(8):
                for core in range(2):
                    along_x = (core == 0) != second
                    to = (y, FLIP[turn][x]) if along_x else (FLIP[turn][y], x)
                    pairs.append((chip(y, x, z, core), chip(*to, z, core)))
    return pairs


SHARE = 128


def places(position, shot):
    def ring(i):
        outer = (i == 0) | (i == 3)
        keep = [jnp.where(outer, 0, 1), jnp.where(outer, 3, 2)]
        send = [jnp.where(outer, 1, 0), jnp.where(outer, 2, 3)]
        return keep + send + [i // 2, 1 - i // 2]

    core = shot % 2
    x = (position // 8) % 4
    y = (shot // 2) * 2 + position // 32
    first, second = jnp.where(core == 0, x, y), jnp.where(core == 0, y, x)
    return jnp.stack([position, core] + ring(first) + ring(second)).astype(jnp.int32)


FIRST, SECOND = 2, 8


def total(a, b):
    return (a.astype(F32) + b.astype(F32)).astype(BF)


def split_core(place, kept_ref, other_ref, keep_ref, send_ref):
    for out_ref, at in ((keep_ref, FIRST), (send_ref, FIRST + 2)):
        for i in range(2):
            for j in range(4):
                first = place[at + i]
                y = pl.ds(jnp.where(place[1] == 0, j, first), 1)
                x = pl.ds(jnp.where(place[1] == 0, first, j), 1)
                out_ref[i : i + 1, j : j + 1] = total(kept_ref[y, x], other_ref[y, x])


def split_first(place, kept_ref, moved_ref, keep_ref, send_ref):
    for j, out_ref in enumerate((keep_ref, send_ref)):
        i = pl.ds(place[FIRST + 4 + j], 1)
        out_ref[...] = total(kept_ref[i], moved_ref[i])


def split_second(place, kept_ref, moved_ref, keep_ref, send_ref):
    for out_ref, at in ((keep_ref, SECOND), (send_ref, SECOND + 2)):
        for j in range(2):
            i = pl.ds(place[at + j], 1)
            out_ref[:, j : j + 1] = total(kept_ref[:, i], moved_ref[:, i])


def split_third(place, kept_ref, moved_ref, keep_ref, send_ref):
    for j, out_ref in enumerate((keep_ref, send_ref)):
        i = pl.ds(place[SECOND + 4 + j], 1)
        out_ref[...] = total(kept_ref[:, i], moved_ref[:, i])


def join_last(place, kept_ref, moved_ref, out_ref):
    out_ref[...] = total(kept_ref[...], moved_ref[...])


def halving(kernel, place, arrays, shapes):
    vmem = pl.BlockSpec(memory_space=pltpu.VMEM)
    return pl.pallas_call(
        kernel,
        in_specs=[pl.BlockSpec(memory_space=pltpu.SMEM)] + [vmem] * len(arrays),
        out_specs=[vmem] * len(shapes),
        out_shape=[jax.ShapeDtypeStruct(shape + (SHARE, TILE), BF) for shape in shapes],
        compiler_params=params(8),
        cost_estimate=cost(2**20, 2**20),
        name=kernel.__name__,
    )(place, *arrays)


def halve_core(place, kept, other):
    arrays = [v.reshape(4, 4, SHARE, TILE) for v in (kept, other)]
    return halving(split_core, place, arrays, [(2, 4)] * 2)


HALVINGS = (
    (split_first, halving_pairs(False, 0), [(1, 4)] * 2),
    (split_second, halving_pairs(False, 1), [(1, 2)] * 2),
    (split_third, halving_pairs(True, 0), [(1, 1)] * 2),
    (join_last, halving_pairs(True, 1), [(1, 1)]),
)


def halve(turn, place, pieces):
    kernel, pairs, shapes = HALVINGS[turn]
    keep, send = pieces
    return halving(kernel, place, [keep, lax.ppermute(send, ("blk", "dp"), pairs)], shapes)


def sum_over_line(total):
    total = lax.all_to_all(total.reshape(8, 16, TILE), "blk", 0, 0, axis_index_groups=LINES)
    return jnp.sum(total.astype(F32), axis=0)


def per_device(tokens, key_valid, weights, out_grad):
    position = lax.axis_index("blk")
    shot = lax.axis_index("dp")
    up = [(i, (i + 1) % 64) for i in range(64)]
    down = [(t, s) for s, t in up]
    x = tokens.reshape(2, BLOCK, D)
    g = out_grad.reshape(2, BLOCK, D)

    core = (shot % 2).reshape(1)
    place = places(position, shot)
    at_last = position == 63
    own, core, place, at_last = lax.optimization_barrier((x, core, place, at_last))
    kv0, wk, wv = own_projections(own, weights)
    kvs = [kv0]
    state_up, state_down = x[0], x[1]
    for hop_index in range(WIN - 1):
        new_up = lax.ppermute(state_up, "blk", up)
        new_down = lax.ppermute(state_down, "blk", down)
        if hop_index == 1:
            q, da, wq, kvs[-1] = lax.optimization_barrier((*query_projections(own, g, weights), kvs[-1]))
            new_up, new_down, q = lax.optimization_barrier((new_up, new_down, q))
        new_up, new_down, kvs[-1] = lax.optimization_barrier((new_up, new_down, kvs[-1]))
        new_down = jnp.where(at_last, state_up, new_down)
        kvs.append(halo_projections(new_up, new_down, wk, wv))
        state_up, state_down = new_up, new_down
    o, dq, d3, d2, d1, d0 = attention(place, key_valid.reshape(64, 2, BLOCK), q, da, kvs[::-1])

    def hop(state):
        return lax.ppermute(state[0], "blk", down), lax.ppermute(state[1], "blk", up)

    kept, sent = outer_products(o, g, core)
    other = lax.ppermute(sent, "dp", CORE_PAIRS)
    d2, _ = lax.optimization_barrier((d2, sent))
    terms = back_projections(d2, wk, wv)
    kept, other, terms = lax.optimization_barrier((kept, other, terms))
    pieces = halve_core(place, kept, other)
    d3, pieces = lax.optimization_barrier((d3, pieces))
    state = back_projections(d3, wk, wv)

    moved = hop(state)
    d1, state = lax.optimization_barrier((d1, state))
    later = back_projections(d1, wk, wv)
    pieces = halve(0, place, pieces)
    moved, pieces, later = lax.optimization_barrier((moved, pieces, later))
    state = hop_back(place, terms, *moved, state[1], False)

    moved = hop(state)
    d0, state = lax.optimization_barrier((d0, state))
    last = last_projections(d0, dq, wq, wk, wv)
    pieces = halve(2, place, halve(1, place, pieces))
    moved, pieces, last = lax.optimization_barrier((moved, pieces, last))
    state = hop_back(place, later, *moved, state[1], False)

    moved = hop(state)
    (plane_sum,) = halve(3, place, pieces)
    moved, plane_sum = lax.optimization_barrier((moved, plane_sum))
    grad_tokens = hop_back(place, last, *moved, state[1], True)
    w_grad = sum_over_line(plane_sum)
    return grad_tokens.reshape(tokens.shape), w_grad


def solution(mesh):
    placed = (
        P("dp", "blk", None, None, None),
        P("dp", None, None, None),
        P(),
        P("dp", "blk", None, None, None),
    )
    return jax.shard_map(
        per_device,
        mesh=mesh,
        in_specs=placed,
        out_specs=(P("dp", "blk", None, None, None), P("blk", "dp")),
        check_vma=False,
    )
```

time: 129 us -> 123 us (0.953)
  waiting for transfers between devices: 42 us -> 54.6 us
  blocking collectives: 10.8 us -> 0 us
  Pallas kernels: 32.5 us -> 42.4 us
  local copies, waits for them, and re-layouts: 10 us -> 1.17 us
  other arithmetic: 6.16 us -> 0.72 us
  starting transfers between devices: 25.2 us -> 22.8 us
    pallas_call x1 -> x10, Pallas kernels: 8.56 us -> 20.8 us  [the longest x1 9.01 us: attention(): pl.pallas_call(attention_kernel, grid_spec=pltpu.PrefetchScalarGridSpec(n...]
    all_to_all x1 -> x0, blocking collectives: 10.8 us -> none  [sum_over_line(): total = lax.all_to_all(total, 'blk', 0, 0, axis_index_groups=LINES)]
    ppermute x10 -> x14, waiting for transfers between devices: 22.6 us -> 32.8 us  [the longest x4 21 us: halve(): lax.ppermute(send, ('blk', 'dp'), pairs)]
    unnamed x14 -> x6, local copies, waits for them, and re-layouts: 6.79 us -> 0.02 us
    all_to_all x1, waiting for transfers between devices: 3.8 us -> 6.71 us  [sum_over_line(): lax.all_to_all(total.reshape(8, 16, TILE), 'blk', 0, 0, axis_index_groups...]
    another operation x8 -> x0, other arithmetic: 2.5 us -> none  [the longest x6 2.41 us: per_device(): jnp.stack([term[0].astype(F32) + from_after.astype(F32) + extra, term[1]....]
    pallas_call x1, Pallas kernels: 7.08 us -> 4.75 us  [own_projections(): pl.pallas_call(own_kernel, grid=(D // TILE,), in_specs=[whole((2, BLOCK,...]
    all_to_all x1, starting transfers between devices: 5.25 us -> 3.35 us  [sum_over_line(): lax.all_to_all(total.reshape(8, 16, TILE), 'blk', 0, 0, axis_index_groups...]
  transfers between devices with their start and end apart: 14 -> 18, of which waited for: 11 -> 14; matrix products, arithmetic and copies ran while one was open for 2% -> 0% of each run, Pallas kernels for 14% -> 23%
where the time goes in v4:
time: 123 us
  waiting for transfers between devices  54.6 us (44%)
  Pallas kernels  42.4 us (34%)
  starting transfers between devices  22.8 us (19%)
    ppermute x4, waiting for transfers between devices, halve(): lax.ppermute(send, ('blk', 'dp'), pairs)  21 us
    ppermute x3, waiting for transfers between devices, per_device(): new_up = lax.ppermute(state_up, 'blk', up)  15.2 us
    ppermute x3, starting transfers between devices, per_device(): new_down = lax.ppermute(state_down, 'blk', down)  10.9 us
    pallas_call x1, Pallas kernels, attention(): pl.pallas_call(attention_kernel, grid_spec=pltpu.PrefetchScalarGridSpec(n...  9.01 us
    pallas_call x3, Pallas kernels, halo_projections(): pl.pallas_call(halo_kernel, grid=(D // TILE,), in_specs=[whole((BLOCK, D)...  7.27 us
    ppermute x3, waiting for transfers between devices, hop(): lax.ppermute(state[1], 'blk', up)  7.19 us
    all_to_all x1, waiting for transfers between devices, sum_over_line(): lax.all_to_all(total.reshape(8, 16, TILE), 'blk', 0, 0, axis_index_groups...  6.71 us
    pallas_call x3, Pallas kernels, back_projections(): pl.pallas_call(back_kernel, grid=(D // TILE,), in_specs=[whole((2, 2, BLO...  5.93 us
  transfers between devices with their start and end apart: 18, of which 14 were waited for; matrix products, arithmetic and copies ran while one was open for 0% of the time, Pallas kernels for 23%

profile of v4, /device:TPU:24, one launch (start us, length us, event | category | flops | bytes accessed | tf_op | source)
XLA Modules:
  0.0 122.6 jit_solution(3462907185831473126)
XLA Ops:
  1.7 8.3 %collective-permute-start.1 = (bf16[128,1024]{1,0:T(8,128)(2,1)S(1)}, bf16[128,1024]{1,0:T(8,128)(2,1)S(1)}, u32[]{:S(2)}, u32[]{:S(2)}) collective-permute-start(bf16[128,1024]{1,0:T(8,128)(2,1)S(1)} %get-tuple-element.164), channel_id=1, source_target_pairs={{4,0},{8,4},{12,8},{16,12},{20,16},{24,20},{28,24},{32,28},{36,32}... | collective-permute-start | bytes 786440 | tf_op jit(solution)/shard_map/ppermute | solution.py:454
  10.1 4.8 %own_projections.1 = (bf16[2,2,128,1024]{3,2,1,0:T(8,128)(2,1)S(1)}, bf16[1024,1024]{1,0:T(8,128)(2,1)S(1)}, bf16[1024,1024]{1,0:T(8,128)(2,1)S(1)}) custom-call(bf16[2,128,1024]{2,1,0:T(8,128)(2,1)} %bitcast.33, bf16[4096,1024]{1,0:T(8,128)(2,1)} %wo_ref.1, bf16[4096,1024]{1,0:T(8,128)(2,1)} %wo_ref.1), custom_call_target="tpu_custom_call" | custom-call | flops 2147483648 | bytes 14155776 | tf_op jit(solution)/shard_map/own_projections/pallas_call | solution.py:70
  15.6 6.4 %collective-permute-done.up_ref = bf16[128,1024]{1,0:T(8,128)(2,1)S(1)} collective-permute-done((bf16[128,1024]{1,0:T(8,128)(2,1)S(1)}, bf16[128,1024]{1,0:T(8,128)(2,1)S(1)}, u32[]{:S(2)}, u32[]{:S(2)}) %collective-permute-start) | collective-permute-done | bytes 262176 | tf_op jit(solution)/shard_map/ppermute | solution.py:453
  22.4 1.7 %collective-permute-start.2 = (bf16[128,1024]{1,0:T(8,128)(2,1)S(1)}, bf16[128,1024]{1,0:T(8,128)(2,1)S(1)}, u32[]{:S(2)}, u32[]{:S(2)}) collective-permute-start(bf16[128,1024]{1,0:T(8,128)(2,1)S(1)} %collective-permute-done.up_ref), channel_id=1, source_target_pairs={{0,4},{4,8},{8,12},{12,16},{16,20},{20,24},{24,28},{28,32},{32,36}... | collective-permute-start | bytes 786440 | tf_op jit(solution)/shard_map/ppermute | solution.py:453
  24.1 4.6 %query_projections.1 = (bf16[2,128,1024]{2,1,0:T(8,128)(2,1)S(1)}, bf16[2,128,1024]{2,1,0:T(8,128)(2,1)S(1)}, bf16[1024,1024]{1,0:T(8,128)(2,1)S(1)}) custom-call(bf16[2,128,1024]{2,1,0:T(8,128)(2,1)} %bitcast.34, bf16[2,128,1024]{2,1,0:T(8,128)(2,1)} %bitcast.29, bf16[4096,1024]{1,0:T(8,128)(2,1)} %wo_ref.1, bf16[4096,1024]{1,0:T(8,128)(2,1)} %wo_ref.1), custom_call_target="tpu_custom_call" | custom-call | flops 2147483648 | bytes 14155776 | tf_op jit(solution)/shard_map/query_projections/pallas_call | solution.py:93
  28.7 2.4 %halo_projections.3.kv1_ref = bf16[2,2,128,1024]{3,2,1,0:T(8,128)(2,1)S(1)} custom-call(bf16[128,1024]{1,0:T(8,128)(2,1)S(1)} %collective-permute-done.up_ref, bf16[128,1024]{1,0:T(8,128)(2,1)S(1)} %broadcast_select_fusion.2.down_ref, bf16[1024,1024]{1,0:T(8,128)(2,1)S(1)} %get-tuple-element.93.wk_ref, bf16[1024,1024]{1,0:T(8,128)(2,1)S(1)} %get-tuple-element.94.wv_ref), custom_call_target="tpu_custom_call" | custom-call | flops 1073741824 | bytes 5767168 | tf_op jit(solution)/shard_map/halo_projections/pallas_call | solution.py:112
  31.2 2.3 %collective-permute-done.2.up_ref = bf16[128,1024]{1,0:T(8,128)(2,1)S(1)} collective-permute-done((bf16[128,1024]{1,0:T(8,128)(2,1)S(1)}, bf16[128,1024]{1,0:T(8,128)(2,1)S(1)}, u32[]{:S(2)}, u32[]{:S(2)}) %collective-permute-start.2) | collective-permute-done | bytes 262176 | tf_op jit(solution)/shard_map/ppermute | solution.py:453
  33.5 2.2 %collective-permute-start.5 = (bf16[128,1024]{1,0:T(8,128)(2,1)S(1)}, bf16[128,1024]{1,0:T(8,128)(2,1)S(1)}, u32[]{:S(2)}, u32[]{:S(2)}) collective-permute-start(bf16[128,1024]{1,0:T(8,128)(2,1)S(1)} %broadcast_select_fusion.1.down_ref), channel_id=1, source_target_pairs={{4,0},{8,4},{12,8},{16,12},{20,16},{24,20},{28,24},{32,28},{36,32}... | collective-permute-start | bytes 786440 | tf_op jit(solution)/shard_map/ppermute | solution.py:454
  35.8 2.4 %halo_projections.4.kv2_ref = bf16[2,2,128,1024]{3,2,1,0:T(8,128)(2,1)S(1)} custom-call(bf16[128,1024]{1,0:T(8,128)(2,1)S(1)} %collective-permute-done.2.up_ref, bf16[128,1024]{1,0:T(8,128)(2,1)S(1)} %broadcast_select_fusion.1.down_ref, bf16[1024,1024]{1,0:T(8,128)(2,1)S(1)} %get-tuple-element.93.wk_ref, bf16[1024,1024]{1,0:T(8,128)(2,1)S(1)} %get-tuple-element.94.wv_ref), custom_call_target="tpu_custom_call" | custom-call | flops 1073741824 | bytes 5767168 | tf_op jit(solution)/shard_map/halo_projections/pallas_call | solution.py:112
  38.2 1.8 %collective-permute-done.5 = bf16[128,1024]{1,0:T(8,128)(2,1)S(1)} collective-permute-done((bf16[128,1024]{1,0:T(8,128)(2,1)S(1)}, bf16[128,1024]{1,0:T(8,128)(2,1)S(1)}, u32[]{:S(2)}, u32[]{:S(2)}) %collective-permute-start.5) | collective-permute-done | bytes 262176 | tf_op jit(solution)/shard_map/ppermute | solution.py:454
  40.0 6.4 %collective-permute-done.4.up_ref = bf16[128,1024]{1,0:T(8,128)(2,1)S(1)} collective-permute-done((bf16[128,1024]{1,0:T(8,128)(2,1)S(1)}, bf16[128,1024]{1,0:T(8,128)(2,1)S(1)}, u32[]{:S(2)}, u32[]{:S(2)}) %collective-permute-start.4) | collective-permute-done | bytes 262176 | tf_op jit(solution)/shard_map/ppermute | solution.py:453
  46.4 2.4 %halo_projections.5.kv3_ref = bf16[2,2,128,1024]{3,2,1,0:T(8,128)(2,1)S(1)} custom-call(bf16[128,1024]{1,0:T(8,128)(2,1)S(1)} %collective-permute-done.4.up_ref, bf16[128,1024]{1,0:T(8,128)(2,1)S(1)} %broadcast_select_fusion.down_ref, bf16[1024,1024]{1,0:T(8,128)(2,1)S(1)} %get-tuple-element.93.wk_ref, bf16[1024,1024]{1,0:T(8,128)(2,1)S(1)} %get-tuple-element.94.wv_ref), custom_call_target="tpu_custom_call" | custom-call | flops 1073741824 | bytes 5767168 | tf_op jit(solution)/shard_map/halo_projections/pallas_call | solution.py:112
  48.9 9.0 %attention.1 = (bf16[2,128,1024]{2,1,0:T(8,128)(2,1)S(1)}, bf16[2,128,1024]{2,1,0:T(8,128)(2,1)S(1)}, bf16[2,2,128,1024]{3,2,1,0:T(8,128)(2,1)S(1)}, bf16[2,2,12...) custom-call(s32[14]{0:T(128)S(1)} %stack.56.place.place_ref, ...), custom_call_target="tpu_custom_call" | custom-call | flops 2684354560 | bytes 12582912 | tf_op jit(solution)/shard_map/attention/pallas_call | solution.py:194
  57.9 1.1 outer_products.1
  59.1 2.0 %back_projections.3 = (bf16[128,1024]{1,0:T(8,128)(2,1)S(1)}, bf16[128,1024]{1,0:T(8,128)(2,1)S(1)}) custom-call(bf16[2,2,128,1024]{3,2,1,0:T(8,128)(2,1)S(1)} %get-tuple-element.112.d_ref, bf16[1024,1024]{1,0:T(8,128)(2,1)S(1)} %get-tuple-element.93.wk_ref, bf16[1024,1024]{1,0:T(8,128)(2,1)S(1)} %get-tuple-element.94.wv_ref), custom_call_target="tpu_custom_call" | custom-call | flops 1073741824 | bytes 5767168 | tf_op jit(solution)/shard_map/back_projections/pallas_call | solution.py:217
  62.7 2.0 %back_projections.4 = (bf16[128,1024]{1,0:T(8,128)(2,1)S(1)}, bf16[128,1024]{1,0:T(8,128)(2,1)S(1)}) custom-call(bf16[2,2,128,1024]{3,2,1,0:T(8,128)(2,1)S(1)} %get-tuple-element.122.d_ref, bf16[1024,1024]{1,0:T(8,128)(2,1)S(1)} %get-tuple-element.93.wk_ref, bf16[1024,1024]{1,0:T(8,128)(2,1)S(1)} %get-tuple-element.94.wv_ref), custom_call_target="tpu_custom_call" | custom-call | flops 1073741824 | bytes 5767168 | tf_op jit(solution)/shard_map/back_projections/pallas_call | solution.py:217
  65.2 1.8 %collective-permute-start.8 = (bf16[128,1024]{1,0:T(8,128)(2,1)S(1)}, bf16[128,1024]{1,0:T(8,128)(2,1)S(1)}, u32[]{:S(2)}, u32[]{:S(2)}) collective-permute-start(bf16[128,1024]{1,0:T(8,128)(2,1)S(1)} %get-tuple-element.135.state_ref), channel_id=1, source_target_pairs={{0,4},{4,8},{8,12},{12,16},{16,20},{20,24},{24,28},{28,32},{32,36}... | collective-permute-start | bytes 786440 | tf_op jit(solution)/shard_map/ppermute | solution.py:465
  66.9 2.0 %back_projections.5 = (bf16[128,1024]{1,0:T(8,128)(2,1)S(1)}, bf16[128,1024]{1,0:T(8,128)(2,1)S(1)}) custom-call(bf16[2,2,128,1024]{3,2,1,0:T(8,128)(2,1)S(1)} %get-tuple-element.130.d_ref, bf16[1024,1024]{1,0:T(8,128)(2,1)S(1)} %get-tuple-element.93.wk_ref, bf16[1024,1024]{1,0:T(8,128)(2,1)S(1)} %get-tuple-element.94.wv_ref), custom_call_target="tpu_custom_call" | custom-call | flops 1073741824 | bytes 5767168 | tf_op jit(solution)/shard_map/back_projections/pallas_call | solution.py:217
  68.9 2.9 %collective-permute-done.9.moved_ref = bf16[2,4,128,256]{3,2,1,0:T(8,128)(2,1)S(1)} collective-permute-done((bf16[2,4,128,256]{3,2,1,0:T(8,128)(2,1)S(1)}, bf16[2,4,128,256]{3,2,1,0:T(8,128)(2,1)S(1)}, u32[]{:S(2)}, u32[]{:S(2)}) %collective-permute-start.9) | collective-permute-done | bytes 524320 | tf_op jit(solution)/shard_map/ppermute | solution.py:429
  72.5 1.4 %collective-permute-done.7.after_ref = bf16[128,1024]{1,0:T(8,128)(2,1)S(1)} collective-permute-done((bf16[128,1024]{1,0:T(8,128)(2,1)S(1)}, bf16[128,1024]{1,0:T(8,128)(2,1)S(1)}, u32[]{:S(2)}, u32[]{:S(2)}) %collective-permute-start.7) | collective-permute-done | bytes 262176 | tf_op jit(solution)/shard_map/ppermute | solution.py:465
  74.0 4.6 %collective-permute-done.8.before_ref = bf16[128,1024]{1,0:T(8,128)(2,1)S(1)} collective-permute-done((bf16[128,1024]{1,0:T(8,128)(2,1)S(1)}, bf16[128,1024]{1,0:T(8,128)(2,1)S(1)}, u32[]{:S(2)}, u32[]{:S(2)}) %collective-permute-start.8) | collective-permute-done | bytes 262176 | tf_op jit(solution)/shard_map/ppermute | solution.py:465
  80.4 1.2 collective-permute-start.11
  81.6 10.2 %collective-permute-done.12.moved_ref = bf16[1,4,128,256]{3,2,1,0:T(8,128)(2,1)S(1)} collective-permute-done((bf16[1,4,128,256]{3,2,1,0:T(8,128)(2,1)S(1)}, bf16[1,4,128,256]{3,2,1,0:T(8,128)(2,1)S(1)}, u32[]{:S(2)}, u32[]{:S(2)}) %collective-permute-start.12) | collective-permute-done | bytes 262176 | tf_op jit(solution)/shard_map/ppermute | solution.py:429
  92.5 2.5 %last_projections.1 = (f32[128,1024]{1,0:T(8,128)S(1)}, f32[128,1024]{1,0:T(8,128)S(1)}) custom-call(bf16[2,2,128,1024]{3,2,1,0:T(8,128)(2,1)S(1)} %get-tuple-element.145.d_ref, bf16[2,128,1024]{2,1,0:T(8,128)(2,1)S(1)} %get-tuple-element.146.dq_ref, bf16[1024,1024]{1,0:T(8,128)(2,1)S(1)} %get-tuple-element.147.wq_ref, ...), custom_call_target="tpu_custom_call" | custom-call | flops 1610612736 | bytes 8388608 | tf_op jit(solution)/shard_map/last_projections/pallas_call | solution.py:238
  95.0 2.4 %collective-permute-done.13.moved_ref = bf16[1,2,128,256]{3,2,1,0:T(8,128)(2,1)S(1)} collective-permute-done((bf16[1,2,128,256]{3,2,1,0:T(8,128)(2,1)S(1)}, bf16[1,2,128,256]{3,2,1,0:T(8,128)(2,1)S(1)}, u32[]{:S(2)}, u32[]{:S(2)}) %collective-permute-start.13) | collective-permute-done | bytes 131104 | tf_op jit(solution)/shard_map/ppermute | solution.py:429
  99.0 2.0 %collective-permute-start.15 = (bf16[128,1024]{1,0:T(8,128)(2,1)S(1)}, bf16[128,1024]{1,0:T(8,128)(2,1)S(1)}, u32[]{:S(2)}, u32[]{:S(2)}) collective-permute-start(bf16[128,1024]{1,0:T(8,128)(2,1)S(1)} %get-tuple-element.158.state_ref), channel_id=1, source_target_pairs={{0,4},{4,8},{8,12},{12,16},{16,20},{20,24},{24,28},{28,32},{32,36}... | collective-permute-start | bytes 786440 | tf_op jit(solution)/shard_map/ppermute | solution.py:465
  101.1 5.5 %collective-permute-done.16.moved_ref = bf16[1,1,128,256]{3,2,1,0:T(8,128)(2,1)S(1)} collective-permute-done((bf16[1,1,128,256]{3,2,1,0:T(8,128)(2,1)S(1)}, bf16[1,1,128,256]{3,2,1,0:T(8,128)(2,1)S(1)}, u32[]{:S(2)}, u32[]{:S(2)}) %collective-permute-start.16) | collective-permute-done | bytes 65568 | tf_op jit(solution)/shard_map/ppermute | solution.py:429
  106.5 1.2 join_last.1
  107.7 2.6 %collective-permute-done.15.before_ref = bf16[128,1024]{1,0:T(8,128)(2,1)S(1)} collective-permute-done((bf16[128,1024]{1,0:T(8,128)(2,1)S(1)}, bf16[128,1024]{1,0:T(8,128)(2,1)S(1)}, u32[]{:S(2)}, u32[]{:S(2)}) %collective-permute-start.15) | collective-permute-done | bytes 262176 | tf_op jit(solution)/shard_map/ppermute | solution.py:465
  110.3 3.3 %all-to-all-start = ((bf16[8,16,256]{2,1,0:T(8,128)(2,1)}), bf16[8,16,256]{2,1,0:T(8,128)(2,1)S(1)}, u32[]{:S(2)}, u32[]{:S(2)}) async-start(bf16[8,16,256]{2,1,0:T(8,128)(2,1)} %bitcast.22), calls=%async_computation | async-start | bytes 131072 | tf_op jit(solution)/shard_map/all_to_all | solution.py:433
  113.7 1.6 %hop_back.5 = bf16[2,128,1024]{2,1,0:T(8,128)(2,1)} custom-call(s32[14]{0:T(128)S(1)} %stack.56.place.place_ref, f32[128,1024]{1,0:T(8,128)S(1)} %get-tuple-element.150.t0_ref, f32[128,1024]{1,0:T(8,128)S(1)} %get-tuple-element.151.t1_ref, bf16[128,1024]{1,0:T(8,128)(2,1)S(1)} %collective-permute-done.14.after_ref, ...), custom_call_target="tpu_custom_call" | custom-call | flops 1048576 | bytes 1835008 | tf_op jit(solution)/shard_map/hop_back/pallas_call | solution.py:310
  115.3 6.7 %all-to-all-done = bf16[8,16,256]{2,1,0:T(8,128)(2,1)S(1)} async-done(((bf16[8,16,256]{2,1,0:T(8,128)(2,1)}), bf16[8,16,256]{2,1,0:T(8,128)(2,1)S(1)}, u32[]{:S(2)}, u32[]{:S(2)}) %all-to-all-start) | async-done | bytes 65568 | tf_op jit(solution)/shard_map/all_to_all | solution.py:433
  (35 shorter events, 9.9 us)
Async XLA Ops:
  1.7 13.9 %collective-permute-start.1 = (bf16[128,1024]{1,0:T(8,128)(2,1)S(1)}, bf16[128,1024]{1,0:T(8,128)(2,1)S(1)}, u32[]{:S(2)}, u32[]{:S(2)}) collective-permute-start(bf16[128,1024]{1,0:T(8,128)(2,1)S(1)} %get-tuple-element.164), channel_id=1, source_target_pairs={{4,0},{8,4},{12,8},{16,12},{20,16},{24,20},{28,24},{32,28},{36,32}... | collective-permute-start | bytes 786440 | tf_op jit(solution)/shard_map/ppermute | solution.py:454
  10.0 12.0 %collective-permute-start = (bf16[128,1024]{1,0:T(8,128)(2,1)S(1)}, bf16[128,1024]{1,0:T(8,128)(2,1)S(1)}, u32[]{:S(2)}, u32[]{:S(2)}) collective-permute-start(bf16[128,1024]{1,0:T(8,128)(2,1)S(1)} %get-tuple-element.165), channel_id=1, source_target_pairs={{0,4},{4,8},{8,12},{12,16},{16,20},{20,24},{24,28},{28,32},{32,36}... | collective-permute-start | bytes 786440 | tf_op jit(solution)/shard_map/ppermute | solution.py:453
  10.1 11.9 %copy-start.2 = (bf16[1,1,2,128,1024]{4,3,2,1,0:T(8,128)(2,1)S(1)}, bf16[1,1,2,128,1024]{4,3,2,1,0:T(8,128)(2,1)}, u32[]{:S(2)}) copy-start(bf16[1,1,2,128,1024]{4,3,2,1,0:T(8,128)(2,1)} %param.4) | copy-start | bytes 1572868
  22.0 9.1 %collective-permute-start.3 = (bf16[128,1024]{1,0:T(8,128)(2,1)S(1)}, bf16[128,1024]{1,0:T(8,128)(2,1)S(1)}, u32[]{:S(2)}, u32[]{:S(2)}) collective-permute-start(bf16[128,1024]{1,0:T(8,128)(2,1)S(1)} %broadcast_select_fusion.2.down_ref), channel_id=1, source_target_pairs={{4,0},{8,4},{12,8},{16,12},{20,16},{24,20},{28,24},{32,28},{36,32}... | collective-permute-start | bytes 786440 | tf_op jit(solution)/shard_map/ppermute | solution.py:454
  22.4 11.1 %collective-permute-start.2 = (bf16[128,1024]{1,0:T(8,128)(2,1)S(1)}, bf16[128,1024]{1,0:T(8,128)(2,1)S(1)}, u32[]{:S(2)}, u32[]{:S(2)}) collective-permute-start(bf16[128,1024]{1,0:T(8,128)(2,1)S(1)} %collective-permute-done.up_ref), channel_id=1, source_target_pairs={{0,4},{4,8},{8,12},{12,16},{16,20},{20,24},{24,28},{28,32},{32,36}... | collective-permute-start | bytes 786440 | tf_op jit(solution)/shard_map/ppermute | solution.py:453
  33.5 6.4 %collective-permute-start.5 = (bf16[128,1024]{1,0:T(8,128)(2,1)S(1)}, bf16[128,1024]{1,0:T(8,128)(2,1)S(1)}, u32[]{:S(2)}, u32[]{:S(2)}) collective-permute-start(bf16[128,1024]{1,0:T(8,128)(2,1)S(1)} %broadcast_select_fusion.1.down_ref), channel_id=1, source_target_pairs={{4,0},{8,4},{12,8},{16,12},{20,16},{24,20},{28,24},{32,28},{36,32}... | collective-permute-start | bytes 786440 | tf_op jit(solution)/shard_map/ppermute | solution.py:454
  35.8 10.6 %collective-permute-start.4 = (bf16[128,1024]{1,0:T(8,128)(2,1)S(1)}, bf16[128,1024]{1,0:T(8,128)(2,1)S(1)}, u32[]{:S(2)}, u32[]{:S(2)}) collective-permute-start(bf16[128,1024]{1,0:T(8,128)(2,1)S(1)} %collective-permute-done.2.up_ref), channel_id=1, source_target_pairs={{0,4},{4,8},{8,12},{12,16},{16,20},{20,24},{24,28},{28,32},{32,36}... | collective-permute-start | bytes 786440 | tf_op jit(solution)/shard_map/ppermute | solution.py:453
  46.4 2.5 %copy-start.1 = (s32[1,64,2,128]{3,2,1,0:T(2,128)S(1)}, s32[1,64,2,128]{3,2,1,0:T(2,128)}, u32[]{:S(2)}) copy-start(s32[1,64,2,128]{3,2,1,0:T(2,128)} %param.5) | copy-start | bytes 196612
  48.9 9.0 %copy-start = (bf16[1,1,2,128,1024]{4,3,2,1,0:T(8,128)(2,1)S(1)}, bf16[1,1,2,128,1024]{4,3,2,1,0:T(8,128)(2,1)}, u32[]{:S(2)}) copy-start(bf16[1,1,2,128,1024]{4,3,2,1,0:T(8,128)(2,1)} %param.7) | copy-start | bytes 1572868
  59.0 2.7 %collective-permute-start.6 = (bf16[2,1024,256]{2,1,0:T(8,128)(2,1)S(1)}, bf16[2,1024,256]{2,1,0:T(8,128)(2,1)S(1)}, u32[]{:S(2)}, u32[]{:S(2)}) collective-permute-start(bf16[2,1024,256]{2,1,0:T(8,128)(2,1)S(1)} %get-tuple-element.110), channel_id=1, source_target_pairs={{0,1},{1,0},{2,3},{3,2},{4,5},{5,4},{6,7},{7,6},{8,9},{9,8},{10,11... | collective-permute-start | bytes 3145736 | tf_op jit(solution)/shard_map/ppermute | solution.py:468
  62.6 9.3 %collective-permute-start.9 = (bf16[2,4,128,256]{3,2,1,0:T(8,128)(2,1)S(1)}, bf16[2,4,128,256]{3,2,1,0:T(8,128)(2,1)S(1)}, u32[]{:S(2)}, u32[]{:S(2)}) collective-permute-start(bf16[2,4,128,256]{3,2,1,0:T(8,128)(2,1)S(1)} %get-tuple-element.126), channel_id=1, source_target_pairs={{0,32},{1,129},{4,36},{5,133},{8,40},{9,137},{12,44},{13,141},{16,... | collective-permute-start | bytes 1572872 | tf_op jit(solution)/shard_map/ppermute | solution.py:429
  64.7 9.3 %collective-permute-start.7 = (bf16[128,1024]{1,0:T(8,128)(2,1)S(1)}, bf16[128,1024]{1,0:T(8,128)(2,1)S(1)}, u32[]{:S(2)}, u32[]{:S(2)}) collective-permute-start(bf16[128,1024]{1,0:T(8,128)(2,1)S(1)} %get-tuple-element.123), channel_id=1, source_target_pairs={{4,0},{8,4},{12,8},{16,12},{20,16},{24,20},{28,24},{32,28},{36,32}... | collective-permute-start | bytes 786440 | tf_op jit(solution)/shard_map/ppermute | solution.py:465
  65.2 13.4 %collective-permute-start.8 = (bf16[128,1024]{1,0:T(8,128)(2,1)S(1)}, bf16[128,1024]{1,0:T(8,128)(2,1)S(1)}, u32[]{:S(2)}, u32[]{:S(2)}) collective-permute-start(bf16[128,1024]{1,0:T(8,128)(2,1)S(1)} %get-tuple-element.135.state_ref), channel_id=1, source_target_pairs={{0,4},{4,8},{8,12},{12,16},{16,20},{20,24},{24,28},{28,32},{32,36}... | collective-permute-start | bytes 786440 | tf_op jit(solution)/shard_map/ppermute | solution.py:465
  78.5 13.2 %collective-permute-start.12 = (bf16[1,4,128,256]{3,2,1,0:T(8,128)(2,1)S(1)}, bf16[1,4,128,256]{3,2,1,0:T(8,128)(2,1)S(1)}, u32[]{:S(2)}, u32[]{:S(2)}) collective-permute-start(bf16[1,4,128,256]{3,2,1,0:T(8,128)(2,1)S(1)} %get-tuple-element.139), channel_id=1, source_target_pairs={{0,96},{1,131},{4,100},{5,135},{8,104},{9,139},{12,108},{13,143},{... | collective-permute-start | bytes 786440 | tf_op jit(solution)/shard_map/ppermute | solution.py:429
  79.5 18.5 %collective-permute-start.10 = (bf16[128,1024]{1,0:T(8,128)(2,1)S(1)}, bf16[128,1024]{1,0:T(8,128)(2,1)S(1)}, u32[]{:S(2)}, u32[]{:S(2)}) collective-permute-start(bf16[128,1024]{1,0:T(8,128)(2,1)S(1)} %get-tuple-element.136), channel_id=1, source_target_pairs={{4,0},{8,4},{12,8},{16,12},{20,16},{24,20},{28,24},{32,28},{36,32}... | collective-permute-start | bytes 786440 | tf_op jit(solution)/shard_map/ppermute | solution.py:465
  80.4 17.7 %collective-permute-start.11 = (bf16[128,1024]{1,0:T(8,128)(2,1)S(1)}, bf16[128,1024]{1,0:T(8,128)(2,1)S(1)}, u32[]{:S(2)}, u32[]{:S(2)}) collective-permute-start(bf16[128,1024]{1,0:T(8,128)(2,1)S(1)} %get-tuple-element.156.state_ref), channel_id=1, source_target_pairs={{0,4},{4,8},{8,12},{12,16},{16,20},{20,24},{24,28},{28,32},{32,36}... | collective-permute-start | bytes 786440 | tf_op jit(solution)/shard_map/ppermute | solution.py:465
  92.4 5.1 %collective-permute-start.13 = (bf16[1,2,128,256]{3,2,1,0:T(8,128)(2,1)S(1)}, bf16[1,2,128,256]{3,2,1,0:T(8,128)(2,1)S(1)}, u32[]{:S(2)}, u32[]{:S(2)}) collective-permute-start(bf16[1,2,128,256]{3,2,1,0:T(8,128)(2,1)S(1)} %get-tuple-element.141), channel_id=1, source_target_pairs={{0,128},{1,33},{4,132},{5,37},{8,136},{9,41},{12,140},{13,45},{16,... | collective-permute-start | bytes 393224 | tf_op jit(solution)/shard_map/ppermute | solution.py:429
  99.0 8.8 %collective-permute-start.14 = (bf16[128,1024]{1,0:T(8,128)(2,1)S(1)}, bf16[128,1024]{1,0:T(8,128)(2,1)S(1)}, u32[]{:S(2)}, u32[]{:S(2)}) collective-permute-start(bf16[128,1024]{1,0:T(8,128)(2,1)S(1)} %get-tuple-element.157), channel_id=1, source_target_pairs={{4,0},{8,4},{12,8},{16,12},{20,16},{24,20},{28,24},{32,28},{36,32}... | collective-permute-start | bytes 786440 | tf_op jit(solution)/shard_map/ppermute | solution.py:465
  99.0 11.3 %collective-permute-start.15 = (bf16[128,1024]{1,0:T(8,128)(2,1)S(1)}, bf16[128,1024]{1,0:T(8,128)(2,1)S(1)}, u32[]{:S(2)}, u32[]{:S(2)}) collective-permute-start(bf16[128,1024]{1,0:T(8,128)(2,1)S(1)} %get-tuple-element.158.state_ref), channel_id=1, source_target_pairs={{0,4},{4,8},{8,12},{12,16},{16,20},{20,24},{24,28},{28,32},{32,36}... | collective-permute-start | bytes 786440 | tf_op jit(solution)/shard_map/ppermute | solution.py:465
  101.1 5.5 %collective-permute-start.16 = (bf16[1,1,128,256]{3,2,1,0:T(8,128)(2,1)S(1)}, bf16[1,1,128,256]{3,2,1,0:T(8,128)(2,1)S(1)}, u32[]{:S(2)}, u32[]{:S(2)}) collective-permute-start(bf16[1,1,128,256]{3,2,1,0:T(8,128)(2,1)S(1)} %get-tuple-element.160), channel_id=1, source_target_pairs={{0,130},{1,97},{4,134},{5,101},{8,138},{9,105},{12,142},{13,109},{... | collective-permute-start | bytes 196616 | tf_op jit(solution)/shard_map/ppermute | solution.py:429
  110.3 11.7 %all-to-all-start = ((bf16[8,16,256]{2,1,0:T(8,128)(2,1)}), bf16[8,16,256]{2,1,0:T(8,128)(2,1)S(1)}, u32[]{:S(2)}, u32[]{:S(2)}) async-start(bf16[8,16,256]{2,1,0:T(8,128)(2,1)} %bitcast.22), calls=%async_computation | async-start | bytes 131072 | tf_op jit(solution)/shard_map/all_to_all | solution.py:433

commit v5 on v4

v5 whole, which is shorter than its diff:
```python
import jax
import jax.numpy as jnp
import numpy as np
from jax import lax
from jax.experimental import pallas as pl
from jax.experimental.pallas import tpu as pltpu
from jax.sharding import PartitionSpec as P

HEADS = 16
HEAD_DIM = 64
WIN = 4
BLOCK = 128
D = 1024
PAIR = 2 * HEAD_DIM
PAIRS_A_STEP = 4
TILE = 256
BF = jnp.bfloat16
F32 = jnp.float32

BARRED = -1e30
FREE = 3e38
SCALE = HEAD_DIM**-0.5
EXP2_SCALE = float(SCALE * np.log2(np.e))

NN = (((1,), (0,)), ((), ()))
NT = (((1,), (1,)), ((), ()))


def mm(a, b, dims=NN):
    return lax.dot_general(a, b, dims, preferred_element_type=F32)


def params(mib):
    return pltpu.CompilerParams(vmem_limit_bytes=mib * 2**20)


def cost(flops, moved, exps=0):
    return pl.CostEstimate(flops=flops // 16, bytes_accessed=moved // 16, transcendentals=exps // 16)


def in_hbm(*arrays):
    return [pltpu.with_memory_space_constraint(a, pltpu.HBM) for a in arrays]


def in_vmem(*arrays):
    return [pltpu.with_memory_space_constraint(a, pltpu.VMEM) for a in arrays]


def weight_cols(which):
    return pl.BlockSpec((D, TILE), lambda t, *_: (which, t))


def weight_rows(which):
    return pl.BlockSpec((TILE, D), lambda t, *_: (which * (D // TILE) + t, 0))


def whole(shape):
    return pl.BlockSpec(shape, lambda t, *_: (0,) * len(shape))


EVEN_PAIRS = [(i, i ^ 1) for i in range(64)]
ODD_PAIRS = [(i, i if i in (0, 63) else ((i + 1) ^ 1) - 1) for i in range(64)]


def exchange(even, odd):
    return lax.ppermute(even, "blk", EVEN_PAIRS), lax.ppermute(odd, "blk", ODD_PAIRS)


def with_parity(kernel, parity, arrays, grid, in_specs, out_specs, out_shape, mib, estimate):
    return pl.pallas_call(
        kernel,
        grid_spec=pltpu.PrefetchScalarGridSpec(
            num_scalar_prefetch=1, grid=grid, in_specs=in_specs, out_specs=out_specs
        ),
        out_shape=out_shape,
        compiler_params=params(mib),
        cost_estimate=estimate,
        name=kernel.__name__,
    )(parity, *arrays)


def halves_of(parity):
    return pl.ds(1 - parity[0], 1), pl.ds(parity[0], 1)


def first_arrays(parity, half_a, half_b, even_ref, odd_ref):
    even_ref[...] = half_a[0]
    odd_ref[...] = half_b[0]


def first_exchange(parity, x):
    shape = (1, BLOCK, D // 2)
    spec = pl.BlockSpec((BLOCK, D // 2), lambda t, p: (0, t))
    return with_parity(
        first_arrays, parity, in_hbm(x, x), (2,),
        [pl.BlockSpec(shape, lambda t, p: (p[0], 0, t)), pl.BlockSpec(shape, lambda t, p: (1 - p[0], 0, t))],
        [spec] * 2, [jax.ShapeDtypeStruct((BLOCK, D), BF)] * 2, 6, cost(0, 8 * BLOCK * D),
    )


def own_kernel(x_ref, wk_ref, wv_ref, kv_ref, wk_out, wv_out):
    wk_out[...] = wk_ref[...]
    wv_out[...] = wv_ref[...]
    x = x_ref[...].reshape(2 * BLOCK, D)
    kv_ref[0] = mm(x, wk_ref[...]).astype(BF).reshape(2, BLOCK, TILE)
    kv_ref[1] = mm(x, wv_ref[...]).astype(BF).reshape(2, BLOCK, TILE)


def own_projections(x, weights):
    return pl.pallas_call(
        own_kernel,
        grid=(D // TILE,),
        in_specs=[whole((2, BLOCK, D)), weight_cols(1), weight_cols(2)],
        out_specs=[pl.BlockSpec((2, 2, BLOCK, TILE), lambda t: (0, 0, 0, t))] + [weight_cols(0)] * 2,
        out_shape=[jax.ShapeDtypeStruct((2, 2, BLOCK, D), BF)] + [jax.ShapeDtypeStruct((D, D), BF)] * 2,
        compiler_params=params(12),
        cost_estimate=cost(8 * 2 * BLOCK * D * D, 12 * D * D + 12 * BLOCK * D),
        name="own_projections",
    )(*in_hbm(x, weights, weights))


def query_kernel(x_ref, g_ref, wq_ref, wo_ref, q_ref, da_ref, wq_out):
    wq_out[...] = wq_ref[...]
    x = x_ref[...].reshape(2 * BLOCK, D)
    g = g_ref[...].reshape(2 * BLOCK, D)
    q_ref[...] = mm(x, wq_ref[...]).astype(BF).reshape(2, BLOCK, TILE)
    da_ref[...] = mm(g, wo_ref[...], NT).astype(BF).reshape(2, BLOCK, TILE)


def query_projections(x, g, weights):
    rows = jax.ShapeDtypeStruct((2, BLOCK, D), BF)
    row_tile = pl.BlockSpec((2, BLOCK, TILE), lambda t: (0, 0, t))
    return pl.pallas_call(
        query_kernel,
        grid=(D // TILE,),
        in_specs=[whole((2, BLOCK, D)), whole((2, BLOCK, D)), weight_cols(0), weight_rows(3)],
        out_specs=[row_tile, row_tile, weight_cols(0)],
        out_shape=[rows, rows, jax.ShapeDtypeStruct((D, D), BF)],
        compiler_params=params(12),
        cost_estimate=cost(8 * 2 * BLOCK * D * D, 12 * D * D + 12 * BLOCK * D),
        name="query_projections",
    )(*in_hbm(x, g, weights, weights))


def halo_projections_kernel(parity, even_ref, odd_ref, wk_ref, wv_ref, kv_ref):
    x = jnp.concatenate([even_ref[...], odd_ref[...]], axis=0)
    for which, w_ref in enumerate((wk_ref, wv_ref)):
        rows = mm(x, w_ref[...]).astype(BF).reshape(2, BLOCK, TILE)
        for i, half in enumerate(halves_of(parity)):
            kv_ref[which, half] = rows[i : i + 1]


def halo_projections(parity, even, odd, wk, wv):
    return with_parity(
        halo_projections_kernel, parity, [even, odd, *in_vmem(wk, wv)], (D // TILE,),
        [whole((BLOCK, D)), whole((BLOCK, D)), weight_cols(0), weight_cols(0)],
        pl.BlockSpec((2, 2, BLOCK, TILE), lambda t, p: (0, 0, 0, t)),
        jax.ShapeDtypeStruct((2, 2, BLOCK, D), BF), 10,
        cost(4 * 2 * BLOCK * D * D, 4 * D * D + 12 * BLOCK * D),
    )


LANES = [slice(i * PAIR, (i + 1) * PAIR) for i in range(PAIRS_A_STEP)]


def first_head():
    return lax.broadcasted_iota(jnp.int32, (BLOCK, PAIR), 1) < HEAD_DIM


def split(rows):
    zero = jnp.zeros_like(rows)
    return jnp.concatenate([jnp.where(first_head(), rows, zero), jnp.where(first_head(), zero, rows)], axis=0)


def merge(rows):
    return jnp.where(first_head(), rows[:BLOCK], rows[BLOCK:])


def stacked(refs, which):
    return [jnp.concatenate([ref[which, 0, :, c] for ref in refs], axis=0) for c in LANES]


def score_limits(block, valid_ref):
    limits = []
    for back in range(WIN - 1, -1, -1):
        key_block = block - back
        slot = jnp.maximum(jnp.where(key_block < 64, key_block, 127 - key_block), 0)
        halves = valid_ref[pl.ds(slot, 1)].reshape(2, BLOCK)
        serves = jnp.where(key_block < 64, halves[:1], halves[1:])
        limit = jnp.where((serves == 1) & (key_block >= 0), FREE, BARRED)
        limits.append(jnp.broadcast_to(limit, (BLOCK, BLOCK)))
    row = lax.broadcasted_iota(jnp.int32, (BLOCK, BLOCK), 0)
    column = lax.broadcasted_iota(jnp.int32, (BLOCK, BLOCK), 1)
    limits[-1] = jnp.where(row == column, FREE, jnp.where(row > column, limits[-1], BARRED))
    bias = jnp.concatenate(limits, axis=1)
    return jnp.concatenate([bias, bias], axis=0)


def attention_out(
    place, valid_ref, q_ref, da_ref, kv3_ref, kv2_ref, kv1_ref, kv0_ref, out_ref, scaled_ref, terms_ref
):
    refs = (kv3_ref, kv2_ref, kv1_ref, kv0_ref)
    bias = score_limits(jnp.where(pl.program_id(0) == 0, place[0], 127 - place[0]), valid_ref)
    ones = jnp.ones((WIN * BLOCK, PAIR), BF)
    keys, values = stacked(refs, 0), stacked(refs, 1)
    scores = [mm(split(q_ref[0, :, c]), k, NT) for c, k in zip(LANES, keys)]
    scores = [jnp.minimum(s, bias) for s in scores]
    tops = [jnp.max(s, axis=1, keepdims=True) for s in scores]
    terms = [jnp.exp2((s - t) * EXP2_SCALE).astype(BF) for s, t in zip(scores, tops)]
    sums = [mm(t, jnp.concatenate([v, ones], axis=1)) for t, v in zip(terms, values)]
    shares = [1.0 / merge(s[:, PAIR:]) for s in sums]
    for i, c in enumerate(LANES):
        out_ref[0, :, c] = (merge(sums[i][:, :PAIR]) * shares[i]).astype(BF)
        scaled_ref[0, :, c] = (da_ref[0, :, c].astype(F32) * shares[i]).astype(BF)
        terms_ref[0, i] = terms[i]


def attention_grads(
    q_ref, kv3_ref, kv2_ref, kv1_ref, kv0_ref, out_ref, scaled_ref, terms_ref,
    dq_ref, d3_ref, d2_ref, d1_ref, d0_ref,
):
    refs = (kv3_ref, kv2_ref, kv1_ref, kv0_ref)
    keys, values = stacked(refs, 0), stacked(refs, 1)
    queries = [split(q_ref[0, :, c]) for c in LANES]
    scaled = [scaled_ref[0, :, c] for c in LANES]
    d_attn = [split(d) for d in scaled]
    terms = [terms_ref[0, i] for i in range(PAIRS_A_STEP)]
    d_probs = [mm(d, v, NT) for d, v in zip(d_attn, values)]
    deltas = [
        jnp.sum(split(d.astype(F32) * out_ref[0, :, c].astype(F32)), axis=1, keepdims=True)
        for c, d in zip(LANES, scaled)
    ]
    d_scores = [(p - d).astype(BF) * t for p, d, t in zip(d_probs, deltas, terms)]
    d_values = [mm(d.T, t).astype(BF).T for d, t in zip(d_attn, terms)]
    d_queries = [merge(mm(d, k)) for d, k in zip(d_scores, keys)]
    for c, d in zip(LANES, d_queries):
        dq_ref[0, :, c] = (d * SCALE).astype(BF)
    d_keys = [(mm(q.T, d) * SCALE).astype(BF).T for q, d in zip(queries, d_scores)]
    for c, dk, dv in zip(LANES, d_keys, d_values):
        for i, ref in enumerate((d3_ref, d2_ref, d1_ref, d0_ref)):
            ref[0, 0, :, c] = dk[i * BLOCK : (i + 1) * BLOCK]
            ref[1, 0, :, c] = dv[i * BLOCK : (i + 1) * BLOCK]


WIDTH = PAIRS_A_STEP * PAIR
ROWS = pl.BlockSpec((1, BLOCK, WIDTH), lambda h, p, *_: (h, 0, p))
PAIRED = pl.BlockSpec((2, 1, BLOCK, WIDTH), lambda h, p, *_: (0, h, 0, p))
VALID = pl.BlockSpec((64, 2, BLOCK), lambda h, p, *_: (0, 0, 0))
TERMS = pl.BlockSpec((1, PAIRS_A_STEP, 2 * BLOCK, WIN * BLOCK), lambda h, p, *_: (h, p, 0, 0))
ROWS_LOW = jax.ShapeDtypeStruct((2, BLOCK, D), BF)
PAIRED_LOW = jax.ShapeDtypeStruct((2, 2, BLOCK, D), BF)
TERMS_LOW = jax.ShapeDtypeStruct((2, HEADS // 2, 2 * BLOCK, WIN * BLOCK), BF)


def attention_forward(place, key_valid, q, da, kvs):
    return with_parity(
        attention_out, place, [key_valid, *in_vmem(q, da, *kvs)], (2, D // WIDTH),
        [VALID, ROWS, ROWS] + [PAIRED] * 4, [ROWS, ROWS, TERMS], [ROWS_LOW, ROWS_LOW, TERMS_LOW], 24,
        cost(2 * 4 * BLOCK * WIN * BLOCK * D * 2, 10 * 2**20, 2**21),
    )


def attention_backward(q, kvs, out, scaled, terms):
    return pl.pallas_call(
        attention_grads,
        grid=(2, D // WIDTH),
        in_specs=[ROWS] + [PAIRED] * 4 + [ROWS, ROWS, TERMS],
        out_specs=[ROWS] + [PAIRED] * 4,
        out_shape=[ROWS_LOW] + [PAIRED_LOW] * 4,
        compiler_params=params(24),
        cost_estimate=cost(2 * 6 * BLOCK * WIN * BLOCK * D * 2, 12 * 2**20),
        name="attention_grads",
    )(*in_vmem(q, *kvs, out, scaled, terms))


def in_order(parity, ref, *lead):
    return jnp.concatenate([ref[(*lead, half)] for half in halves_of(parity)], axis=0).reshape(2 * BLOCK, D)


def back_projections_kernel(parity, d_ref, wk_ref, wv_ref, even_ref, odd_ref):
    rows = mm(in_order(parity, d_ref, 0), wk_ref[...], NT)
    rows += mm(in_order(parity, d_ref, 1), wv_ref[...], NT)
    even_ref[...] = rows[:BLOCK].astype(BF)
    odd_ref[...] = rows[BLOCK:].astype(BF)


def last_projections_kernel(parity, d_ref, dq_ref, wq_ref, wk_ref, wv_ref, even_ref, odd_ref):
    rows = mm(in_order(parity, dq_ref), wq_ref[...], NT)
    rows += mm(in_order(parity, d_ref, 0), wk_ref[...], NT)
    rows += mm(in_order(parity, d_ref, 1), wv_ref[...], NT)
    even_ref[...] = rows[:BLOCK]
    odd_ref[...] = rows[BLOCK:]


def back_projections(parity, d, wk, wv):
    return with_parity(
        back_projections_kernel, parity, in_vmem(d, wk, wv), (D // TILE,),
        [whole((2, 2, BLOCK, D)), weight_rows(0), weight_rows(0)],
        [pl.BlockSpec((BLOCK, TILE), lambda t, p: (0, t))] * 2,
        [jax.ShapeDtypeStruct((BLOCK, D), BF)] * 2, 10,
        cost(4 * 2 * BLOCK * D * D, 4 * D * D + 12 * BLOCK * D),
    )


def last_projections(parity, d, dq, wq, wk, wv):
    return with_parity(
        last_projections_kernel, parity, in_vmem(d, dq, wq, wk, wv), (D // TILE,),
        [whole((2, 2, BLOCK, D)), whole((2, BLOCK, D)), weight_rows(0), weight_rows(0), weight_rows(0)],
        [pl.BlockSpec((BLOCK, TILE), lambda t, p: (0, t))] * 2,
        [jax.ShapeDtypeStruct((BLOCK, D), F32)] * 2, 12,
        cost(6 * 2 * BLOCK * D * D, 6 * D * D + 16 * BLOCK * D),
    )


def outer_kernel(core_ref, o_ref, keep_ref, send_ref, kept_ref, sent_ref):
    o_t = o_ref[...].reshape(2 * BLOCK, D).T
    for g_ref, r_ref in ((send_ref, sent_ref), (keep_ref, kept_ref)):
        r_ref[0] = mm(o_t, g_ref[...].reshape(2 * BLOCK, TILE)).astype(BF)


def outer_products(o, g, core):
    result = jax.ShapeDtypeStruct((2, D, TILE), BF)
    result_spec = pl.BlockSpec((1, D, TILE), lambda y, c: (y, 0, 0))
    return pl.pallas_call(
        outer_kernel,
        grid_spec=pltpu.PrefetchScalarGridSpec(
            num_scalar_prefetch=1,
            grid=(2,),
            in_specs=[
                pl.BlockSpec((2, BLOCK, D), lambda y, c: (0, 0, 0)),
                pl.BlockSpec((2, BLOCK, TILE), lambda y, c: (0, 0, 2 * y + c[0])),
                pl.BlockSpec((2, BLOCK, TILE), lambda y, c: (0, 0, 2 * y + 1 - c[0])),
            ],
            out_specs=[result_spec, result_spec],
        ),
        out_shape=[result, result],
        compiler_params=params(12),
        cost_estimate=cost(4 * BLOCK * D * D, 2 * D * D + 8 * BLOCK * D),
        name="outer_products",
    )(core, *in_vmem(o, g, g))


def hop_sums(even_ref, odd_ref, from_even, from_odd):
    return (
        (even_ref[...].astype(F32) + from_odd[...].astype(F32)).astype(BF),
        (odd_ref[...].astype(F32) + from_even[...].astype(F32)).astype(BF),
    )


def hop_kernel(parity, even_ref, odd_ref, from_even, from_odd, even_out, odd_out):
    even_out[...], odd_out[...] = hop_sums(even_ref, odd_ref, from_even, from_odd)


def final_kernel(parity, even_ref, odd_ref, from_even, from_odd, out_ref):
    for half, rows in zip(halves_of(parity), hop_sums(even_ref, odd_ref, from_even, from_odd)):
        out_ref[half] = rows[None]


def hop_back(parity, terms, moved, last=False):
    spec = pl.BlockSpec((BLOCK, D // 2), lambda t, p: (0, t))
    if last:
        out_specs = pl.BlockSpec((2, BLOCK, D // 2), lambda t, p: (0, 0, t))
        out_shape = jax.ShapeDtypeStruct((2, BLOCK, D), BF)
    else:
        out_specs = [spec] * 2
        out_shape = [jax.ShapeDtypeStruct((BLOCK, D), BF)] * 2
    return with_parity(
        final_kernel if last else hop_kernel, parity, in_vmem(*terms, *moved), (2,),
        [spec] * 4, out_specs, out_shape, 6, cost(8 * BLOCK * D, 14 * BLOCK * D),
    )


def chip(y, x, z, core):
    return ((y % 2) * 32 + x * 8 + z) * 4 + (y // 2) * 2 + core


CORE_PAIRS = [(i, i ^ 1) for i in range(4)]
LINES = [[32 * y + 8 * x + z for z in range(8)] for y in range(2) for x in range(4)]
FLIP = ((1, 0, 3, 2), (3, 2, 1, 0))


def halving_pairs(second, turn):
    pairs = []
    for y in range(4):
        for x in range(4):
            for z in range(8):
                for core in range(2):
                    along_x = (core == 0) != second
                    to = (y, FLIP[turn][x]) if along_x else (FLIP[turn][y], x)
                    pairs.append((chip(y, x, z, core), chip(*to, z, core)))
    return pairs


SHARE = 128


def places(position, shot):
    def ring(i):
        outer = (i == 0) | (i == 3)
        keep = [jnp.where(outer, 0, 1), jnp.where(outer, 3, 2)]
        send = [jnp.where(outer, 1, 0), jnp.where(outer, 2, 3)]
        return keep + send + [i // 2, 1 - i // 2]

    core = shot % 2
    x = (position // 8) % 4
    y = (shot // 2) * 2 + position // 32
    first, second = jnp.where(core == 0, x, y), jnp.where(core == 0, y, x)
    return jnp.stack([position, core] + ring(first) + ring(second)).astype(jnp.int32)


FIRST, SECOND = 2, 8


def total(a, b):
    return (a.astype(F32) + b.astype(F32)).astype(BF)


def split_core(place, kept_ref, other_ref, keep_ref, send_ref):
    for out_ref, at in ((keep_ref, FIRST), (send_ref, FIRST + 2)):
        for i in range(2):
            for j in range(4):
                first = place[at + i]
                y = pl.ds(jnp.where(place[1] == 0, j, first), 1)
                x = pl.ds(jnp.where(place[1] == 0, first, j), 1)
                out_ref[i : i + 1, j : j + 1] = total(kept_ref[y, x], other_ref[y, x])


def split_first(place, kept_ref, moved_ref, keep_ref, send_ref):
    for j, out_ref in enumerate((keep_ref, send_ref)):
        i = pl.ds(place[FIRST + 4 + j], 1)
        out_ref[...] = total(kept_ref[i], moved_ref[i])


def split_second(place, kept_ref, moved_ref, keep_ref, send_ref):
    for out_ref, at in ((keep_ref, SECOND), (send_ref, SECOND + 2)):
        for j in range(2):
            i = pl.ds(place[at + j], 1)
            out_ref[:, j : j + 1] = total(kept_ref[:, i], moved_ref[:, i])


def split_third(place, kept_ref, moved_ref, keep_ref, send_ref):
    for j, out_ref in enumerate((keep_ref, send_ref)):
        i = pl.ds(place[SECOND + 4 + j], 1)
        out_ref[...] = total(kept_ref[:, i], moved_ref[:, i])


def join_last(place, kept_ref, moved_ref, out_ref):
    out_ref[...] = total(kept_ref[...], moved_ref[...])


def halving(kernel, place, arrays, shapes):
    vmem = pl.BlockSpec(memory_space=pltpu.VMEM)
    return pl.pallas_call(
        kernel,
        in_specs=[pl.BlockSpec(memory_space=pltpu.SMEM)] + [vmem] * len(arrays),
        out_specs=[vmem] * len(shapes),
        out_shape=[jax.ShapeDtypeStruct(shape + (SHARE, TILE), BF) for shape in shapes],
        compiler_params=params(8),
        cost_estimate=cost(2**20, 2**20),
        name=kernel.__name__,
    )(place, *arrays)


def halve_core(place, kept, other):
    arrays = [v.reshape(4, 4, SHARE, TILE) for v in (kept, other)]
    return halving(split_core, place, arrays, [(2, 4)] * 2)


HALVINGS = (
    (split_first, halving_pairs(False, 0), [(1, 4)] * 2),
    (split_second, halving_pairs(False, 1), [(1, 2)] * 2),
    (split_third, halving_pairs(True, 0), [(1, 1)] * 2),
    (join_last, halving_pairs(True, 1), [(1, 1)]),
)


def after(values, ready):
    return lax.optimization_barrier((values, ready))[0]


def halve(turn, place, pieces, ready):
    kernel, pairs, shapes = HALVINGS[turn]
    keep, send = pieces
    moved = after(lax.ppermute(send, ("blk", "dp"), pairs), ready)
    return halving(kernel, place, [keep, moved], shapes)


def sum_over_line(total):
    total = lax.all_to_all(total.reshape(8, 16, TILE), "blk", 0, 0, axis_index_groups=LINES)
    return jnp.sum(total.astype(F32), axis=0)


def per_device(tokens, key_valid, weights, out_grad):
    position = lax.axis_index("blk")
    shot = lax.axis_index("dp")
    x = tokens.reshape(2, BLOCK, D)
    g = out_grad.reshape(2, BLOCK, D)

    parity = (position % 2).reshape(1)
    state = first_exchange(parity, x)
    core = (shot % 2).reshape(1)
    place = places(position, shot)
    own, core, place = lax.optimization_barrier((x, core, place))
    kv0, wk, wv = own_projections(own, weights)
    kvs = [kv0]
    for hop_index in range(WIN - 1):
        from_even, from_odd = exchange(*state)
        if hop_index == 1:
            q, da, wq, kvs[-1] = lax.optimization_barrier((*query_projections(own, g, weights), kvs[-1]))
            from_even, from_odd, q = lax.optimization_barrier((from_even, from_odd, q))
        from_even, from_odd, kvs[-1] = lax.optimization_barrier((from_even, from_odd, kvs[-1]))
        kvs.append(halo_projections(parity, from_even, from_odd, wk, wv))
        state = from_odd, from_even
    kvs = kvs[::-1]
    o, scaled, exps = attention_forward(place, key_valid.reshape(64, 2, BLOCK), q, da, kvs)

    kept, sent = outer_products(o, g, core)
    pieces = halve_core(place, kept, lax.ppermute(sent, "dp", CORE_PAIRS))
    exps, pieces = lax.optimization_barrier((exps, pieces))
    dq, d3, d2, d1, d0 = attention_backward(q, kvs, o, scaled, exps)
    state = back_projections(parity, d3, wk, wv)

    moved = exchange(*state)
    d2, d1, state = lax.optimization_barrier((d2, d1, state))
    terms = back_projections(parity, d2, wk, wv)
    later = back_projections(parity, d1, wk, wv)
    pieces = halve(1, place, halve(0, place, pieces, terms), later)
    pieces = halve(2, place, pieces, pieces)
    state = hop_back(parity, terms, after(moved, pieces))

    moved = exchange(*state)
    last = last_projections(parity, after(d0, state), dq, wq, wk, wv)
    (plane_sum,) = halve(3, place, pieces, last)
    state = hop_back(parity, later, after(moved, plane_sum))

    moved = exchange(*state)
    grad_tokens = hop_back(parity, last, moved, True)
    w_grad = sum_over_line(plane_sum)
    return grad_tokens.reshape(tokens.shape), w_grad


def solution(mesh):
    placed = (
        P("dp", "blk", None, None, None),
        P("dp", None, None, None),
        P(),
        P("dp", "blk", None, None, None),
    )
    return jax.shard_map(
        per_device,
        mesh=mesh,
        in_specs=placed,
        out_specs=(P("dp", "blk", None, None, None), P("blk", "dp")),
        check_vma=False,
    )
```

time: 123 us -> 118 us (0.959)
  waiting for transfers between devices: 54.6 us -> 21 us
  starting transfers between devices: 22.8 us -> 40.9 us
  blocking collectives: 0 us -> 10.8 us
    ppermute x17, waiting for transfers between devices: 47.9 us -> 21 us  [the longest x4 11.3 us: halve(): moved = after(lax.ppermute(send, ('blk', 'dp'), pairs), ready)]
    ppermute x17, starting transfers between devices: 19.4 us -> 40.9 us  [the longest x6 38 us: exchange(): lax.ppermute(odd, 'blk', ODD_PAIRS)]
    all_to_all x0 -> x1, blocking collectives: none -> 10.8 us  [sum_over_line(): lax.all_to_all(total.reshape(8, 16, TILE), 'blk', 0, 0, axis_index_groups...]
    all_to_all x1 -> x0, waiting for transfers between devices: 6.71 us -> none  [sum_over_line(): lax.all_to_all(total.reshape(8, 16, TILE), 'blk', 0, 0, axis_index_groups...]
    all_to_all x1 -> x0, starting transfers between devices: 3.35 us -> none  [sum_over_line(): lax.all_to_all(total.reshape(8, 16, TILE), 'blk', 0, 0, axis_index_groups...]
    pallas_call x11 -> x13, Pallas kernels: 28.2 us -> 28.9 us  [the longest x12 23.7 us: with_parity(): pl.pallas_call(kernel, grid_spec=pltpu.PrefetchScalarGridSpec(num_scalar_...]
  transfers between devices with their start and end apart: 18 -> 17, of which waited for: 14 -> 6; matrix products, arithmetic and copies ran while one was open for 0% -> 1% of each run, Pallas kernels for 23% -> 25%
where the time goes in v5:
time: 118 us; the launch traced here: 117 us
  Pallas kernels  42.5 us (36%)
  starting transfers between devices  40.9 us (35%)
  waiting for transfers between devices  21 us (18%)
  blocking collectives  10.8 us (9%)
    ppermute x6, starting transfers between devices, exchange(): lax.ppermute(odd, 'blk', ODD_PAIRS)  38 us
    pallas_call x12, Pallas kernels, with_parity(): pl.pallas_call(kernel, grid_spec=pltpu.PrefetchScalarGridSpec(num_scalar_...  23.7 us
    ppermute x4, waiting for transfers between devices, halve(): moved = after(lax.ppermute(send, ('blk', 'dp'), pairs), ready)  11.3 us
    all_to_all x1, blocking collectives, sum_over_line(): lax.all_to_all(total.reshape(8, 16, TILE), 'blk', 0, 0, axis_index_groups...  10.8 us
    ppermute x6, waiting for transfers between devices, exchange(): lax.ppermute(odd, 'blk', ODD_PAIRS)  6.95 us
    pallas_call x1, Pallas kernels, attention_backward(): pl.pallas_call(attention_grads, grid=(2, D // WIDTH), in_specs=[ROWS] + [...  5.21 us
    pallas_call x1, Pallas kernels, own_projections(): pl.pallas_call(own_kernel, grid=(D // TILE,), in_specs=[whole((2, BLOCK,...  4.71 us
    pallas_call x1, Pallas kernels, query_projections(): pl.pallas_call(query_kernel, grid=(D // TILE,), in_specs=[whole((2, BLOCK...  4.6 us
  transfers between devices with their start and end apart: 17, of which 6 were waited for; matrix products, arithmetic and copies ran while one was open for 1% of the time, Pallas kernels for 25%

profile of v5, /device:TPU:24, one launch (start us, length us, event | category | flops | bytes accessed | tf_op | source)
XLA Modules:
  0.0 117.0 jit_solution(1770719336301351098)
XLA Ops:
  0.6 1.2 %first_arrays.1 = (bf16[128,1024]{1,0:T(8,128)(2,1)S(1)}, bf16[128,1024]{1,0:T(8,128)(2,1)S(1)}) custom-call(s32[1]{0:T(128)} %bitcast.parity, bf16[2,128,1024]{2,1,0:T(8,128)(2,1)} %bitcast.29, bf16[2,128,1024]{2,1,0:T(8,128)(2,1)} %bitcast.30), custom_call_target="tpu_custom_call" | custom-call | bytes 65536 | tf_op jit(solution)/shard_map/first_arrays/pallas_call | solution.py:70
  1.8 2.0 %collective-permute-start = (bf16[128,1024]{1,0:T(8,128)(2,1)S(1)}, bf16[128,1024]{1,0:T(8,128)(2,1)S(1)}, u32[]{:S(2)}, u32[]{:S(2)}) collective-permute-start(bf16[128,1024]{1,0:T(8,128)(2,1)S(1)} %get-tuple-element.73), channel_id=1, source_target_pairs={{0,4},{4,0},{8,12},{12,8},{16,20},{20,16},{24,28},{28,24},{32,36},... | collective-permute-start | bytes 786440 | tf_op jit(solution)/shard_map/ppermute | solution.py:66
  3.8 9.2 %collective-permute-start.1 = (bf16[128,1024]{1,0:T(8,128)(2,1)S(1)}, bf16[128,1024]{1,0:T(8,128)(2,1)S(1)}, u32[]{:S(2)}, u32[]{:S(2)}) collective-permute-start(bf16[128,1024]{1,0:T(8,128)(2,1)S(1)} %get-tuple-element.74), channel_id=1, source_target_pairs={{0,0},{4,8},{8,4},{12,16},{16,12},{20,24},{24,20},{28,32},{32,28},... | collective-permute-start | bytes 786440 | tf_op jit(solution)/shard_map/ppermute | solution.py:66
  13.3 4.7 %own_projections.1 = (bf16[2,2,128,1024]{3,2,1,0:T(8,128)(2,1)S(1)}, bf16[1024,1024]{1,0:T(8,128)(2,1)S(1)}, bf16[1024,1024]{1,0:T(8,128)(2,1)S(1)}) custom-call(bf16[2,128,1024]{2,1,0:T(8,128)(2,1)} %bitcast.31, bf16[4096,1024]{1,0:T(8,128)(2,1)} %wo_ref.1, bf16[4096,1024]{1,0:T(8,128)(2,1)} %wo_ref.1), custom_call_target="tpu_custom_call" | custom-call | flops 134217728 | bytes 884736 | tf_op jit(solution)/shard_map/own_projections/pallas_call | solution.py:110
  18.0 1.1 collective-permute-done.1.odd_ref
  19.1 7.8 %collective-permute-start.3 = (bf16[128,1024]{1,0:T(8,128)(2,1)S(1)}, bf16[128,1024]{1,0:T(8,128)(2,1)S(1)}, u32[]{:S(2)}, u32[]{:S(2)}) collective-permute-start(bf16[128,1024]{1,0:T(8,128)(2,1)S(1)} %collective-permute-done.even_ref), channel_id=1, source_target_pairs={{0,0},{4,8},{8,4},{12,16},{16,12},{20,24},{24,20},{28,32},{32,28},... | collective-permute-start | bytes 786440 | tf_op jit(solution)/shard_map/ppermute | solution.py:66
  26.9 4.6 %query_projections.1 = (bf16[2,128,1024]{2,1,0:T(8,128)(2,1)S(1)}, bf16[2,128,1024]{2,1,0:T(8,128)(2,1)S(1)}, bf16[1024,1024]{1,0:T(8,128)(2,1)S(1)}) custom-call(bf16[2,128,1024]{2,1,0:T(8,128)(2,1)} %bitcast.32, bf16[2,128,1024]{2,1,0:T(8,128)(2,1)} %bitcast.22, bf16[4096,1024]{1,0:T(8,128)(2,1)} %wo_ref.1, bf16[4096,1024]{1,0:T(8,128)(2,1)} %wo_ref.1), custom_call_target="tpu_custom_call" | custom-call | flops 134217728 | bytes 884736 | tf_op jit(solution)/shard_map/query_projections/pallas_call | solution.py:133
  31.5 2.5 %halo_projections_kernel.3.kv1_ref = bf16[2,2,128,1024]{3,2,1,0:T(8,128)(2,1)S(1)} custom-call(s32[1]{0:T(128)} %bitcast.parity, bf16[128,1024]{1,0:T(8,128)(2,1)S(1)} %collective-permute-done.even_ref, bf16[128,1024]{1,0:T(8,128)(2,1)S(1)} %collective-permute-done.1.odd_ref, bf16[1024,1024]{1,0:T(8,128)(2,1)S(1)} %get-tuple-element.82.wk_ref, ...), custom_call_target="tpu_custom_call" | custom-call | flops 67108864 | bytes 360448 | tf_op jit(solution)/shard_map/halo_projections_kernel/pallas_call | solution.py:70
  34.2 5.7 %collective-permute-start.5 = (bf16[128,1024]{1,0:T(8,128)(2,1)S(1)}, bf16[128,1024]{1,0:T(8,128)(2,1)S(1)}, u32[]{:S(2)}, u32[]{:S(2)}) collective-permute-start(bf16[128,1024]{1,0:T(8,128)(2,1)S(1)} %collective-permute-done.2.even_ref), channel_id=1, source_target_pairs={{0,0},{4,8},{8,4},{12,16},{16,12},{20,24},{24,20},{28,32},{32,28},... | collective-permute-start | bytes 786440 | tf_op jit(solution)/shard_map/ppermute | solution.py:66
  39.9 2.5 %halo_projections_kernel.4.kv2_ref = bf16[2,2,128,1024]{3,2,1,0:T(8,128)(2,1)S(1)} custom-call(s32[1]{0:T(128)} %bitcast.parity, bf16[128,1024]{1,0:T(8,128)(2,1)S(1)} %collective-permute-done.2.even_ref, bf16[128,1024]{1,0:T(8,128)(2,1)S(1)} %collective-permute-done.3.odd_ref, bf16[1024,1024]{1,0:T(8,128)(2,1)S(1)} %get-tuple-element.82.wk_ref, ...), custom_call_target="tpu_custom_call" | custom-call | flops 67108864 | bytes 360448 | tf_op jit(solution)/shard_map/halo_projections_kernel/pallas_call | solution.py:70
  42.5 4.4 %collective-permute-done.5.odd_ref = bf16[128,1024]{1,0:T(8,128)(2,1)S(1)} collective-permute-done((bf16[128,1024]{1,0:T(8,128)(2,1)S(1)}, bf16[128,1024]{1,0:T(8,128)(2,1)S(1)}, u32[]{:S(2)}, u32[]{:S(2)}) %collective-permute-start.5) | collective-permute-done | bytes 262176 | tf_op jit(solution)/shard_map/ppermute | solution.py:66
  46.9 2.5 %halo_projections_kernel.5.kv3_ref = bf16[2,2,128,1024]{3,2,1,0:T(8,128)(2,1)S(1)} custom-call(s32[1]{0:T(128)} %bitcast.parity, bf16[128,1024]{1,0:T(8,128)(2,1)S(1)} %collective-permute-done.4.even_ref, bf16[128,1024]{1,0:T(8,128)(2,1)S(1)} %collective-permute-done.5.odd_ref, bf16[1024,1024]{1,0:T(8,128)(2,1)S(1)} %get-tuple-element.82.wk_ref, ...), custom_call_target="tpu_custom_call" | custom-call | flops 67108864 | bytes 360448 | tf_op jit(solution)/shard_map/halo_projections_kernel/pallas_call | solution.py:70
  49.4 4.9 %attention_out.1 = (bf16[2,128,1024]{2,1,0:T(8,128)(2,1)S(1)}, bf16[2,128,1024]{2,1,0:T(8,128)(2,1)S(1)}, bf16[2,8,256,512]{3,2,1,0:T(8,128)(2,1)S(1)}) custom-call(s32[14]{0:T(128)S(1)} %stack.56.place, s32[64,2,128]{2,1,0:T(2,128)S(1)} %bitcast.28, bf16[2,128,1024]{2,1,0:T(8,128)(2,1)S(1)} %get-tuple-element.85.q_ref, ...), custom_call_target="tpu_custom_call" | custom-call | flops 67108864 | bytes 655360 | tf_op jit(solution)/shard_map/attention_out/pallas_call | solution.py:70
  54.3 1.1 outer_products.1
  55.5 2.6 %collective-permute-done.6 = bf16[2,1024,256]{2,1,0:T(8,128)(2,1)S(1)} collective-permute-done((bf16[2,1024,256]{2,1,0:T(8,128)(2,1)S(1)}, bf16[2,1024,256]{2,1,0:T(8,128)(2,1)S(1)}, u32[]{:S(2)}, u32[]{:S(2)}) %collective-permute-start.6) | collective-permute-done | bytes 1048608 | tf_op jit(solution)/shard_map/ppermute | solution.py:518
  58.2 0.8 split_core.1
  59.1 5.2 %attention_grads.1 = (bf16[2,128,1024]{2,1,0:T(8,128)(2,1)S(1)}, bf16[2,2,128,1024]{3,2,1,0:T(8,128)(2,1)S(1)}, bf16[2,2,128,1024]{3,2,1,0:T(8,128)(2,1)S(1)}, b...) custom-call(bf16[2,128,1024]{2,1,0:T(8,128)(2,1)S(1)} %get-tuple-element.85.q_ref, ...), custom_call_target="tpu_custom_call" | custom-call | flops 100663296 | bytes 786432 | tf_op jit(solution)/shard_map/attention_grads/pallas_call | solution.py:264
  64.3 2.0 %back_projections_kernel.3 = (bf16[128,1024]{1,0:T(8,128)(2,1)S(1)}, bf16[128,1024]{1,0:T(8,128)(2,1)S(1)}) custom-call(s32[1]{0:T(128)} %bitcast.parity, bf16[2,2,128,1024]{3,2,1,0:T(8,128)(2,1)S(1)} %get-tuple-element.110.d_ref, bf16[1024,1024]{1,0:T(8,128)(2,1)S(1)} %get-tuple-element.82.wk_ref, bf16[1024,1024]{1,0:T(8,128)(2,1)S(1)} %get-tuple-element.83.wv_ref), custom_call_target="tpu_custom_call" | custom-call | flops 67108864 | bytes 360448 | tf_op jit(solution)/shard_map/back_projections_kernel/pallas_call | solution.py:70
  66.3 2.0 %back_projections_kernel.4 = (bf16[128,1024]{1,0:T(8,128)(2,1)S(1)}, bf16[128,1024]{1,0:T(8,128)(2,1)S(1)}) custom-call(s32[1]{0:T(128)} %bitcast.parity, bf16[2,2,128,1024]{3,2,1,0:T(8,128)(2,1)S(1)} %get-tuple-element.113.d_ref, bf16[1024,1024]{1,0:T(8,128)(2,1)S(1)} %get-tuple-element.82.wk_ref, bf16[1024,1024]{1,0:T(8,128)(2,1)S(1)} %get-tuple-element.83.wv_ref), custom_call_target="tpu_custom_call" | custom-call | flops 67108864 | bytes 360448 | tf_op jit(solution)/shard_map/back_projections_kernel/pallas_call | solution.py:70
  68.3 0.7 split_first.1
  69.2 5.5 %collective-permute-start.8 = (bf16[128,1024]{1,0:T(8,128)(2,1)S(1)}, bf16[128,1024]{1,0:T(8,128)(2,1)S(1)}, u32[]{:S(2)}, u32[]{:S(2)}) collective-permute-start(bf16[128,1024]{1,0:T(8,128)(2,1)S(1)} %get-tuple-element.112), channel_id=1, source_target_pairs={{0,0},{4,8},{8,4},{12,16},{16,12},{20,24},{24,20},{28,32},{32,28},... | collective-permute-start | bytes 786440 | tf_op jit(solution)/shard_map/ppermute | solution.py:66
  74.7 2.0 %back_projections_kernel.5 = (bf16[128,1024]{1,0:T(8,128)(2,1)S(1)}, bf16[128,1024]{1,0:T(8,128)(2,1)S(1)}) custom-call(s32[1]{0:T(128)} %bitcast.parity, bf16[2,2,128,1024]{3,2,1,0:T(8,128)(2,1)S(1)} %get-tuple-element.121.d_ref, bf16[1024,1024]{1,0:T(8,128)(2,1)S(1)} %get-tuple-element.82.wk_ref, bf16[1024,1024]{1,0:T(8,128)(2,1)S(1)} %get-tuple-element.83.wv_ref), custom_call_target="tpu_custom_call" | custom-call | flops 67108864 | bytes 360448 | tf_op jit(solution)/shard_map/back_projections_kernel/pallas_call | solution.py:70
  76.7 0.6 split_second.1
  77.4 8.4 %collective-permute-done.11.moved_ref = bf16[1,2,128,256]{3,2,1,0:T(8,128)(2,1)S(1)} collective-permute-done((bf16[1,2,128,256]{3,2,1,0:T(8,128)(2,1)S(1)}, bf16[1,2,128,256]{3,2,1,0:T(8,128)(2,1)S(1)}, u32[]{:S(2)}, u32[]{:S(2)}) %collective-permute-start.11) | collective-permute-done | bytes 131104 | tf_op jit(solution)/shard_map/ppermute | solution.py:484
  86.8 4.9 %collective-permute-start.13 = (bf16[128,1024]{1,0:T(8,128)(2,1)S(1)}, bf16[128,1024]{1,0:T(8,128)(2,1)S(1)}, u32[]{:S(2)}, u32[]{:S(2)}) collective-permute-start(bf16[128,1024]{1,0:T(8,128)(2,1)S(1)} %get-tuple-element.133), channel_id=1, source_target_pairs={{0,0},{4,8},{8,4},{12,16},{16,12},{20,24},{24,20},{28,32},{32,28},... | collective-permute-start | bytes 786440 | tf_op jit(solution)/shard_map/ppermute | solution.py:66
  91.8 2.5 %last_projections_kernel.1 = (f32[128,1024]{1,0:T(8,128)S(1)}, f32[128,1024]{1,0:T(8,128)S(1)}) custom-call(s32[1]{0:T(128)} %bitcast.parity, bf16[2,2,128,1024]{3,2,1,0:T(8,128)(2,1)S(1)} %get-tuple-element.134.d_ref, bf16[2,128,1024]{2,1,0:T(8,128)(2,1)S(1)} %get-tuple-element.135.dq_ref, bf16[1024,1024]{1,0:T(8,128)(2,1)S(1)} %get-tuple-element.136.wq_ref, ...), custom_call_target="tpu_custom_call" | custom-call | flops 100663296 | bytes 524288 | tf_op jit(solution)/shard_map/last_projections_kernel/pallas_call | solution.py:70
  94.4 2.9 %collective-permute-done.14.moved_ref = bf16[1,1,128,256]{3,2,1,0:T(8,128)(2,1)S(1)} collective-permute-done((bf16[1,1,128,256]{3,2,1,0:T(8,128)(2,1)S(1)}, bf16[1,1,128,256]{3,2,1,0:T(8,128)(2,1)S(1)}, u32[]{:S(2)}, u32[]{:S(2)}) %collective-permute-start.14) | collective-permute-done | bytes 65568 | tf_op jit(solution)/shard_map/ppermute | solution.py:484
  97.9 1.4 %collective-permute-done.13.from_odd = bf16[128,1024]{1,0:T(8,128)(2,1)S(1)} collective-permute-done((bf16[128,1024]{1,0:T(8,128)(2,1)S(1)}, bf16[128,1024]{1,0:T(8,128)(2,1)S(1)}, u32[]{:S(2)}, u32[]{:S(2)}) %collective-permute-start.13) | collective-permute-done | bytes 262176 | tf_op jit(solution)/shard_map/ppermute | solution.py:66
  99.7 4.9 %collective-permute-start.16 = (bf16[128,1024]{1,0:T(8,128)(2,1)S(1)}, bf16[128,1024]{1,0:T(8,128)(2,1)S(1)}, u32[]{:S(2)}, u32[]{:S(2)}) collective-permute-start(bf16[128,1024]{1,0:T(8,128)(2,1)S(1)} %get-tuple-element.143), channel_id=1, source_target_pairs={{0,0},{4,8},{8,4},{12,16},{16,12},{20,24},{24,20},{28,32},{32,28},... | collective-permute-start | bytes 786440 | tf_op jit(solution)/shard_map/ppermute | solution.py:66
  104.6 10.8 %all_to_all.5 = bf16[8,16,256]{2,1,0:T(8,128)(2,1)S(1)} all-to-all(bf16[8,16,256]{2,1,0:T(8,128)(2,1)S(1)} %bitcast.27), channel_id=1, replica_groups={{0,4,8,12,16,20,24,28},{32,36,40,44,48,52,56,60},{64,68,72,76,80,84,88,..., dimensions={0} | all-to-all | bytes 131072 | tf_op jit(solution)/shard_map/all_to_all | solution.py:489
  115.4 0.6 convert_reduce_fusion
  116.0 1.0 final_kernel.1
  (30 shorter events, 2.7 us)
Async XLA Ops:
  1.8 16.2 %collective-permute-start = (bf16[128,1024]{1,0:T(8,128)(2,1)S(1)}, bf16[128,1024]{1,0:T(8,128)(2,1)S(1)}, u32[]{:S(2)}, u32[]{:S(2)}) collective-permute-start(bf16[128,1024]{1,0:T(8,128)(2,1)S(1)} %get-tuple-element.73), channel_id=1, source_target_pairs={{0,4},{4,0},{8,12},{12,8},{16,20},{20,16},{24,28},{28,24},{32,36},... | collective-permute-start | bytes 786440 | tf_op jit(solution)/shard_map/ppermute | solution.py:66
  3.8 15.2 %collective-permute-start.1 = (bf16[128,1024]{1,0:T(8,128)(2,1)S(1)}, bf16[128,1024]{1,0:T(8,128)(2,1)S(1)}, u32[]{:S(2)}, u32[]{:S(2)}) collective-permute-start(bf16[128,1024]{1,0:T(8,128)(2,1)S(1)} %get-tuple-element.74), channel_id=1, source_target_pairs={{0,0},{4,8},{8,4},{12,16},{16,12},{20,24},{24,20},{28,32},{32,28},... | collective-permute-start | bytes 786440 | tf_op jit(solution)/shard_map/ppermute | solution.py:66
  19.1 15.0 %collective-permute-start.2 = (bf16[128,1024]{1,0:T(8,128)(2,1)S(1)}, bf16[128,1024]{1,0:T(8,128)(2,1)S(1)}, u32[]{:S(2)}, u32[]{:S(2)}) collective-permute-start(bf16[128,1024]{1,0:T(8,128)(2,1)S(1)} %collective-permute-done.1.odd_ref), channel_id=1, source_target_pairs={{0,4},{4,0},{8,12},{12,8},{16,20},{20,16},{24,28},{28,24},{32,36},... | collective-permute-start | bytes 786440 | tf_op jit(solution)/shard_map/ppermute | solution.py:66
  19.1 15.0 %collective-permute-start.3 = (bf16[128,1024]{1,0:T(8,128)(2,1)S(1)}, bf16[128,1024]{1,0:T(8,128)(2,1)S(1)}, u32[]{:S(2)}, u32[]{:S(2)}) collective-permute-start(bf16[128,1024]{1,0:T(8,128)(2,1)S(1)} %collective-permute-done.even_ref), channel_id=1, source_target_pairs={{0,0},{4,8},{8,4},{12,16},{16,12},{20,24},{24,20},{28,32},{32,28},... | collective-permute-start | bytes 786440 | tf_op jit(solution)/shard_map/ppermute | solution.py:66
  34.1 8.4 %collective-permute-start.4 = (bf16[128,1024]{1,0:T(8,128)(2,1)S(1)}, bf16[128,1024]{1,0:T(8,128)(2,1)S(1)}, u32[]{:S(2)}, u32[]{:S(2)}) collective-permute-start(bf16[128,1024]{1,0:T(8,128)(2,1)S(1)} %collective-permute-done.3.odd_ref), channel_id=1, source_target_pairs={{0,4},{4,0},{8,12},{12,8},{16,20},{20,16},{24,28},{28,24},{32,36},... | collective-permute-start | bytes 786440 | tf_op jit(solution)/shard_map/ppermute | solution.py:66
  34.2 12.7 %collective-permute-start.5 = (bf16[128,1024]{1,0:T(8,128)(2,1)S(1)}, bf16[128,1024]{1,0:T(8,128)(2,1)S(1)}, u32[]{:S(2)}, u32[]{:S(2)}) collective-permute-start(bf16[128,1024]{1,0:T(8,128)(2,1)S(1)} %collective-permute-done.2.even_ref), channel_id=1, source_target_pairs={{0,0},{4,8},{8,4},{12,16},{16,12},{20,24},{24,20},{28,32},{32,28},... | collective-permute-start | bytes 786440 | tf_op jit(solution)/shard_map/ppermute | solution.py:66
  42.4 7.0 %copy-start.1 = (s32[1,64,2,128]{3,2,1,0:T(2,128)S(1)}, s32[1,64,2,128]{3,2,1,0:T(2,128)}, u32[]{:S(2)}) copy-start(s32[1,64,2,128]{3,2,1,0:T(2,128)} %param.5) | copy-start | bytes 196612
  49.4 4.9 %copy-start = (bf16[1,1,2,128,1024]{4,3,2,1,0:T(8,128)(2,1)S(1)}, bf16[1,1,2,128,1024]{4,3,2,1,0:T(8,128)(2,1)}, u32[]{:S(2)}) copy-start(bf16[1,1,2,128,1024]{4,3,2,1,0:T(8,128)(2,1)} %param.7) | copy-start | bytes 1572868
  55.4 2.7 %collective-permute-start.6 = (bf16[2,1024,256]{2,1,0:T(8,128)(2,1)S(1)}, bf16[2,1024,256]{2,1,0:T(8,128)(2,1)S(1)}, u32[]{:S(2)}, u32[]{:S(2)}) collective-permute-start(bf16[2,1024,256]{2,1,0:T(8,128)(2,1)S(1)} %get-tuple-element.103), channel_id=1, source_target_pairs={{0,1},{1,0},{2,3},{3,2},{4,5},{5,4},{6,7},{7,6},{8,9},{9,8},{10,11... | collective-permute-start | bytes 3145736 | tf_op jit(solution)/shard_map/ppermute | solution.py:518
  59.0 9.3 %collective-permute-start.9 = (bf16[2,4,128,256]{3,2,1,0:T(8,128)(2,1)S(1)}, bf16[2,4,128,256]{3,2,1,0:T(8,128)(2,1)S(1)}, u32[]{:S(2)}, u32[]{:S(2)}) collective-permute-start(bf16[2,4,128,256]{3,2,1,0:T(8,128)(2,1)S(1)} %get-tuple-element.117), channel_id=1, source_target_pairs={{0,32},{1,129},{4,36},{5,133},{8,40},{9,137},{12,44},{13,141},{16,... | collective-permute-start | bytes 1572872 | tf_op jit(solution)/shard_map/ppermute | solution.py:484
  69.0 7.7 %collective-permute-start.10 = (bf16[1,4,128,256]{3,2,1,0:T(8,128)(2,1)S(1)}, bf16[1,4,128,256]{3,2,1,0:T(8,128)(2,1)S(1)}, u32[]{:S(2)}, u32[]{:S(2)}) collective-permute-start(bf16[1,4,128,256]{3,2,1,0:T(8,128)(2,1)S(1)} %get-tuple-element.120), channel_id=1, source_target_pairs={{0,96},{1,131},{4,100},{5,135},{8,104},{9,139},{12,108},{13,143},{... | collective-permute-start | bytes 786440 | tf_op jit(solution)/shard_map/ppermute | solution.py:484
  69.1 17.3 %collective-permute-start.7 = (bf16[128,1024]{1,0:T(8,128)(2,1)S(1)}, bf16[128,1024]{1,0:T(8,128)(2,1)S(1)}, u32[]{:S(2)}, u32[]{:S(2)}) collective-permute-start(bf16[128,1024]{1,0:T(8,128)(2,1)S(1)} %get-tuple-element.111), channel_id=1, source_target_pairs={{0,4},{4,0},{8,12},{12,8},{16,20},{20,16},{24,28},{28,24},{32,36},... | collective-permute-start | bytes 786440 | tf_op jit(solution)/shard_map/ppermute | solution.py:66
  69.2 17.2 %collective-permute-start.8 = (bf16[128,1024]{1,0:T(8,128)(2,1)S(1)}, bf16[128,1024]{1,0:T(8,128)(2,1)S(1)}, u32[]{:S(2)}, u32[]{:S(2)}) collective-permute-start(bf16[128,1024]{1,0:T(8,128)(2,1)S(1)} %get-tuple-element.112), channel_id=1, source_target_pairs={{0,0},{4,8},{8,4},{12,16},{16,12},{20,24},{24,20},{28,32},{32,28},... | collective-permute-start | bytes 786440 | tf_op jit(solution)/shard_map/ppermute | solution.py:66
  77.3 8.5 %collective-permute-start.11 = (bf16[1,2,128,256]{3,2,1,0:T(8,128)(2,1)S(1)}, bf16[1,2,128,256]{3,2,1,0:T(8,128)(2,1)S(1)}, u32[]{:S(2)}, u32[]{:S(2)}) collective-permute-start(bf16[1,2,128,256]{3,2,1,0:T(8,128)(2,1)S(1)} %get-tuple-element.126), channel_id=1, source_target_pairs={{0,128},{1,33},{4,132},{5,37},{8,136},{9,41},{12,140},{13,45},{16,... | collective-permute-start | bytes 393224 | tf_op jit(solution)/shard_map/ppermute | solution.py:484
  86.7 11.1 %collective-permute-start.12 = (bf16[128,1024]{1,0:T(8,128)(2,1)S(1)}, bf16[128,1024]{1,0:T(8,128)(2,1)S(1)}, u32[]{:S(2)}, u32[]{:S(2)}) collective-permute-start(bf16[128,1024]{1,0:T(8,128)(2,1)S(1)} %get-tuple-element.132), channel_id=1, source_target_pairs={{0,4},{4,0},{8,12},{12,8},{16,20},{20,16},{24,28},{28,24},{32,36},... | collective-permute-start | bytes 786440 | tf_op jit(solution)/shard_map/ppermute | solution.py:66
  86.8 12.5 %collective-permute-start.13 = (bf16[128,1024]{1,0:T(8,128)(2,1)S(1)}, bf16[128,1024]{1,0:T(8,128)(2,1)S(1)}, u32[]{:S(2)}, u32[]{:S(2)}) collective-permute-start(bf16[128,1024]{1,0:T(8,128)(2,1)S(1)} %get-tuple-element.133), channel_id=1, source_target_pairs={{0,0},{4,8},{8,4},{12,16},{16,12},{20,24},{24,20},{28,32},{32,28},... | collective-permute-start | bytes 786440 | tf_op jit(solution)/shard_map/ppermute | solution.py:66
  91.7 5.6 %collective-permute-start.14 = (bf16[1,1,128,256]{3,2,1,0:T(8,128)(2,1)S(1)}, bf16[1,1,128,256]{3,2,1,0:T(8,128)(2,1)S(1)}, u32[]{:S(2)}, u32[]{:S(2)}) collective-permute-start(bf16[1,1,128,256]{3,2,1,0:T(8,128)(2,1)S(1)} %get-tuple-element.129), channel_id=1, source_target_pairs={{0,130},{1,97},{4,134},{5,101},{8,138},{9,105},{12,142},{13,109},{... | collective-permute-start | bytes 196616 | tf_op jit(solution)/shard_map/ppermute | solution.py:484
  99.6 16.4 %collective-permute-start.15 = (bf16[128,1024]{1,0:T(8,128)(2,1)S(1)}, bf16[128,1024]{1,0:T(8,128)(2,1)S(1)}, u32[]{:S(2)}, u32[]{:S(2)}) collective-permute-start(bf16[128,1024]{1,0:T(8,128)(2,1)S(1)} %get-tuple-element.142), channel_id=1, source_target_pairs={{0,4},{4,0},{8,12},{12,8},{16,20},{20,16},{24,28},{28,24},{32,36},... | collective-permute-start | bytes 786440 | tf_op jit(solution)/shard_map/ppermute | solution.py:66
  99.7 16.3 %collective-permute-start.16 = (bf16[128,1024]{1,0:T(8,128)(2,1)S(1)}, bf16[128,1024]{1,0:T(8,128)(2,1)S(1)}, u32[]{:S(2)}, u32[]{:S(2)}) collective-permute-start(bf16[128,1024]{1,0:T(8,128)(2,1)S(1)} %get-tuple-element.143), channel_id=1, source_target_pairs={{0,0},{4,8},{8,4},{12,16},{16,12},{20,24},{24,20},{28,32},{32,28},... | collective-permute-start | bytes 786440 | tf_op jit(solution)/shard_map/ppermute | solution.py:66

commit v6 on v5

--- a/solution.py
+++ b/solution.py
@@ -260,17 +260,25 @@
     )
 
 
-def attention_backward(q, kvs, out, scaled, terms):
-    return pl.pallas_call(
-        attention_grads,
-        grid=(2, D // WIDTH),
-        in_specs=[ROWS] + [PAIRED] * 4 + [ROWS, ROWS, TERMS],
-        out_specs=[ROWS] + [PAIRED] * 4,
+def attention_backward(half, q, kvs, out, scaled, terms, so_far=()):
+    rows = pl.BlockSpec((1, BLOCK, WIDTH), lambda p: (half, 0, p))
+    paired = pl.BlockSpec((2, 1, BLOCK, WIDTH), lambda p: (0, half, 0, p))
+    held = pl.BlockSpec((1, PAIRS_A_STEP, 2 * BLOCK, WIN * BLOCK), lambda p: (half, p, 0, 0))
+
+    def kernel(*refs):
+        attention_grads(*refs[:8], *refs[8 + len(so_far) :])
+
+    return pl.pallas_call(
+        kernel,
+        grid=(D // WIDTH,),
+        in_specs=[rows] + [paired] * 4 + [rows, rows, held] + [pl.BlockSpec(memory_space=pl.ANY)] * len(so_far),
+        out_specs=[rows] + [paired] * 4,
         out_shape=[ROWS_LOW] + [PAIRED_LOW] * 4,
+        input_output_aliases={8 + i: i for i in range(len(so_far))},
         compiler_params=params(24),
-        cost_estimate=cost(2 * 6 * BLOCK * WIN * BLOCK * D * 2, 12 * 2**20),
+        cost_estimate=cost(6 * BLOCK * WIN * BLOCK * D * 2, 6 * 2**20),
         name="attention_grads",
-    )(*in_vmem(q, *kvs, out, scaled, terms))
+    )(*in_vmem(q, *kvs, out, scaled, terms), *so_far)
 
 
 def in_order(parity, ref, *lead):
@@ -347,8 +355,8 @@
     )
 
 
-def hop_kernel(parity, even_ref, odd_ref, from_even, from_odd, even_out, odd_out):
-    even_out[...], odd_out[...] = hop_sums(even_ref, odd_ref, from_even, from_odd)
+def hop_kernel(term_ref, moved_ref, out_ref):
+    out_ref[...] = (term_ref[...].astype(F32) + moved_ref[...].astype(F32)).astype(BF)
 
 
 def final_kernel(parity, even_ref, odd_ref, from_even, from_odd, out_ref):
@@ -356,17 +364,26 @@
         out_ref[half] = rows[None]
 
 
-def hop_back(parity, terms, moved, last=False):
+def hop_back(term, moved):
+    spec = pl.BlockSpec((BLOCK, D // 2), lambda t: (0, t))
+    return pl.pallas_call(
+        hop_kernel,
+        grid=(2,),
+        in_specs=[spec] * 2,
+        out_specs=spec,
+        out_shape=jax.ShapeDtypeStruct((BLOCK, D), BF),
+        compiler_params=params(6),
+        cost_estimate=cost(4 * BLOCK * D, 6 * BLOCK * D),
+        name="hop_back",
+    )(*in_vmem(term, moved))
+
+
+def final_hop(parity, terms, moved):
     spec = pl.BlockSpec((BLOCK, D // 2), lambda t, p: (0, t))
-    if last:
-        out_specs = pl.BlockSpec((2, BLOCK, D // 2), lambda t, p: (0, 0, t))
-        out_shape = jax.ShapeDtypeStruct((2, BLOCK, D), BF)
-    else:
-        out_specs = [spec] * 2
-        out_shape = [jax.ShapeDtypeStruct((BLOCK, D), BF)] * 2
     return with_parity(
-        final_kernel if last else hop_kernel, parity, in_vmem(*terms, *moved), (2,),
-        [spec] * 4, out_specs, out_shape, 6, cost(8 * BLOCK * D, 14 * BLOCK * D),
+        final_kernel, parity, in_vmem(*terms, *moved), (2,), [spec] * 4,
+        pl.BlockSpec((2, BLOCK, D // 2), lambda t, p: (0, 0, t)),
+        jax.ShapeDtypeStruct((2, BLOCK, D), BF), 6, cost(8 * BLOCK * D, 14 * BLOCK * D),
     )
 
 
@@ -448,17 +465,24 @@
     out_ref[...] = total(kept_ref[...], moved_ref[...])
 
 
-def halving(kernel, place, arrays, shapes):
+def halving(kernel, place, arrays, shapes, ready=()):
     vmem = pl.BlockSpec(memory_space=pltpu.VMEM)
-    return pl.pallas_call(
-        kernel,
-        in_specs=[pl.BlockSpec(memory_space=pltpu.SMEM)] + [vmem] * len(arrays),
+    count = 1 + len(arrays)
+
+    def body(*refs):
+        kernel(*refs[:count], *refs[count + len(ready) :])
+
+    return pl.pallas_call(
+        body,
+        in_specs=[pl.BlockSpec(memory_space=pltpu.SMEM)]
+        + [vmem] * len(arrays)
+        + [pl.BlockSpec(memory_space=pl.ANY)] * len(ready),
         out_specs=[vmem] * len(shapes),
         out_shape=[jax.ShapeDtypeStruct(shape + (SHARE, TILE), BF) for shape in shapes],
         compiler_params=params(8),
         cost_estimate=cost(2**20, 2**20),
         name=kernel.__name__,
-    )(place, *arrays)
+    )(place, *arrays, *ready)
 
 
 def halve_core(place, kept, other):
@@ -474,20 +498,21 @@
 )
 
 
-def after(values, ready):
-    return lax.optimization_barrier((values, ready))[0]
-
-
-def halve(turn, place, pieces, ready):
-    kernel, pairs, shapes = HALVINGS[turn]
-    keep, send = pieces
-    moved = after(lax.ppermute(send, ("blk", "dp"), pairs), ready)
-    return halving(kernel, place, [keep, moved], shapes)
-
-
-def sum_over_line(total):
+together = lax.optimization_barrier
+
+
+def send_pieces(turn, pieces):
+    return lax.ppermute(pieces[1], ("blk", "dp"), HALVINGS[turn][1])
+
+
+def halve(turn, place, pieces, moved, ready=()):
+    kernel, _, shapes = HALVINGS[turn]
+    return halving(kernel, place, [pieces[0], moved], shapes, ready)
+
+
+def sum_over_line(total, ready):
     total = lax.all_to_all(total.reshape(8, 16, TILE), "blk", 0, 0, axis_index_groups=LINES)
-    return jnp.sum(total.astype(F32), axis=0)
+    return jnp.sum(together((total, ready))[0].astype(F32), axis=0)
 
 
 def per_device(tokens, key_valid, weights, out_grad):
@@ -502,40 +527,41 @@
     place = places(position, shot)
     own, core, place = lax.optimization_barrier((x, core, place))
     kv0, wk, wv = own_projections(own, weights)
-    kvs = [kv0]
-    for hop_index in range(WIN - 1):
-        from_even, from_odd = exchange(*state)
-        if hop_index == 1:
-            q, da, wq, kvs[-1] = lax.optimization_barrier((*query_projections(own, g, weights), kvs[-1]))
-            from_even, from_odd, q = lax.optimization_barrier((from_even, from_odd, q))
-        from_even, from_odd, kvs[-1] = lax.optimization_barrier((from_even, from_odd, kvs[-1]))
-        kvs.append(halo_projections(parity, from_even, from_odd, wk, wv))
-        state = from_odd, from_even
+    even, odd = exchange(*state)
+    even, kv0 = together((even, kv0))
+    even_2, odd_2 = exchange(odd, even)
+    kv1 = halo_projections(parity, even, odd, wk, wv)
+    q, da, wq = query_projections(own, g, weights)
+    even_2, q = together((even_2, q))
+    even_3, odd_3 = exchange(odd_2, even_2)
+    kv2 = halo_projections(parity, even_2, odd_2, wk, wv)
+    kvs = [kv0, kv1, kv2, halo_projections(parity, even_3, odd_3, wk, wv)]
     kvs = kvs[::-1]
     o, scaled, exps = attention_forward(place, key_valid.reshape(64, 2, BLOCK), q, da, kvs)
 
     kept, sent = outer_products(o, g, core)
-    pieces = halve_core(place, kept, lax.ppermute(sent, "dp", CORE_PAIRS))
-    exps, pieces = lax.optimization_barrier((exps, pieces))
-    dq, d3, d2, d1, d0 = attention_backward(q, kvs, o, scaled, exps)
+    other = lax.ppermute(sent, "dp", CORE_PAIRS)
+    other, *grads = together((other, *attention_backward(0, q, kvs, o, scaled, exps)))
+    exps, pieces = together((exps, halve_core(place, kept, other)))
+    part = send_pieces(0, pieces)
+    dq, d3, d2, d1, d0 = attention_backward(1, q, kvs, o, scaled, exps, grads)
     state = back_projections(parity, d3, wk, wv)
 
     moved = exchange(*state)
-    d2, d1, state = lax.optimization_barrier((d2, d1, state))
-    terms = back_projections(parity, d2, wk, wv)
-    later = back_projections(parity, d1, wk, wv)
-    pieces = halve(1, place, halve(0, place, pieces, terms), later)
-    pieces = halve(2, place, pieces, pieces)
-    state = hop_back(parity, terms, after(moved, pieces))
-
-    moved = exchange(*state)
-    last = last_projections(parity, after(d0, state), dq, wq, wk, wv)
-    (plane_sum,) = halve(3, place, pieces, last)
-    state = hop_back(parity, later, after(moved, plane_sum))
-
-    moved = exchange(*state)
-    grad_tokens = hop_back(parity, last, moved, True)
-    w_grad = sum_over_line(plane_sum)
+    pieces = halve(0, place, pieces, part, state)
+    terms, later = back_projections(parity, d2, wk, wv), back_projections(parity, d1, wk, wv)
+    pieces = halve(1, place, pieces, send_pieces(1, pieces), (*terms, *later))
+    pieces = halve(2, place, pieces, send_pieces(2, pieces))
+    even, odd = moved
+    odd, pieces, d0 = together((odd, pieces, d0))
+    moved = exchange(hop_back(terms[0], odd), hop_back(terms[1], even))
+    last = last_projections(parity, d0, dq, wq, wk, wv)
+    (plane_sum,) = halve(3, place, pieces, send_pieces(3, pieces), last)
+    even, odd = moved
+    odd, plane_sum = together((odd, plane_sum))
+    moved = exchange(hop_back(later[0], odd), hop_back(later[1], even))
+    grad_tokens = final_hop(parity, last, moved)
+    w_grad = sum_over_line(plane_sum, grad_tokens)
     return grad_tokens.reshape(tokens.shape), w_grad
 
 

time: 118 us -> 109 us (0.924)
  blocking collectives: 10.8 us -> 0 us
    all_to_all x1 -> x0, blocking collectives: 10.8 us -> none  [sum_over_line(): lax.all_to_all(total.reshape(8, 16, TILE), 'blk', 0, 0, axis_index_groups...]
    ppermute x5, waiting for transfers between devices: 14 us -> 7.67 us  [the longest x4 7.61 us: send_pieces(): return lax.ppermute(pieces[1], ('blk', 'dp'), HALVINGS[turn][1])]
    ppermute x6, waiting for transfers between devices: 6.95 us -> 11.1 us  [exchange(): lax.ppermute(odd, 'blk', ODD_PAIRS)]
    ppermute x6, starting transfers between devices: 38 us -> 34.4 us  [exchange(): lax.ppermute(odd, 'blk', ODD_PAIRS)]
    all_to_all x0 -> x1, starting transfers between devices: none -> 3.36 us  [sum_over_line(): lax.all_to_all(total.reshape(8, 16, TILE), 'blk', 0, 0, axis_index_groups...]
    all_to_all x0 -> x1, waiting for transfers between devices: none -> 1.57 us  [sum_over_line(): lax.all_to_all(total.reshape(8, 16, TILE), 'blk', 0, 0, axis_index_groups...]
    pallas_call x6 -> x11, Pallas kernels: 8.44 us -> 9.72 us  [the longest x2 5.17 us: attention_backward(): pl.pallas_call(kernel, grid=(D // WIDTH,), in_specs=[rows] + [paired] * 4...]
    pallas_call x12 -> x10, Pallas kernels: 23.7 us -> 23.1 us  [with_parity(): pl.pallas_call(kernel, grid_spec=pltpu.PrefetchScalarGridSpec(num_scalar_...]
  transfers between devices with their start and end apart: 17 -> 18, of which waited for: 6 -> 9; matrix products, arithmetic and copies ran while one was open for 1% -> 0% of each run, Pallas kernels for 25% -> 30%
where the time goes in v6:
time: 109 us; the launch traced here: 108 us
  Pallas kernels  43.2 us (40%)
  starting transfers between devices  41.4 us (38%)
  waiting for transfers between devices  21.1 us (19%)
  between operations  1.14 us (1%)
    ppermute x6, starting transfers between devices, exchange(): lax.ppermute(odd, 'blk', ODD_PAIRS)  34.4 us
    pallas_call x10, Pallas kernels, with_parity(): pl.pallas_call(kernel, grid_spec=pltpu.PrefetchScalarGridSpec(num_scalar_...  23.1 us
    ppermute x6, waiting for transfers between devices, exchange(): lax.ppermute(odd, 'blk', ODD_PAIRS)  11.1 us
    ppermute x4, waiting for transfers between devices, send_pieces(): return lax.ppermute(pieces[1], ('blk', 'dp'), HALVINGS[turn][1])  7.61 us
    pallas_call x2, Pallas kernels, attention_backward(): pl.pallas_call(kernel, grid=(D // WIDTH,), in_specs=[rows] + [paired] * 4...  5.17 us
    pallas_call x1, Pallas kernels, own_projections(): pl.pallas_call(own_kernel, grid=(D // TILE,), in_specs=[whole((2, BLOCK,...  4.71 us
    pallas_call x1, Pallas kernels, query_projections(): pl.pallas_call(query_kernel, grid=(D // TILE,), in_specs=[whole((2, BLOCK...  4.6 us
    pallas_call x5, Pallas kernels, halving(): pl.pallas_call(body, in_specs=[pl.BlockSpec(memory_space=pltpu.SMEM)] + [...  3.85 us
  transfers between devices with their start and end apart: 18, of which 9 were waited for; matrix products, arithmetic and copies ran while one was open for 0% of the time, Pallas kernels for 30%

profile of v6, /device:TPU:24, one launch (start us, length us, event | category | flops | bytes accessed | tf_op | source)
XLA Modules:
  0.0 107.6 jit_solution(3821681489581553816)
XLA Ops:
  0.6 1.2 %first_arrays.1 = (bf16[128,1024]{1,0:T(8,128)(2,1)S(1)}, bf16[128,1024]{1,0:T(8,128)(2,1)S(1)}) custom-call(s32[1]{0:T(128)} %bitcast.parity, bf16[2,128,1024]{2,1,0:T(8,128)(2,1)} %bitcast.28, bf16[2,128,1024]{2,1,0:T(8,128)(2,1)} %bitcast.29), custom_call_target="tpu_custom_call" | custom-call | bytes 65536 | tf_op jit(solution)/shard_map/first_arrays/pallas_call | solution.py:70
  1.8 10.1 %collective-permute-start = (bf16[128,1024]{1,0:T(8,128)(2,1)S(1)}, bf16[128,1024]{1,0:T(8,128)(2,1)S(1)}, u32[]{:S(2)}, u32[]{:S(2)}) collective-permute-start(bf16[128,1024]{1,0:T(8,128)(2,1)S(1)} %get-tuple-element.64), channel_id=1, source_target_pairs={{0,0},{4,8},{8,4},{12,16},{16,12},{20,24},{24,20},{28,32},{32,28},... | collective-permute-start | bytes 786440 | tf_op jit(solution)/shard_map/ppermute | solution.py:66
  12.3 4.7 %own_projections.1 = (bf16[2,2,128,1024]{3,2,1,0:T(8,128)(2,1)S(1)}, bf16[1024,1024]{1,0:T(8,128)(2,1)S(1)}, bf16[1024,1024]{1,0:T(8,128)(2,1)S(1)}) custom-call(bf16[2,128,1024]{2,1,0:T(8,128)(2,1)} %bitcast.30, bf16[4096,1024]{1,0:T(8,128)(2,1)} %wv_ref.1, bf16[4096,1024]{1,0:T(8,128)(2,1)} %wv_ref.1), custom_call_target="tpu_custom_call" | custom-call | flops 134217728 | bytes 884736 | tf_op jit(solution)/shard_map/own_projections/pallas_call | solution.py:110
  17.0 1.3 %collective-permute-done.odd_ref = bf16[128,1024]{1,0:T(8,128)(2,1)S(1)} collective-permute-done((bf16[128,1024]{1,0:T(8,128)(2,1)S(1)}, bf16[128,1024]{1,0:T(8,128)(2,1)S(1)}, u32[]{:S(2)}, u32[]{:S(2)}) %collective-permute-start) | collective-permute-done | bytes 262176 | tf_op jit(solution)/shard_map/ppermute | solution.py:66
  19.0 0.8 collective-permute-done.2.even_ref
  19.8 6.3 %collective-permute-start.3 = (bf16[128,1024]{1,0:T(8,128)(2,1)S(1)}, bf16[128,1024]{1,0:T(8,128)(2,1)S(1)}, u32[]{:S(2)}, u32[]{:S(2)}) collective-permute-start(bf16[128,1024]{1,0:T(8,128)(2,1)S(1)} %collective-permute-done.2.even_ref), channel_id=1, source_target_pairs={{0,0},{4,8},{8,4},{12,16},{16,12},{20,24},{24,20},{28,32},{32,28},... | collective-permute-start | bytes 786440 | tf_op jit(solution)/shard_map/ppermute | solution.py:66
  26.1 4.6 %query_projections.1 = (bf16[2,128,1024]{2,1,0:T(8,128)(2,1)S(1)}, bf16[2,128,1024]{2,1,0:T(8,128)(2,1)S(1)}, bf16[1024,1024]{1,0:T(8,128)(2,1)S(1)}) custom-call(bf16[2,128,1024]{2,1,0:T(8,128)(2,1)} %bitcast.31, bf16[2,128,1024]{2,1,0:T(8,128)(2,1)} %bitcast.22, bf16[4096,1024]{1,0:T(8,128)(2,1)} %wv_ref.1, bf16[4096,1024]{1,0:T(8,128)(2,1)} %wv_ref.1), custom_call_target="tpu_custom_call" | custom-call | flops 134217728 | bytes 884736 | tf_op jit(solution)/shard_map/query_projections/pallas_call | solution.py:133
  30.8 3.8 %collective-permute-start.5 = (bf16[128,1024]{1,0:T(8,128)(2,1)S(1)}, bf16[128,1024]{1,0:T(8,128)(2,1)S(1)}, u32[]{:S(2)}, u32[]{:S(2)}) collective-permute-start(bf16[128,1024]{1,0:T(8,128)(2,1)S(1)} %collective-permute-done.1.even_ref), channel_id=1, source_target_pairs={{0,0},{4,8},{8,4},{12,16},{16,12},{20,24},{24,20},{28,32},{32,28},... | collective-permute-start | bytes 786440 | tf_op jit(solution)/shard_map/ppermute | solution.py:66
  34.6 2.5 %halo_projections_kernel.5.kv1_ref.refs_3_ = bf16[2,2,128,1024]{3,2,1,0:T(8,128)(2,1)S(1)} custom-call(s32[1]{0:T(128)} %bitcast.parity, bf16[128,1024]{1,0:T(8,128)(2,1)S(1)} %collective-permute-done.2.even_ref, bf16[128,1024]{1,0:T(8,128)(2,1)S(1)} %collective-permute-done.odd_ref, bf16[1024,1024]{1,0:T(8,128)(2,1)S(1)} %get-tuple-element.72.wk_ref, ...), custom_call_target="tpu_custom_call" | custom-call | flops 67108864 | bytes 360448 | tf_op jit(solution)/shard_map/halo_projections_kernel/pallas_call | solution.py:70
  37.2 2.5 %halo_projections_kernel.4.kv2_ref.refs_2_ = bf16[2,2,128,1024]{3,2,1,0:T(8,128)(2,1)S(1)} custom-call(s32[1]{0:T(128)} %bitcast.parity, bf16[128,1024]{1,0:T(8,128)(2,1)S(1)} %collective-permute-done.1.even_ref, bf16[128,1024]{1,0:T(8,128)(2,1)S(1)} %collective-permute-done.3.odd_ref, bf16[1024,1024]{1,0:T(8,128)(2,1)S(1)} %get-tuple-element.72.wk_ref, ...), custom_call_target="tpu_custom_call" | custom-call | flops 67108864 | bytes 360448 | tf_op jit(solution)/shard_map/halo_projections_kernel/pallas_call | solution.py:70
  39.7 4.0 %collective-permute-done.5.odd_ref = bf16[128,1024]{1,0:T(8,128)(2,1)S(1)} collective-permute-done((bf16[128,1024]{1,0:T(8,128)(2,1)S(1)}, bf16[128,1024]{1,0:T(8,128)(2,1)S(1)}, u32[]{:S(2)}, u32[]{:S(2)}) %collective-permute-start.5) | collective-permute-done | bytes 262176 | tf_op jit(solution)/shard_map/ppermute | solution.py:66
  43.8 2.5 %halo_projections_kernel.3.kv3_ref.refs_1_ = bf16[2,2,128,1024]{3,2,1,0:T(8,128)(2,1)S(1)} custom-call(s32[1]{0:T(128)} %bitcast.parity, bf16[128,1024]{1,0:T(8,128)(2,1)S(1)} %collective-permute-done.4.even_ref, bf16[128,1024]{1,0:T(8,128)(2,1)S(1)} %collective-permute-done.5.odd_ref, bf16[1024,1024]{1,0:T(8,128)(2,1)S(1)} %get-tuple-element.72.wk_ref, ...), custom_call_target="tpu_custom_call" | custom-call | flops 67108864 | bytes 360448 | tf_op jit(solution)/shard_map/halo_projections_kernel/pallas_call | solution.py:70
  46.3 4.9 %attention_out.1 = (bf16[2,128,1024]{2,1,0:T(8,128)(2,1)S(1)}, bf16[2,128,1024]{2,1,0:T(8,128)(2,1)S(1)}, bf16[2,8,256,512]{3,2,1,0:T(8,128)(2,1)S(1)}) custom-call(s32[14]{0:T(128)S(1)} %stack.56.place.refs_0_, s32[64,2,128]{2,1,0:T(2,128)S(1)} %bitcast.27, bf16[2,128,1024]{2,1,0:T(8,128)(2,1)S(1)} %get-tuple-element.67.q_ref.refs_0_, ...), custom_call_target="tpu_custom_call" | custom-call | flops 67108864 | bytes 655360 | tf_op jit(solution)/shard_map/attention_out/pallas_call | solution.py:70
  51.2 1.1 %outer_products.1 = (bf16[2,1024,256]{2,1,0:T(8,128)(2,1)S(1)}, bf16[2,1024,256]{2,1,0:T(8,128)(2,1)S(1)}) custom-call(s32[1]{0:T(128)} %bitcast.2.core_ref, bf16[2,128,1024]{2,1,0:T(8,128)(2,1)S(1)} %get-tuple-element.77.o_ref.refs_5_, bf16[2,128,1024]{2,1,0:T(8,128)(2,1)S(1)} %bitcast.23, bf16[2,128,1024]{2,1,0:T(8,128)(2,1)S(1)} %bitcast.24), custom_call_target="tpu_custom_call" | custom-call | flops 33554432 | bytes 196608 | tf_op jit(solution)/shard_map/outer_products/pallas_call | solution.py:332
  52.4 2.6 %attention_grads.2 = (bf16[2,128,1024]{2,1,0:T(8,128)(2,1)S(1)}, bf16[2,2,128,1024]{3,2,1,0:T(8,128)(2,1)S(1)}, bf16[2,2,128,1024]{3,2,1,0:T(8,128)(2,1)S(1)}, b...) custom-call(bf16[2,128,1024]{2,1,0:T(8,128)(2,1)S(1)} %get-tuple-element.67.q_ref.refs_0_, ...), custom_call_target="tpu_custom_call" | custom-call | flops 50331648 | bytes 393216 | tf_op jit(solution)/shard_map/attention_grads/pallas_call | solution.py:271
  55.0 0.8 split_core.1
  56.0 2.6 %attention_grads.3 = (bf16[2,128,1024]{2,1,0:T(8,128)(2,1)S(1)}, bf16[2,2,128,1024]{3,2,1,0:T(8,128)(2,1)S(1)}, bf16[2,2,128,1024]{3,2,1,0:T(8,128)(2,1)S(1)}, b...) custom-call(bf16[2,128,1024]{2,1,0:T(8,128)(2,1)S(1)} %get-tuple-ele, ...), custom_call_target="tpu_custom_call", output_to_operand_aliasing={{0}: (8, {}), {1}: (9, {}), {2}: (10, {}), {3}: (11, {}), {... | custom-call | flops 50331648 | bytes 393216 | tf_op jit(solution)/shard_map/attention_grads/pallas_call | solution.py:271
  58.6 2.0 %back_projections_kernel.3 = (bf16[128,1024]{1,0:T(8,128)(2,1)S(1)}, bf16[128,1024]{1,0:T(8,128)(2,1)S(1)}) custom-call(s32[1]{0:T(128)} %bitcast.parity, bf16[2,2,128,1024]{3,2,1,0:T(8,128)(2,1)S(1)} %get-tuple-element.97.d_ref, bf16[1024,1024]{1,0:T(8,128)(2,1)S(1)} %get-tuple-element.72.wk_ref, bf16[1024,1024]{1,0:T(8,128)(2,1)S(1)} %get-tuple-element.73.wv_ref), custom_call_target="tpu_custom_call" | custom-call | flops 67108864 | bytes 360448 | tf_op jit(solution)/shard_map/back_projections_kernel/pallas_call | solution.py:70
  60.6 4.6 %collective-permute-done.8.refs_2_ = bf16[2,4,128,256]{3,2,1,0:T(8,128)(2,1)S(1)} collective-permute-done((bf16[2,4,128,256]{3,2,1,0:T(8,128)(2,1)S(1)}, bf16[2,4,128,256]{3,2,1,0:T(8,128)(2,1)S(1)}, u32[]{:S(2)}, u32[]{:S(2)}) %collective-permute-start.8) | collective-permute-done | bytes 524320 | tf_op jit(solution)/shard_map/ppermute | solution.py:505
  66.0 4.4 %collective-permute-start.7 = (bf16[128,1024]{1,0:T(8,128)(2,1)S(1)}, bf16[128,1024]{1,0:T(8,128)(2,1)S(1)}, u32[]{:S(2)}, u32[]{:S(2)}) collective-permute-start(bf16[128,1024]{1,0:T(8,128)(2,1)S(1)} %get-tuple-element.98.refs_4_), channel_id=1, source_target_pairs={{0,0},{4,8},{8,4},{12,16},{16,12},{20,24},{24,20},{28,32},{32,28},... | collective-permute-start | bytes 786440 | tf_op jit(solution)/shard_map/ppermute | solution.py:66
  70.5 2.0 %back_projections_kernel.4 = (bf16[128,1024]{1,0:T(8,128)(2,1)S(1)}, bf16[128,1024]{1,0:T(8,128)(2,1)S(1)}) custom-call(s32[1]{0:T(128)} %bitcast.parity, bf16[2,2,128,1024]{3,2,1,0:T(8,128)(2,1)S(1)} %get-tuple-element.104.d_ref, bf16[1024,1024]{1,0:T(8,128)(2,1)S(1)} %get-tuple-element.72.wk_ref, bf16[1024,1024]{1,0:T(8,128)(2,1)S(1)} %get-tuple-element.73.wv_ref), custom_call_target="tpu_custom_call" | custom-call | flops 67108864 | bytes 360448 | tf_op jit(solution)/shard_map/back_projections_kernel/pallas_call | solution.py:70
  72.5 2.0 %back_projections_kernel.5 = (bf16[128,1024]{1,0:T(8,128)(2,1)S(1)}, bf16[128,1024]{1,0:T(8,128)(2,1)S(1)}) custom-call(s32[1]{0:T(128)} %bitcast.parity, bf16[2,2,128,1024]{3,2,1,0:T(8,128)(2,1)S(1)} %get-tuple-element.107.d_ref, bf16[1024,1024]{1,0:T(8,128)(2,1)S(1)} %get-tuple-element.72.wk_ref, bf16[1024,1024]{1,0:T(8,128)(2,1)S(1)} %get-tuple-element.73.wv_ref), custom_call_target="tpu_custom_call" | custom-call | flops 67108864 | bytes 360448 | tf_op jit(solution)/shard_map/back_projections_kernel/pallas_call | solution.py:70
  75.4 5.8 %collective-permute-start.12 = (bf16[128,1024]{1,0:T(8,128)(2,1)S(1)}, bf16[128,1024]{1,0:T(8,128)(2,1)S(1)}, u32[]{:S(2)}, u32[]{:S(2)}) collective-permute-start(bf16[128,1024]{1,0:T(8,128)(2,1)S(1)} %hop_back.4), channel_id=1, source_target_pairs={{0,0},{4,8},{8,4},{12,16},{16,12},{20,24},{24,20},{28,32},{32,28},... | collective-permute-start | bytes 786440 | tf_op jit(solution)/shard_map/ppermute | solution.py:66
  82.3 2.5 %last_projections_kernel.1 = (f32[128,1024]{1,0:T(8,128)S(1)}, f32[128,1024]{1,0:T(8,128)S(1)}) custom-call(s32[1]{0:T(128)} %bitcast.parity, bf16[2,2,128,1024]{3,2,1,0:T(8,128)(2,1)S(1)} %get-tuple-element.115.d_ref, bf16[2,128,1024]{2,1,0:T(8,128)(2,1)S(1)} %get-tuple-element.116.dq_ref, bf16[1024,1024]{1,0:T(8,128)(2,1)S(1)} %get-tuple-element.117.wq_ref, ...), custom_call_target="tpu_custom_call" | custom-call | flops 100663296 | bytes 524288 | tf_op jit(solution)/shard_map/last_projections_kernel/pallas_call | solution.py:70
  84.9 2.9 %collective-permute-done.13.refs_2_ = bf16[1,1,128,256]{3,2,1,0:T(8,128)(2,1)S(1)} collective-permute-done((bf16[1,1,128,256]{3,2,1,0:T(8,128)(2,1)S(1)}, bf16[1,1,128,256]{3,2,1,0:T(8,128)(2,1)S(1)}, u32[]{:S(2)}, u32[]{:S(2)}) %collective-permute-start.13) | collective-permute-done | bytes 65568 | tf_op jit(solution)/shard_map/ppermute | solution.py:505
  87.8 1.2 %join_last.1 = bf16[1,1,128,256]{3,2,1,0:T(8,128)(2,1)} custom-call(s32[14]{0:T(128)S(1)} %stack.56.place.refs_0_, bf16[1,1,128,256]{3,2,1,0:T(8,128)(2,1)S(1)} %get-tuple-element.120.refs_1_, bf16[1,1,128,256]{3,2,1,0:T(8,128)(2,1)S(1)} %collective-permute-done.13.refs_2_, f32[128,1024]{1,0:T(8,128)S(1)} %get-tuple-element.118.refs_3_.even_ref, ...), custom_call_target="tpu_custom_call" | custom-call | flops 65536 | bytes 65536 | tf_op jit(solution)/shard_map/join_last/pallas_call | solution.py:475
  89.1 2.0 %collective-permute-start.14 = (bf16[128,1024]{1,0:T(8,128)(2,1)S(1)}, bf16[128,1024]{1,0:T(8,128)(2,1)S(1)}, u32[]{:S(2)}, u32[]{:S(2)}) collective-permute-start(bf16[128,1024]{1,0:T(8,128)(2,1)S(1)} %hop_back.5), channel_id=1, source_target_pairs={{0,4},{4,0},{8,12},{12,8},{16,20},{20,16},{24,28},{28,24},{32,36},... | collective-permute-start | bytes 786440 | tf_op jit(solution)/shard_map/ppermute | solution.py:66
  91.3 4.0 %collective-permute-start.16 = (bf16[128,1024]{1,0:T(8,128)(2,1)S(1)}, bf16[128,1024]{1,0:T(8,128)(2,1)S(1)}, u32[]{:S(2)}, u32[]{:S(2)}) collective-permute-start(bf16[128,1024]{1,0:T(8,128)(2,1)S(1)} %hop_back.7), channel_id=1, source_target_pairs={{0,0},{4,8},{8,4},{12,16},{16,12},{20,24},{24,20},{28,32},{32,28},... | collective-permute-start | bytes 786440 | tf_op jit(solution)/shard_map/ppermute | solution.py:66
  95.3 3.4 %all-to-all-start = ((bf16[8,16,256]{2,1,0:T(8,128)(2,1)}), bf16[8,16,256]{2,1,0:T(8,128)(2,1)S(1)}, u32[]{:S(2)}, u32[]{:S(2)}) async-start(bf16[8,16,256]{2,1,0:T(8,128)(2,1)} %bitcast.21), calls=%async_computation | async-start | bytes 131072 | tf_op jit(solution)/shard_map/all_to_all | solution.py:514
  98.7 5.8 %collective-permute-done.16.from_odd = bf16[128,1024]{1,0:T(8,128)(2,1)S(1)} collective-permute-done((bf16[128,1024]{1,0:T(8,128)(2,1)S(1)}, bf16[128,1024]{1,0:T(8,128)(2,1)S(1)}, u32[]{:S(2)}, u32[]{:S(2)}) %collective-permute-start.16) | collective-permute-done | bytes 262176 | tf_op jit(solution)/shard_map/ppermute | solution.py:66
  104.4 1.0 final_kernel.1
  105.4 1.6 %all-to-all-done = bf16[8,16,256]{2,1,0:T(8,128)(2,1)S(1)} async-done(((bf16[8,16,256]{2,1,0:T(8,128)(2,1)}), bf16[8,16,256]{2,1,0:T(8,128)(2,1)S(1)}, u32[]{:S(2)}, u32[]{:S(2)}) %all-to-all-start) | async-done | bytes 65568 | tf_op jit(solution)/shard_map/all_to_all | solution.py:514
  (34 shorter events, 5.1 us)
Async XLA Ops:
  1.8 16.4 %collective-permute-start = (bf16[128,1024]{1,0:T(8,128)(2,1)S(1)}, bf16[128,1024]{1,0:T(8,128)(2,1)S(1)}, u32[]{:S(2)}, u32[]{:S(2)}) collective-permute-start(bf16[128,1024]{1,0:T(8,128)(2,1)S(1)} %get-tuple-element.64), channel_id=1, source_target_pairs={{0,0},{4,8},{8,4},{12,16},{16,12},{20,24},{24,20},{28,32},{32,28},... | collective-permute-start | bytes 786440 | tf_op jit(solution)/shard_map/ppermute | solution.py:66
  12.0 7.9 %collective-permute-start.2 = (bf16[128,1024]{1,0:T(8,128)(2,1)S(1)}, bf16[128,1024]{1,0:T(8,128)(2,1)S(1)}, u32[]{:S(2)}, u32[]{:S(2)}) collective-permute-start(bf16[128,1024]{1,0:T(8,128)(2,1)S(1)} %get-tuple-element.68), channel_id=1, source_target_pairs={{0,4},{4,0},{8,12},{12,8},{16,20},{20,16},{24,28},{28,24},{32,36},... | collective-permute-start | bytes 786440 | tf_op jit(solution)/shard_map/ppermute | solution.py:66
  18.3 12.5 %collective-permute-start.1 = (bf16[128,1024]{1,0:T(8,128)(2,1)S(1)}, bf16[128,1024]{1,0:T(8,128)(2,1)S(1)}, u32[]{:S(2)}, u32[]{:S(2)}) collective-permute-start(bf16[128,1024]{1,0:T(8,128)(2,1)S(1)} %collective-permute-done.odd_ref), channel_id=1, source_target_pairs={{0,4},{4,0},{8,12},{12,8},{16,20},{20,16},{24,28},{28,24},{32,36},... | collective-permute-start | bytes 786440 | tf_op jit(solution)/shard_map/ppermute | solution.py:66
  19.8 14.7 %collective-permute-start.3 = (bf16[128,1024]{1,0:T(8,128)(2,1)S(1)}, bf16[128,1024]{1,0:T(8,128)(2,1)S(1)}, u32[]{:S(2)}, u32[]{:S(2)}) collective-permute-start(bf16[128,1024]{1,0:T(8,128)(2,1)S(1)} %collective-permute-done.2.even_ref), channel_id=1, source_target_pairs={{0,0},{4,8},{8,4},{12,16},{16,12},{20,24},{24,20},{28,32},{32,28},... | collective-permute-start | bytes 786440 | tf_op jit(solution)/shard_map/ppermute | solution.py:66
  30.8 13.0 %collective-permute-start.5 = (bf16[128,1024]{1,0:T(8,128)(2,1)S(1)}, bf16[128,1024]{1,0:T(8,128)(2,1)S(1)}, u32[]{:S(2)}, u32[]{:S(2)}) collective-permute-start(bf16[128,1024]{1,0:T(8,128)(2,1)S(1)} %collective-permute-done.1.even_ref), channel_id=1, source_target_pairs={{0,0},{4,8},{8,4},{12,16},{16,12},{20,24},{24,20},{28,32},{32,28},... | collective-permute-start | bytes 786440 | tf_op jit(solution)/shard_map/ppermute | solution.py:66
  34.5 9.2 %collective-permute-start.4 = (bf16[128,1024]{1,0:T(8,128)(2,1)S(1)}, bf16[128,1024]{1,0:T(8,128)(2,1)S(1)}, u32[]{:S(2)}, u32[]{:S(2)}) collective-permute-start(bf16[128,1024]{1,0:T(8,128)(2,1)S(1)} %collective-permute-done.3.odd_ref), channel_id=1, source_target_pairs={{0,4},{4,0},{8,12},{12,8},{16,20},{20,16},{24,28},{28,24},{32,36},... | collective-permute-start | bytes 786440 | tf_op jit(solution)/shard_map/ppermute | solution.py:66
  39.7 6.6 %copy-start.1 = (s32[1,64,2,128]{3,2,1,0:T(2,128)S(1)}, s32[1,64,2,128]{3,2,1,0:T(2,128)}, u32[]{:S(2)}) copy-start(s32[1,64,2,128]{3,2,1,0:T(2,128)} %param.5) | copy-start | bytes 196612
  46.3 4.9 %copy-start = (bf16[1,1,2,128,1024]{4,3,2,1,0:T(8,128)(2,1)S(1)}, bf16[1,1,2,128,1024]{4,3,2,1,0:T(8,128)(2,1)}, u32[]{:S(2)}) copy-start(bf16[1,1,2,128,1024]{4,3,2,1,0:T(8,128)(2,1)} %param.7) | copy-start | bytes 1572868
  52.3 2.7 %collective-permute-start.6 = (bf16[2,1024,256]{2,1,0:T(8,128)(2,1)S(1)}, bf16[2,1024,256]{2,1,0:T(8,128)(2,1)S(1)}, u32[]{:S(2)}, u32[]{:S(2)}) collective-permute-start(bf16[2,1024,256]{2,1,0:T(8,128)(2,1)S(1)} %get-tuple-element.82), channel_id=1, source_target_pairs={{0,1},{1,0},{2,3},{3,2},{4,5},{5,4},{6,7},{7,6},{8,9},{9,8},{10,11... | collective-permute-start | bytes 3145736 | tf_op jit(solution)/shard_map/ppermute | solution.py:543
  55.9 9.3 %collective-permute-start.8 = (bf16[2,4,128,256]{3,2,1,0:T(8,128)(2,1)S(1)}, bf16[2,4,128,256]{3,2,1,0:T(8,128)(2,1)S(1)}, u32[]{:S(2)}, u32[]{:S(2)}) collective-permute-start(bf16[2,4,128,256]{3,2,1,0:T(8,128)(2,1)S(1)} %get-tuple-element.100), channel_id=1, source_target_pairs={{0,32},{1,129},{4,36},{5,133},{8,40},{9,137},{12,44},{13,141},{16,... | collective-permute-start | bytes 1572872 | tf_op jit(solution)/shard_map/ppermute | solution.py:505
  65.8 8.6 %collective-permute-start.9 = (bf16[1,4,128,256]{3,2,1,0:T(8,128)(2,1)S(1)}, bf16[1,4,128,256]{3,2,1,0:T(8,128)(2,1)S(1)}, u32[]{:S(2)}, u32[]{:S(2)}) collective-permute-start(bf16[1,4,128,256]{3,2,1,0:T(8,128)(2,1)S(1)} %get-tuple-element.103), channel_id=1, source_target_pairs={{0,96},{1,131},{4,100},{5,135},{8,104},{9,139},{12,108},{13,143},{... | collective-permute-start | bytes 786440 | tf_op jit(solution)/shard_map/ppermute | solution.py:505
  65.9 9.3 %collective-permute-start.11 = (bf16[128,1024]{1,0:T(8,128)(2,1)S(1)}, bf16[128,1024]{1,0:T(8,128)(2,1)S(1)}, u32[]{:S(2)}, u32[]{:S(2)}) collective-permute-start(bf16[128,1024]{1,0:T(8,128)(2,1)S(1)} %get-tuple-element.101.refs_3_), channel_id=1, source_target_pairs={{0,4},{4,0},{8,12},{12,8},{16,20},{20,16},{24,28},{28,24},{32,36},... | collective-permute-start | bytes 786440 | tf_op jit(solution)/shard_map/ppermute | solution.py:66
  66.0 15.9 %collective-permute-start.7 = (bf16[128,1024]{1,0:T(8,128)(2,1)S(1)}, bf16[128,1024]{1,0:T(8,128)(2,1)S(1)}, u32[]{:S(2)}, u32[]{:S(2)}) collective-permute-start(bf16[128,1024]{1,0:T(8,128)(2,1)S(1)} %get-tuple-element.98.refs_4_), channel_id=1, source_target_pairs={{0,0},{4,8},{8,4},{12,16},{16,12},{20,24},{24,20},{28,32},{32,28},... | collective-permute-start | bytes 786440 | tf_op jit(solution)/shard_map/ppermute | solution.py:66
  75.1 6.2 %collective-permute-start.10 = (bf16[1,2,128,256]{3,2,1,0:T(8,128)(2,1)S(1)}, bf16[1,2,128,256]{3,2,1,0:T(8,128)(2,1)S(1)}, u32[]{:S(2)}, u32[]{:S(2)}) collective-permute-start(bf16[1,2,128,256]{3,2,1,0:T(8,128)(2,1)S(1)} %get-tuple-element.111), channel_id=1, source_target_pairs={{0,128},{1,33},{4,132},{5,37},{8,136},{9,41},{12,140},{13,45},{16,... | collective-permute-start | bytes 393224 | tf_op jit(solution)/shard_map/ppermute | solution.py:505
  75.4 13.6 %collective-permute-start.12 = (bf16[128,1024]{1,0:T(8,128)(2,1)S(1)}, bf16[128,1024]{1,0:T(8,128)(2,1)S(1)}, u32[]{:S(2)}, u32[]{:S(2)}) collective-permute-start(bf16[128,1024]{1,0:T(8,128)(2,1)S(1)} %hop_back.4), channel_id=1, source_target_pairs={{0,0},{4,8},{8,4},{12,16},{16,12},{20,24},{24,20},{28,32},{32,28},... | collective-permute-start | bytes 786440 | tf_op jit(solution)/shard_map/ppermute | solution.py:66
  82.1 9.0 %collective-permute-start.15 = (bf16[128,1024]{1,0:T(8,128)(2,1)S(1)}, bf16[128,1024]{1,0:T(8,128)(2,1)S(1)}, u32[]{:S(2)}, u32[]{:S(2)}) collective-permute-start(bf16[128,1024]{1,0:T(8,128)(2,1)S(1)} %hop_back.6), channel_id=1, source_target_pairs={{0,4},{4,0},{8,12},{12,8},{16,20},{20,16},{24,28},{28,24},{32,36},... | collective-permute-start | bytes 786440 | tf_op jit(solution)/shard_map/ppermute | solution.py:66
  82.2 5.6 %collective-permute-start.13 = (bf16[1,1,128,256]{3,2,1,0:T(8,128)(2,1)S(1)}, bf16[1,1,128,256]{3,2,1,0:T(8,128)(2,1)S(1)}, u32[]{:S(2)}, u32[]{:S(2)}) collective-permute-start(bf16[1,1,128,256]{3,2,1,0:T(8,128)(2,1)S(1)} %get-tuple-element.121), channel_id=1, source_target_pairs={{0,130},{1,97},{4,134},{5,101},{8,138},{9,105},{12,142},{13,109},{... | collective-permute-start | bytes 196616 | tf_op jit(solution)/shard_map/ppermute | solution.py:505
  89.1 9.5 %collective-permute-start.14 = (bf16[128,1024]{1,0:T(8,128)(2,1)S(1)}, bf16[128,1024]{1,0:T(8,128)(2,1)S(1)}, u32[]{:S(2)}, u32[]{:S(2)}) collective-permute-start(bf16[128,1024]{1,0:T(8,128)(2,1)S(1)} %hop_back.5), channel_id=1, source_target_pairs={{0,4},{4,0},{8,12},{12,8},{16,20},{20,16},{24,28},{28,24},{32,36},... | collective-permute-start | bytes 786440 | tf_op jit(solution)/shard_map/ppermute | solution.py:66
  91.3 13.1 %collective-permute-start.16 = (bf16[128,1024]{1,0:T(8,128)(2,1)S(1)}, bf16[128,1024]{1,0:T(8,128)(2,1)S(1)}, u32[]{:S(2)}, u32[]{:S(2)}) collective-permute-start(bf16[128,1024]{1,0:T(8,128)(2,1)S(1)} %hop_back.7), channel_id=1, source_target_pairs={{0,0},{4,8},{8,4},{12,16},{16,12},{20,24},{24,20},{28,32},{32,28},... | collective-permute-start | bytes 786440 | tf_op jit(solution)/shard_map/ppermute | solution.py:66
  95.3 11.7 %all-to-all-start = ((bf16[8,16,256]{2,1,0:T(8,128)(2,1)}), bf16[8,16,256]{2,1,0:T(8,128)(2,1)S(1)}, u32[]{:S(2)}, u32[]{:S(2)}) async-start(bf16[8,16,256]{2,1,0:T(8,128)(2,1)} %bitcast.21), calls=%async_computation | async-start | bytes 131072 | tf_op jit(solution)/shard_map/all_to_all | solution.py:514

commit v7 on v6

--- a/solution.py
+++ b/solution.py
@@ -558,7 +558,6 @@
     last = last_projections(parity, d0, dq, wq, wk, wv)
     (plane_sum,) = halve(3, place, pieces, send_pieces(3, pieces), last)
     even, odd = moved
-    odd, plane_sum = together((odd, plane_sum))
     moved = exchange(hop_back(later[0], odd), hop_back(later[1], even))
     grad_tokens = final_hop(parity, last, moved)
     w_grad = sum_over_line(plane_sum, grad_tokens)

time: 109 us -> 115 us (1.055)
  waiting for transfers between devices: 21.1 us -> 27.9 us
    all_to_all x1, waiting for transfers between devices: 1.57 us -> 7.29 us  [sum_over_line(): lax.all_to_all(total.reshape(8, 16, TILE), 'blk', 0, 0, axis_index_groups...]
    ppermute x6, starting transfers between devices: 3.11 us -> 1.19 us  [exchange(): lax.ppermute(even, 'blk', EVEN_PAIRS)]
    ppermute x6, starting transfers between devices: 34.4 us -> 36.2 us  [exchange(): lax.ppermute(odd, 'blk', ODD_PAIRS)]
  transfers between devices with their start and end apart: 18 -> 18, of which waited for: 9 -> 10; matrix products, arithmetic and copies ran while one was open for 0% -> 0% of each run, Pallas kernels for 30% -> 28%
where the time goes in v7:
time: 115 us; the launch traced here: 114 us
  Pallas kernels  43.2 us (38%)
  starting transfers between devices  41.2 us (36%)
  waiting for transfers between devices  27.9 us (24%)
  between operations  1.16 us (1%)
    ppermute x6, starting transfers between devices, exchange(): lax.ppermute(odd, 'blk', ODD_PAIRS)  36.2 us
    pallas_call x10, Pallas kernels, with_parity(): pl.pallas_call(kernel, grid_spec=pltpu.PrefetchScalarGridSpec(num_scalar_...  23.1 us
    ppermute x6, waiting for transfers between devices, exchange(): lax.ppermute(odd, 'blk', ODD_PAIRS)  11.8 us
    ppermute x4, waiting for transfers between devices, send_pieces(): return lax.ppermute(pieces[1], ('blk', 'dp'), HALVINGS[turn][1])  7.61 us
    all_to_all x1, waiting for transfers between devices, sum_over_line(): lax.all_to_all(total.reshape(8, 16, TILE), 'blk', 0, 0, axis_index_groups...  7.29 us
    pallas_call x2, Pallas kernels, attention_backward(): pl.pallas_call(kernel, grid=(D // WIDTH,), in_specs=[rows] + [paired] * 4...  5.17 us
    pallas_call x1, Pallas kernels, own_projections(): pl.pallas_call(own_kernel, grid=(D // TILE,), in_specs=[whole((2, BLOCK,...  4.71 us
    pallas_call x1, Pallas kernels, query_projections(): pl.pallas_call(query_kernel, grid=(D // TILE,), in_specs=[whole((2, BLOCK...  4.6 us
  transfers between devices with their start and end apart: 18, of which 10 were waited for; matrix products, arithmetic and copies ran while one was open for 0% of the time, Pallas kernels for 28%

profile of v7, /device:TPU:24, one launch (start us, length us, event | category | flops | bytes accessed | tf_op | source)
XLA Modules:
  0.0 114.3 jit_solution(13195004075064967312)
XLA Ops:
  0.6 1.2 %first_arrays.1 = (bf16[128,1024]{1,0:T(8,128)(2,1)S(1)}, bf16[128,1024]{1,0:T(8,128)(2,1)S(1)}) custom-call(s32[1]{0:T(128)} %bitcast.parity, bf16[2,128,1024]{2,1,0:T(8,128)(2,1)} %bitcast.28, bf16[2,128,1024]{2,1,0:T(8,128)(2,1)} %bitcast.29), custom_call_target="tpu_custom_call" | custom-call | bytes 65536 | tf_op jit(solution)/shard_map/first_arrays/pallas_call | solution.py:70
  1.8 10.1 %collective-permute-start = (bf16[128,1024]{1,0:T(8,128)(2,1)S(1)}, bf16[128,1024]{1,0:T(8,128)(2,1)S(1)}, u32[]{:S(2)}, u32[]{:S(2)}) collective-permute-start(bf16[128,1024]{1,0:T(8,128)(2,1)S(1)} %get-tuple-element.62), channel_id=1, source_target_pairs={{0,0},{4,8},{8,4},{12,16},{16,12},{20,24},{24,20},{28,32},{32,28},... | collective-permute-start | bytes 786440 | tf_op jit(solution)/shard_map/ppermute | solution.py:66
  12.3 4.7 %own_projections.1 = (bf16[2,2,128,1024]{3,2,1,0:T(8,128)(2,1)S(1)}, bf16[1024,1024]{1,0:T(8,128)(2,1)S(1)}, bf16[1024,1024]{1,0:T(8,128)(2,1)S(1)}) custom-call(bf16[2,128,1024]{2,1,0:T(8,128)(2,1)} %bitcast.30, bf16[4096,1024]{1,0:T(8,128)(2,1)} %wv_ref.1, bf16[4096,1024]{1,0:T(8,128)(2,1)} %wv_ref.1), custom_call_target="tpu_custom_call" | custom-call | flops 134217728 | bytes 884736 | tf_op jit(solution)/shard_map/own_projections/pallas_call | solution.py:110
  17.0 1.3 %collective-permute-done.odd_ref = bf16[128,1024]{1,0:T(8,128)(2,1)S(1)} collective-permute-done((bf16[128,1024]{1,0:T(8,128)(2,1)S(1)}, bf16[128,1024]{1,0:T(8,128)(2,1)S(1)}, u32[]{:S(2)}, u32[]{:S(2)}) %collective-permute-start) | collective-permute-done | bytes 262176 | tf_op jit(solution)/shard_map/ppermute | solution.py:66
  18.3 0.7 collective-permute-start.1
  19.0 0.8 collective-permute-done.2.even_ref
  19.8 6.3 %collective-permute-start.3 = (bf16[128,1024]{1,0:T(8,128)(2,1)S(1)}, bf16[128,1024]{1,0:T(8,128)(2,1)S(1)}, u32[]{:S(2)}, u32[]{:S(2)}) collective-permute-start(bf16[128,1024]{1,0:T(8,128)(2,1)S(1)} %collective-permute-done.2.even_ref), channel_id=1, source_target_pairs={{0,0},{4,8},{8,4},{12,16},{16,12},{20,24},{24,20},{28,32},{32,28},... | collective-permute-start | bytes 786440 | tf_op jit(solution)/shard_map/ppermute | solution.py:66
  26.1 4.6 %query_projections.1 = (bf16[2,128,1024]{2,1,0:T(8,128)(2,1)S(1)}, bf16[2,128,1024]{2,1,0:T(8,128)(2,1)S(1)}, bf16[1024,1024]{1,0:T(8,128)(2,1)S(1)}) custom-call(bf16[2,128,1024]{2,1,0:T(8,128)(2,1)} %bitcast.31, bf16[2,128,1024]{2,1,0:T(8,128)(2,1)} %bitcast.22, bf16[4096,1024]{1,0:T(8,128)(2,1)} %wv_ref.1, bf16[4096,1024]{1,0:T(8,128)(2,1)} %wv_ref.1), custom_call_target="tpu_custom_call" | custom-call | flops 134217728 | bytes 884736 | tf_op jit(solution)/shard_map/query_projections/pallas_call | solution.py:133
  30.8 3.8 %collective-permute-start.5 = (bf16[128,1024]{1,0:T(8,128)(2,1)S(1)}, bf16[128,1024]{1,0:T(8,128)(2,1)S(1)}, u32[]{:S(2)}, u32[]{:S(2)}) collective-permute-start(bf16[128,1024]{1,0:T(8,128)(2,1)S(1)} %collective-permute-done.1.even_ref), channel_id=1, source_target_pairs={{0,0},{4,8},{8,4},{12,16},{16,12},{20,24},{24,20},{28,32},{32,28},... | collective-permute-start | bytes 786440 | tf_op jit(solution)/shard_map/ppermute | solution.py:66
  34.6 2.5 %halo_projections_kernel.5.kv1_ref.refs_3_ = bf16[2,2,128,1024]{3,2,1,0:T(8,128)(2,1)S(1)} custom-call(s32[1]{0:T(128)} %bitcast.parity, bf16[128,1024]{1,0:T(8,128)(2,1)S(1)} %collective-permute-done.2.even_ref, bf16[128,1024]{1,0:T(8,128)(2,1)S(1)} %collective-permute-done.odd_ref, bf16[1024,1024]{1,0:T(8,128)(2,1)S(1)} %get-tuple-element.70.wk_ref, ...), custom_call_target="tpu_custom_call" | custom-call | flops 67108864 | bytes 360448 | tf_op jit(solution)/shard_map/halo_projections_kernel/pallas_call | solution.py:70
  37.2 2.5 %halo_projections_kernel.4.kv2_ref.refs_2_ = bf16[2,2,128,1024]{3,2,1,0:T(8,128)(2,1)S(1)} custom-call(s32[1]{0:T(128)} %bitcast.parity, bf16[128,1024]{1,0:T(8,128)(2,1)S(1)} %collective-permute-done.1.even_ref, bf16[128,1024]{1,0:T(8,128)(2,1)S(1)} %collective-permute-done.3.odd_ref, bf16[1024,1024]{1,0:T(8,128)(2,1)S(1)} %get-tuple-element.70.wk_ref, ...), custom_call_target="tpu_custom_call" | custom-call | flops 67108864 | bytes 360448 | tf_op jit(solution)/shard_map/halo_projections_kernel/pallas_call | solution.py:70
  39.7 4.0 %collective-permute-done.5.odd_ref = bf16[128,1024]{1,0:T(8,128)(2,1)S(1)} collective-permute-done((bf16[128,1024]{1,0:T(8,128)(2,1)S(1)}, bf16[128,1024]{1,0:T(8,128)(2,1)S(1)}, u32[]{:S(2)}, u32[]{:S(2)}) %collective-permute-start.5) | collective-permute-done | bytes 262176 | tf_op jit(solution)/shard_map/ppermute | solution.py:66
  43.8 2.5 %halo_projections_kernel.3.kv3_ref.refs_1_ = bf16[2,2,128,1024]{3,2,1,0:T(8,128)(2,1)S(1)} custom-call(s32[1]{0:T(128)} %bitcast.parity, bf16[128,1024]{1,0:T(8,128)(2,1)S(1)} %collective-permute-done.4.even_ref, bf16[128,1024]{1,0:T(8,128)(2,1)S(1)} %collective-permute-done.5.odd_ref, bf16[1024,1024]{1,0:T(8,128)(2,1)S(1)} %get-tuple-element.70.wk_ref, ...), custom_call_target="tpu_custom_call" | custom-call | flops 67108864 | bytes 360448 | tf_op jit(solution)/shard_map/halo_projections_kernel/pallas_call | solution.py:70
  46.3 4.9 %attention_out.1 = (bf16[2,128,1024]{2,1,0:T(8,128)(2,1)S(1)}, bf16[2,128,1024]{2,1,0:T(8,128)(2,1)S(1)}, bf16[2,8,256,512]{3,2,1,0:T(8,128)(2,1)S(1)}) custom-call(s32[14]{0:T(128)S(1)} %stack.56.place.refs_0_, s32[64,2,128]{2,1,0:T(2,128)S(1)} %bitcast.27, bf16[2,128,1024]{2,1,0:T(8,128)(2,1)S(1)} %get-tuple-element.65.q_ref.refs_0_, ...), custom_call_target="tpu_custom_call" | custom-call | flops 67108864 | bytes 655360 | tf_op jit(solution)/shard_map/attention_out/pallas_call | solution.py:70
  51.2 1.1 outer_products.1
  52.4 2.6 %attention_grads.2 = (bf16[2,128,1024]{2,1,0:T(8,128)(2,1)S(1)}, bf16[2,2,128,1024]{3,2,1,0:T(8,128)(2,1)S(1)}, bf16[2,2,128,1024]{3,2,1,0:T(8,128)(2,1)S(1)}, b...) custom-call(bf16[2,128,1024]{2,1,0:T(8,128)(2,1)S(1)} %get-tuple-element.65.q_ref.refs_0_, ...), custom_call_target="tpu_custom_call" | custom-call | flops 50331648 | bytes 393216 | tf_op jit(solution)/shard_map/attention_grads/pallas_call | solution.py:271
  55.0 0.8 split_core.1
  56.0 2.6 %attention_grads.3 = (bf16[2,128,1024]{2,1,0:T(8,128)(2,1)S(1)}, bf16[2,2,128,1024]{3,2,1,0:T(8,128)(2,1)S(1)}, bf16[2,2,128,1024]{3,2,1,0:T(8,128)(2,1)S(1)}, b...) custom-call(bf16[2,128,1024]{2,1,0:T(8,128)(2,1)S(1)} %get-tuple-ele, ...), custom_call_target="tpu_custom_call", output_to_operand_aliasing={{0}: (8, {}), {1}: (9, {}), {2}: (10, {}), {3}: (11, {}), {... | custom-call | flops 50331648 | bytes 393216 | tf_op jit(solution)/shard_map/attention_grads/pallas_call | solution.py:271
  58.6 2.0 %back_projections_kernel.3 = (bf16[128,1024]{1,0:T(8,128)(2,1)S(1)}, bf16[128,1024]{1,0:T(8,128)(2,1)S(1)}) custom-call(s32[1]{0:T(128)} %bitcast.parity, bf16[2,2,128,1024]{3,2,1,0:T(8,128)(2,1)S(1)} %get-tuple-element.95.d_ref, bf16[1024,1024]{1,0:T(8,128)(2,1)S(1)} %get-tuple-element.70.wk_ref, bf16[1024,1024]{1,0:T(8,128)(2,1)S(1)} %get-tuple-element.71.wv_ref), custom_call_target="tpu_custom_call" | custom-call | flops 67108864 | bytes 360448 | tf_op jit(solution)/shard_map/back_projections_kernel/pallas_call | solution.py:70
  60.6 4.6 %collective-permute-done.8.refs_2_ = bf16[2,4,128,256]{3,2,1,0:T(8,128)(2,1)S(1)} collective-permute-done((bf16[2,4,128,256]{3,2,1,0:T(8,128)(2,1)S(1)}, bf16[2,4,128,256]{3,2,1,0:T(8,128)(2,1)S(1)}, u32[]{:S(2)}, u32[]{:S(2)}) %collective-permute-start.8) | collective-permute-done | bytes 524320 | tf_op jit(solution)/shard_map/ppermute | solution.py:505
  66.0 4.4 %collective-permute-start.7 = (bf16[128,1024]{1,0:T(8,128)(2,1)S(1)}, bf16[128,1024]{1,0:T(8,128)(2,1)S(1)}, u32[]{:S(2)}, u32[]{:S(2)}) collective-permute-start(bf16[128,1024]{1,0:T(8,128)(2,1)S(1)} %get-tuple-element.96.refs_4_), channel_id=1, source_target_pairs={{0,0},{4,8},{8,4},{12,16},{16,12},{20,24},{24,20},{28,32},{32,28},... | collective-permute-start | bytes 786440 | tf_op jit(solution)/shard_map/ppermute | solution.py:66
  70.5 2.0 %back_projections_kernel.4 = (bf16[128,1024]{1,0:T(8,128)(2,1)S(1)}, bf16[128,1024]{1,0:T(8,128)(2,1)S(1)}) custom-call(s32[1]{0:T(128)} %bitcast.parity, bf16[2,2,128,1024]{3,2,1,0:T(8,128)(2,1)S(1)} %get-tuple-element.102.d_ref, bf16[1024,1024]{1,0:T(8,128)(2,1)S(1)} %get-tuple-element.70.wk_ref, bf16[1024,1024]{1,0:T(8,128)(2,1)S(1)} %get-tuple-element.71.wv_ref), custom_call_target="tpu_custom_call" | custom-call | flops 67108864 | bytes 360448 | tf_op jit(solution)/shard_map/back_projections_kernel/pallas_call | solution.py:70
  72.5 2.0 %back_projections_kernel.5 = (bf16[128,1024]{1,0:T(8,128)(2,1)S(1)}, bf16[128,1024]{1,0:T(8,128)(2,1)S(1)}) custom-call(s32[1]{0:T(128)} %bitcast.parity, bf16[2,2,128,1024]{3,2,1,0:T(8,128)(2,1)S(1)} %get-tuple-element.105.d_ref, bf16[1024,1024]{1,0:T(8,128)(2,1)S(1)} %get-tuple-element.70.wk_ref, bf16[1024,1024]{1,0:T(8,128)(2,1)S(1)} %get-tuple-element.71.wv_ref), custom_call_target="tpu_custom_call" | custom-call | flops 67108864 | bytes 360448 | tf_op jit(solution)/shard_map/back_projections_kernel/pallas_call | solution.py:70
  75.4 5.8 %collective-permute-start.12 = (bf16[128,1024]{1,0:T(8,128)(2,1)S(1)}, bf16[128,1024]{1,0:T(8,128)(2,1)S(1)}, u32[]{:S(2)}, u32[]{:S(2)}) collective-permute-start(bf16[128,1024]{1,0:T(8,128)(2,1)S(1)} %hop_back.4), channel_id=1, source_target_pairs={{0,0},{4,8},{8,4},{12,16},{16,12},{20,24},{24,20},{28,32},{32,28},... | collective-permute-start | bytes 786440 | tf_op jit(solution)/shard_map/ppermute | solution.py:66
  82.2 6.5 %collective-permute-done.12.moved_ref = bf16[128,1024]{1,0:T(8,128)(2,1)S(1)} collective-permute-done((bf16[128,1024]{1,0:T(8,128)(2,1)S(1)}, bf16[128,1024]{1,0:T(8,128)(2,1)S(1)}, u32[]{:S(2)}, u32[]{:S(2)}) %collective-permute-start.12) | collective-permute-done | bytes 262176 | tf_op jit(solution)/shard_map/ppermute | solution.py:66
  89.5 5.8 %collective-permute-start.15 = (bf16[128,1024]{1,0:T(8,128)(2,1)S(1)}, bf16[128,1024]{1,0:T(8,128)(2,1)S(1)}, u32[]{:S(2)}, u32[]{:S(2)}) collective-permute-start(bf16[128,1024]{1,0:T(8,128)(2,1)S(1)} %hop_back.7), channel_id=1, source_target_pairs={{0,0},{4,8},{8,4},{12,16},{16,12},{20,24},{24,20},{28,32},{32,28},... | collective-permute-start | bytes 786440 | tf_op jit(solution)/shard_map/ppermute | solution.py:66
  95.4 2.5 %last_projections_kernel.1 = (f32[128,1024]{1,0:T(8,128)S(1)}, f32[128,1024]{1,0:T(8,128)S(1)}) custom-call(s32[1]{0:T(128)} %bitcast.parity, bf16[2,2,128,1024]{3,2,1,0:T(8,128)(2,1)S(1)} %get-tuple-element.113.d_ref, bf16[2,128,1024]{2,1,0:T(8,128)(2,1)S(1)} %get-tuple-element.114.dq_ref, bf16[1024,1024]{1,0:T(8,128)(2,1)S(1)} %get-tuple-element.115.wq_ref, ...), custom_call_target="tpu_custom_call" | custom-call | flops 100663296 | bytes 524288 | tf_op jit(solution)/shard_map/last_projections_kernel/pallas_call | solution.py:70
  97.9 2.9 %collective-permute-done.16.refs_2_ = bf16[1,1,128,256]{3,2,1,0:T(8,128)(2,1)S(1)} collective-permute-done((bf16[1,1,128,256]{3,2,1,0:T(8,128)(2,1)S(1)}, bf16[1,1,128,256]{3,2,1,0:T(8,128)(2,1)S(1)}, u32[]{:S(2)}, u32[]{:S(2)}) %collective-permute-start.16) | collective-permute-done | bytes 65568 | tf_op jit(solution)/shard_map/ppermute | solution.py:505
  100.9 1.2 %join_last.1 = bf16[1,1,128,256]{3,2,1,0:T(8,128)(2,1)} custom-call(s32[14]{0:T(128)S(1)} %stack.56.place.refs_0_, bf16[1,1,128,256]{3,2,1,0:T(8,128)(2,1)S(1)} %get-tuple-element.119.refs_1_, bf16[1,1,128,256]{3,2,1,0:T(8,128)(2,1)S(1)} %collective-permute-done.16.refs_2_, f32[128,1024]{1,0:T(8,128)S(1)} %get-tuple-element.116.even_ref.refs_3_, ...), custom_call_target="tpu_custom_call" | custom-call | flops 65536 | bytes 65536 | tf_op jit(solution)/shard_map/join_last/pallas_call | solution.py:475
  102.0 3.3 %all-to-all-start = ((bf16[8,16,256]{2,1,0:T(8,128)(2,1)}), bf16[8,16,256]{2,1,0:T(8,128)(2,1)S(1)}, u32[]{:S(2)}, u32[]{:S(2)}) async-start(bf16[8,16,256]{2,1,0:T(8,128)(2,1)} %bitcast.21), calls=%async_computation | async-start | bytes 131072 | tf_op jit(solution)/shard_map/all_to_all | solution.py:514
  105.4 1.0 final_kernel.1
  106.4 7.3 %all-to-all-done = bf16[8,16,256]{2,1,0:T(8,128)(2,1)S(1)} async-done(((bf16[8,16,256]{2,1,0:T(8,128)(2,1)}), bf16[8,16,256]{2,1,0:T(8,128)(2,1)S(1)}, u32[]{:S(2)}, u32[]{:S(2)}) %all-to-all-start) | async-done | bytes 65568 | tf_op jit(solution)/shard_map/all_to_all | solution.py:514
  (34 shorter events, 4.7 us)
Async XLA Ops:
  1.8 16.4 %collective-permute-start = (bf16[128,1024]{1,0:T(8,128)(2,1)S(1)}, bf16[128,1024]{1,0:T(8,128)(2,1)S(1)}, u32[]{:S(2)}, u32[]{:S(2)}) collective-permute-start(bf16[128,1024]{1,0:T(8,128)(2,1)S(1)} %get-tuple-element.62), channel_id=1, source_target_pairs={{0,0},{4,8},{8,4},{12,16},{16,12},{20,24},{24,20},{28,32},{32,28},... | collective-permute-start | bytes 786440 | tf_op jit(solution)/shard_map/ppermute | solution.py:66
  12.0 7.9 %collective-permute-start.2 = (bf16[128,1024]{1,0:T(8,128)(2,1)S(1)}, bf16[128,1024]{1,0:T(8,128)(2,1)S(1)}, u32[]{:S(2)}, u32[]{:S(2)}) collective-permute-start(bf16[128,1024]{1,0:T(8,128)(2,1)S(1)} %get-tuple-element.66), channel_id=1, source_target_pairs={{0,4},{4,0},{8,12},{12,8},{16,20},{20,16},{24,28},{28,24},{32,36},... | collective-permute-start | bytes 786440 | tf_op jit(solution)/shard_map/ppermute | solution.py:66
  18.3 12.5 %collective-permute-start.1 = (bf16[128,1024]{1,0:T(8,128)(2,1)S(1)}, bf16[128,1024]{1,0:T(8,128)(2,1)S(1)}, u32[]{:S(2)}, u32[]{:S(2)}) collective-permute-start(bf16[128,1024]{1,0:T(8,128)(2,1)S(1)} %collective-permute-done.odd_ref), channel_id=1, source_target_pairs={{0,4},{4,0},{8,12},{12,8},{16,20},{20,16},{24,28},{28,24},{32,36},... | collective-permute-start | bytes 786440 | tf_op jit(solution)/shard_map/ppermute | solution.py:66
  19.8 14.7 %collective-permute-start.3 = (bf16[128,1024]{1,0:T(8,128)(2,1)S(1)}, bf16[128,1024]{1,0:T(8,128)(2,1)S(1)}, u32[]{:S(2)}, u32[]{:S(2)}) collective-permute-start(bf16[128,1024]{1,0:T(8,128)(2,1)S(1)} %collective-permute-done.2.even_ref), channel_id=1, source_target_pairs={{0,0},{4,8},{8,4},{12,16},{16,12},{20,24},{24,20},{28,32},{32,28},... | collective-permute-start | bytes 786440 | tf_op jit(solution)/shard_map/ppermute | solution.py:66
  30.8 13.0 %collective-permute-start.5 = (bf16[128,1024]{1,0:T(8,128)(2,1)S(1)}, bf16[128,1024]{1,0:T(8,128)(2,1)S(1)}, u32[]{:S(2)}, u32[]{:S(2)}) collective-permute-start(bf16[128,1024]{1,0:T(8,128)(2,1)S(1)} %collective-permute-done.1.even_ref), channel_id=1, source_target_pairs={{0,0},{4,8},{8,4},{12,16},{16,12},{20,24},{24,20},{28,32},{32,28},... | collective-permute-start | bytes 786440 | tf_op jit(solution)/shard_map/ppermute | solution.py:66
  34.5 9.2 %collective-permute-start.4 = (bf16[128,1024]{1,0:T(8,128)(2,1)S(1)}, bf16[128,1024]{1,0:T(8,128)(2,1)S(1)}, u32[]{:S(2)}, u32[]{:S(2)}) collective-permute-start(bf16[128,1024]{1,0:T(8,128)(2,1)S(1)} %collective-permute-done.3.odd_ref), channel_id=1, source_target_pairs={{0,4},{4,0},{8,12},{12,8},{16,20},{20,16},{24,28},{28,24},{32,36},... | collective-permute-start | bytes 786440 | tf_op jit(solution)/shard_map/ppermute | solution.py:66
  39.7 6.6 %copy-start.1 = (s32[1,64,2,128]{3,2,1,0:T(2,128)S(1)}, s32[1,64,2,128]{3,2,1,0:T(2,128)}, u32[]{:S(2)}) copy-start(s32[1,64,2,128]{3,2,1,0:T(2,128)} %param.5) | copy-start | bytes 196612
  46.3 4.9 %copy-start = (bf16[1,1,2,128,1024]{4,3,2,1,0:T(8,128)(2,1)S(1)}, bf16[1,1,2,128,1024]{4,3,2,1,0:T(8,128)(2,1)}, u32[]{:S(2)}) copy-start(bf16[1,1,2,128,1024]{4,3,2,1,0:T(8,128)(2,1)} %param.7) | copy-start | bytes 1572868
  52.3 2.7 %collective-permute-start.6 = (bf16[2,1024,256]{2,1,0:T(8,128)(2,1)S(1)}, bf16[2,1024,256]{2,1,0:T(8,128)(2,1)S(1)}, u32[]{:S(2)}, u32[]{:S(2)}) collective-permute-start(bf16[2,1024,256]{2,1,0:T(8,128)(2,1)S(1)} %get-tuple-element.80), channel_id=1, source_target_pairs={{0,1},{1,0},{2,3},{3,2},{4,5},{5,4},{6,7},{7,6},{8,9},{9,8},{10,11... | collective-permute-start | bytes 3145736 | tf_op jit(solution)/shard_map/ppermute | solution.py:543
  55.9 9.3 %collective-permute-start.8 = (bf16[2,4,128,256]{3,2,1,0:T(8,128)(2,1)S(1)}, bf16[2,4,128,256]{3,2,1,0:T(8,128)(2,1)S(1)}, u32[]{:S(2)}, u32[]{:S(2)}) collective-permute-start(bf16[2,4,128,256]{3,2,1,0:T(8,128)(2,1)S(1)} %get-tuple-element.98), channel_id=1, source_target_pairs={{0,32},{1,129},{4,36},{5,133},{8,40},{9,137},{12,44},{13,141},{16,... | collective-permute-start | bytes 1572872 | tf_op jit(solution)/shard_map/ppermute | solution.py:505
  65.8 8.6 %collective-permute-start.9 = (bf16[1,4,128,256]{3,2,1,0:T(8,128)(2,1)S(1)}, bf16[1,4,128,256]{3,2,1,0:T(8,128)(2,1)S(1)}, u32[]{:S(2)}, u32[]{:S(2)}) collective-permute-start(bf16[1,4,128,256]{3,2,1,0:T(8,128)(2,1)S(1)} %get-tuple-element.101), channel_id=1, source_target_pairs={{0,96},{1,131},{4,100},{5,135},{8,104},{9,139},{12,108},{13,143},{... | collective-permute-start | bytes 786440 | tf_op jit(solution)/shard_map/ppermute | solution.py:505
  65.9 9.3 %collective-permute-start.11 = (bf16[128,1024]{1,0:T(8,128)(2,1)S(1)}, bf16[128,1024]{1,0:T(8,128)(2,1)S(1)}, u32[]{:S(2)}, u32[]{:S(2)}) collective-permute-start(bf16[128,1024]{1,0:T(8,128)(2,1)S(1)} %get-tuple-element.99.refs_3_), channel_id=1, source_target_pairs={{0,4},{4,0},{8,12},{12,8},{16,20},{20,16},{24,28},{28,24},{32,36},... | collective-permute-start | bytes 786440 | tf_op jit(solution)/shard_map/ppermute | solution.py:66
  66.0 15.9 %collective-permute-start.7 = (bf16[128,1024]{1,0:T(8,128)(2,1)S(1)}, bf16[128,1024]{1,0:T(8,128)(2,1)S(1)}, u32[]{:S(2)}, u32[]{:S(2)}) collective-permute-start(bf16[128,1024]{1,0:T(8,128)(2,1)S(1)} %get-tuple-element.96.refs_4_), channel_id=1, source_target_pairs={{0,0},{4,8},{8,4},{12,16},{16,12},{20,24},{24,20},{28,32},{32,28},... | collective-permute-start | bytes 786440 | tf_op jit(solution)/shard_map/ppermute | solution.py:66
  75.1 6.2 %collective-permute-start.10 = (bf16[1,2,128,256]{3,2,1,0:T(8,128)(2,1)S(1)}, bf16[1,2,128,256]{3,2,1,0:T(8,128)(2,1)S(1)}, u32[]{:S(2)}, u32[]{:S(2)}) collective-permute-start(bf16[1,2,128,256]{3,2,1,0:T(8,128)(2,1)S(1)} %get-tuple-element.109), channel_id=1, source_target_pairs={{0,128},{1,33},{4,132},{5,37},{8,136},{9,41},{12,140},{13,45},{16,... | collective-permute-start | bytes 393224 | tf_op jit(solution)/shard_map/ppermute | solution.py:505
  75.4 13.3 %collective-permute-start.12 = (bf16[128,1024]{1,0:T(8,128)(2,1)S(1)}, bf16[128,1024]{1,0:T(8,128)(2,1)S(1)}, u32[]{:S(2)}, u32[]{:S(2)}) collective-permute-start(bf16[128,1024]{1,0:T(8,128)(2,1)S(1)} %hop_back.4), channel_id=1, source_target_pairs={{0,0},{4,8},{8,4},{12,16},{16,12},{20,24},{24,20},{28,32},{32,28},... | collective-permute-start | bytes 786440 | tf_op jit(solution)/shard_map/ppermute | solution.py:66
  82.1 7.2 %collective-permute-start.14 = (bf16[128,1024]{1,0:T(8,128)(2,1)S(1)}, bf16[128,1024]{1,0:T(8,128)(2,1)S(1)}, u32[]{:S(2)}, u32[]{:S(2)}) collective-permute-start(bf16[128,1024]{1,0:T(8,128)(2,1)S(1)} %hop_back.6), channel_id=1, source_target_pairs={{0,4},{4,0},{8,12},{12,8},{16,20},{20,16},{24,28},{28,24},{32,36},... | collective-permute-start | bytes 786440 | tf_op jit(solution)/shard_map/ppermute | solution.py:66
  88.9 16.5 %collective-permute-start.13 = (bf16[128,1024]{1,0:T(8,128)(2,1)S(1)}, bf16[128,1024]{1,0:T(8,128)(2,1)S(1)}, u32[]{:S(2)}, u32[]{:S(2)}) collective-permute-start(bf16[128,1024]{1,0:T(8,128)(2,1)S(1)} %hop_back.5), channel_id=1, source_target_pairs={{0,4},{4,0},{8,12},{12,8},{16,20},{20,16},{24,28},{28,24},{32,36},... | collective-permute-start | bytes 786440 | tf_op jit(solution)/shard_map/ppermute | solution.py:66
  89.5 15.9 %collective-permute-start.15 = (bf16[128,1024]{1,0:T(8,128)(2,1)S(1)}, bf16[128,1024]{1,0:T(8,128)(2,1)S(1)}, u32[]{:S(2)}, u32[]{:S(2)}) collective-permute-start(bf16[128,1024]{1,0:T(8,128)(2,1)S(1)} %hop_back.7), channel_id=1, source_target_pairs={{0,0},{4,8},{8,4},{12,16},{16,12},{20,24},{24,20},{28,32},{32,28},... | collective-permute-start | bytes 786440 | tf_op jit(solution)/shard_map/ppermute | solution.py:66
  95.3 5.6 %collective-permute-start.16 = (bf16[1,1,128,256]{3,2,1,0:T(8,128)(2,1)S(1)}, bf16[1,1,128,256]{3,2,1,0:T(8,128)(2,1)S(1)}, u32[]{:S(2)}, u32[]{:S(2)}) collective-permute-start(bf16[1,1,128,256]{3,2,1,0:T(8,128)(2,1)S(1)} %get-tuple-element.120), channel_id=1, source_target_pairs={{0,130},{1,97},{4,134},{5,101},{8,138},{9,105},{12,142},{13,109},{... | collective-permute-start | bytes 196616 | tf_op jit(solution)/shard_map/ppermute | solution.py:505
  102.0 11.7 %all-to-all-start = ((bf16[8,16,256]{2,1,0:T(8,128)(2,1)}), bf16[8,16,256]{2,1,0:T(8,128)(2,1)S(1)}, u32[]{:S(2)}, u32[]{:S(2)}) async-start(bf16[8,16,256]{2,1,0:T(8,128)(2,1)} %bitcast.21), calls=%async_computation | async-start | bytes 131072 | tf_op jit(solution)/shard_map/all_to_all | solution.py:514
